TPU v7x, 32 devices: a whole 2x2x4 slice. The times are simulated.
32 devices in a mesh: section: 2 (over x), ctx: 4 (over z), fsdp: 4 (over y, core).
Axes of the slice: x: 2, y: 2, z: 4, core: 2. Of those that a mesh axis runs over, the one named last changes fastest.
Arguments:
- inputs: bfloat16 [2, 1024, 1536], P(None, ('ctx', 'fsdp')), may hold values from -6 to 6
- cotangent: bfloat16 [2, 1024, 1536], P(None, ('ctx', 'fsdp')), may hold values from -6 to 6
- attention_gain: bfloat16 [2, 1536], P('section', 'fsdp'), may hold values from 0.5 to 1.5
- query_key_value: bfloat16 [2, 1536, 3072], P('section', 'fsdp'), may hold values from -0.15625 to 0.15625
- output_weight: bfloat16 [2, 1536, 1536], P('section', 'fsdp'), may hold values from -1.25 to 1.25
- feed_gain: bfloat16 [2, 1536], P('section', 'fsdp'), may hold values from 0.5 to 1.5
- gate_up: bfloat16 [2, 1536, 8192], P('section', 'fsdp'), may hold values from -0.15625 to 0.15625
- down_weight: bfloat16 [2, 4096, 1536], P('section', 'fsdp'), may hold values from -0.09375 to 0.09375
- block_order: int32 [2, 16], replicated, may hold values from 0 to 15, each once within a row
Outputs:
- section_outputs: bfloat16 [2, 2, 1024, 1536], P('section', None, ('ctx', 'fsdp'))
- section_input_grads: float32 [2, 2, 1024, 1536], P('section', None, ('ctx', 'fsdp'))
- attention_gain_grad: float32 [2, 1536], P('section', 'fsdp')
- query_key_value_grad: float32 [2, 1536, 3072], P('section', 'fsdp')
- output_weight_grad: float32 [2, 1536, 1536], P('section', 'fsdp')
- feed_gain_grad: float32 [2, 1536], P('section', 'fsdp')
- gate_up_grad: float32 [2, 1536, 8192], P('section', 'fsdp')
- down_weight_grad: float32 [2, 4096, 1536], P('section', 'fsdp')
Inputs may be any that keep to these rules, and one draw needn't show every extreme that they name: `block_order`: each row holds every block place once.
All inputs are finite; a program needn't handle non-finite values.
Results may differ from a plain program's by a relative error of at most 0.035.
Values may be sent and summed in bfloat16 or wider, within the bound.
A program may use at most 320 MiB of HBM per device.

v0:
```python
import jax
import jax.numpy as jnp
from jax import lax
from jax.sharding import PartitionSpec as P

KV_HEADS = 8
HEAD = 96


norm_eps = 1e-05
rope_base = 100000.0
masked_value = -1e30
key_blocks = 8


def from_behind(block, axis, distance):
    devices = range(lax.axis_size(axis))
    route = [(i - distance, i) for i in devices if i - distance in devices]
    return lax.ppermute(block, axis, route)


def rms_parts(values, gain):
    factor = lax.rsqrt(jnp.mean(values * values, axis=-1, keepdims=True) + norm_eps)
    return (values * factor * gain, factor)


def norm_back(grad_out, values, factor, gain):
    shaped = grad_out * gain
    common = jnp.mean(shaped * values, axis=-1, keepdims=True)
    grad_in = factor * shaped - values * (factor * factor * factor) * common
    gain_grad = jnp.sum(grad_out * values * factor, axis=0)
    return (grad_in, gain_grad)


def angle_tables(positions, head_size):
    frequency = rope_base ** (-(jnp.arange(head_size // 2, dtype=jnp.float32) * 2.0 / head_size))
    angles = positions.astype(jnp.float32)[:, None] * frequency[None, :]
    return (jnp.cos(angles)[:, None, :], jnp.sin(angles)[:, None, :])


def rotate(values, cosine, sine):
    half = values.shape[-1] // 2
    first = values[..., :half]
    second = values[..., half:]
    return jnp.concatenate(
        [first * cosine - second * sine, second * cosine + first * sine], axis=-1
    )


def rotate_back(grads, cosine, sine):
    half = grads.shape[-1] // 2
    first = grads[..., :half]
    second = grads[..., half:]
    return jnp.concatenate(
        [first * cosine + second * sine, second * cosine - first * sine], axis=-1
    )


def block_positions(order_row, start, count, block_rows):
    places = start + jnp.arange(count, dtype=jnp.int32)
    owner = places // block_rows
    hits = owner[:, None] == jnp.arange(order_row.shape[0], dtype=jnp.int32)[None, :]
    return (
        jnp.sum(jnp.where(hits, order_row[None, :], 0), axis=1) * block_rows + places % block_rows
    )


def spread_order(values, outer, inner):
    shape = values.shape
    remain = shape[-1] // (outer * inner)
    reshaped = values.reshape(shape[:-1] + (outer, inner, remain))
    return jnp.swapaxes(reshaped, -3, -2).reshape(shape)


def attend_piece(carry, piece, start, queries, query_places, order_row, block_rows):
    running_top, running_total, running_sum = carry
    count = piece.shape[0]
    groups = queries.shape[1]
    head_size = queries.shape[3]
    kv_width = piece.shape[1] // 2
    keys = piece[:, :kv_width].reshape(count, groups, head_size)
    values = piece[:, kv_width:].reshape(count, groups, head_size)
    scores = jnp.einsum(
        "qgrd,kgd->grqk", queries, keys, preferred_element_type=jnp.float32
    ) * head_size ** (-0.5)
    allowed = block_positions(order_row, start, count, block_rows)[None, :] <= query_places[:, None]
    scores = jnp.where(allowed, scores, masked_value)
    new_top = jnp.maximum(running_top, jnp.max(scores, axis=-1))
    weights = jnp.where(allowed, jnp.exp(scores - new_top[..., None]), 0.0)
    running_total = jnp.sum(weights, axis=-1)
    part = jnp.einsum(
        "grqk,kgd->qgrd", weights.astype(jnp.bfloat16), values, preferred_element_type=jnp.float32
    )
    running_sum = part
    return (new_top, running_total, running_sum)


def attend_back(
    every_key, queries, context_grad, context, log_total, query_places, order_row, block_rows
):
    count, groups, ratio, head_size = queries.shape
    kv_width = every_key.shape[1] // 2
    span = every_key.shape[0] // key_blocks
    scale = head_size ** (-0.5)
    grad_heads = context_grad.reshape(count, groups, ratio, head_size)
    common = jnp.sum(
        grad_heads.astype(jnp.float32) * context.reshape(count, groups, ratio, head_size), axis=-1
    )
    common = jnp.transpose(common, (1, 2, 0))
    blocks = every_key.reshape(key_blocks, span, 2 * kv_width)

    def step(query_grad, item):
        index, piece = item
        keys = piece[:, :kv_width].reshape(span, groups, head_size)
        values = piece[:, kv_width:].reshape(span, groups, head_size)
        scores = (
            jnp.einsum("qgrd,kgd->grqk", queries, keys, preferred_element_type=jnp.float32) * scale
        )
        allowed = (
            block_positions(order_row, index * span, span, block_rows)[None, :]
            <= query_places[:, None]
        )
        weights = jnp.exp(jnp.where(allowed, scores, masked_value) - log_total[..., None])
        weight_grad = jnp.einsum(
            "qgrd,kgd->grqk", grad_heads, values, preferred_element_type=jnp.float32
        )
        score_grad = (weights * (weight_grad - common[..., None])).astype(jnp.bfloat16)
        value_grad = jnp.einsum(
            "grqk,qgrd->kgd",
            weights.astype(jnp.bfloat16),
            grad_heads,
            preferred_element_type=jnp.float32,
        )
        key_grad = (
            jnp.einsum("grqk,qgrd->kgd", score_grad, queries, preferred_element_type=jnp.float32)
            * scale
        )
        query_grad = query_grad + jnp.einsum(
            "grqk,kgd->qgrd", score_grad, keys, preferred_element_type=jnp.float32
        )
        return (
            query_grad,
            jnp.concatenate(
                [key_grad.reshape(span, kv_width), value_grad.reshape(span, kv_width)], axis=1
            ),
        )

    start_grad = jnp.zeros((count, groups, ratio, head_size), jnp.float32)
    query_grad, terms = lax.scan(
        step, start_grad, (jnp.arange(key_blocks, dtype=jnp.int32), blocks)
    )
    return (query_grad * scale, terms.reshape(every_key.shape[0], 2 * kv_width))


def on_device(
    inputs,
    cotangent,
    attention_gain,
    query_key_value,
    output_weight,
    feed_gain,
    gate_up,
    down_weight,
    block_order,
):
    section = lax.axis_index("section")
    sections = lax.axis_size("section")
    micro = inputs.shape[0]
    rows = inputs.shape[1]
    ticks = micro + sections - 1
    own_block = lax.axis_index(("ctx", "fsdp"))
    gathered = (
        lax.all_gather(attention_gain[0], "fsdp", axis=0, tiled=True),
        lax.all_gather(query_key_value[0], "fsdp", axis=0, tiled=True),
        lax.all_gather(output_weight[0], "fsdp", axis=0, tiled=True),
        lax.all_gather(feed_gain[0], "fsdp", axis=0, tiled=True),
        lax.all_gather(gate_up[0], "fsdp", axis=0, tiled=True),
        lax.all_gather(down_weight[0], "fsdp", axis=0, tiled=True),
    )
    first_gain = gathered[0].astype(jnp.float32)
    mix_full = gathered[1]
    out_full = gathered[2]
    second_gain = gathered[3].astype(jnp.float32)
    gate_full = gathered[4]
    down_full = gathered[5]
    width = first_gain.shape[0]
    hidden_units = down_full.shape[0]
    kv_width = (mix_full.shape[1] - width) // 2
    head_size = HEAD
    groups = KV_HEADS
    ratio = width // head_size // groups
    contract = (((1,), (1,)), ((), ()))
    row_contract = (((0,), (0,)), ((), ()))
    received = jnp.zeros((rows, width), jnp.bfloat16)
    outputs = []
    saved = []
    for tick in range(ticks):
        batch = jnp.clip(tick - section, 0, micro - 1)
        order_row = lax.dynamic_index_in_dim(block_order, batch, 0, keepdims=False)
        start_rows = jnp.where(section == 0, inputs[min(tick, micro - 1)], received).astype(
            jnp.float32
        )
        forward_positions = block_positions(order_row, own_block * rows, rows, rows)
        forward_cosine, forward_sine = angle_tables(forward_positions, head_size)
        forward_normed, forward_first_factor = rms_parts(start_rows, first_gain)
        forward_normed = forward_normed.astype(jnp.bfloat16)
        mixed = jnp.dot(forward_normed, mix_full, preferred_element_type=jnp.float32)
        forward_queries = (
            rotate(
                mixed[:, :width].reshape(rows, groups * ratio, head_size),
                forward_cosine,
                forward_sine,
            )
            .astype(jnp.bfloat16)
            .reshape(rows, groups, ratio, head_size)
        )
        keys = rotate(
            mixed[:, width : width + kv_width].reshape(rows, groups, head_size),
            forward_cosine,
            forward_sine,
        ).astype(jnp.bfloat16)
        key_values = jnp.concatenate(
            [keys.reshape(rows, kv_width), mixed[:, width + kv_width :].astype(jnp.bfloat16)],
            axis=1,
        )
        empty = (
            jnp.full((groups, ratio, rows), masked_value, jnp.float32),
            jnp.zeros((groups, ratio, rows), jnp.float32),
            jnp.zeros((rows, groups, ratio, head_size), jnp.float32),
        )
        state = attend_piece(
            empty,
            lax.all_gather(key_values, ("ctx", "fsdp"), axis=0, tiled=True),
            jnp.int32(0),
            forward_queries,
            forward_positions,
            order_row,
            rows,
        )
        top, total, summed = state
        forward_context = (summed / jnp.transpose(total, (2, 0, 1))[..., None]).reshape(rows, width)
        forward_log_total = top + jnp.log(total)
        forward_context_low = forward_context.astype(jnp.bfloat16)
        forward_middle = start_rows + jnp.dot(
            forward_context_low, out_full, preferred_element_type=jnp.float32
        )
        forward_normed_two, forward_second_factor = rms_parts(forward_middle, second_gain)
        forward_normed_two = forward_normed_two.astype(jnp.bfloat16)
        forward_both = jnp.dot(forward_normed_two, gate_full, preferred_element_type=jnp.float32)
        forward_hidden = (
            jax.nn.silu(forward_both[:, :hidden_units]) * forward_both[:, hidden_units:]
        ).astype(jnp.bfloat16)
        result = forward_middle + jnp.dot(
            forward_hidden, down_full, preferred_element_type=jnp.float32
        )
        forward_kept = (
            start_rows,
            forward_first_factor,
            forward_normed,
            forward_queries,
            key_values,
            forward_context,
            forward_context_low,
            forward_log_total,
            forward_middle,
            forward_second_factor,
            forward_normed_two,
            forward_both,
            forward_hidden,
        )
        result, kept = (result, forward_kept)
        result_low = result.astype(jnp.bfloat16)
        outputs.append(result_low)
        saved.append(kept)
        if tick + 1 < ticks:
            received = from_behind(result_low, "section", 1)
    stacked = jax.tree.map(lambda *arrays: jnp.stack(arrays), *saved)
    section_outputs = lax.dynamic_slice_in_dim(jnp.stack(outputs), section, micro, 0)
    returned = jnp.zeros((rows, width), jnp.bfloat16)
    input_grads = []
    pieces = []
    first_gain_sum = jnp.zeros((width,), jnp.float32)
    second_gain_sum = jnp.zeros((width,), jnp.float32)
    for tick in range(ticks):
        offset = tick - (sections - 1 - section)
        live = jnp.logical_and(offset >= 0, offset < micro)
        batch = jnp.clip(offset, 0, micro - 1)
        order_row = lax.dynamic_index_in_dim(block_order, batch, 0, keepdims=False)
        kept = jax.tree.map(
            lambda array: lax.dynamic_index_in_dim(array, batch + section, 0, keepdims=False),
            stacked,
        )
        incoming = jnp.where(
            section == sections - 1, cotangent[min(tick, micro - 1)], returned
        ).astype(jnp.float32)
        (
            backward_start_rows,
            first_factor,
            normed,
            queries,
            all_keys,
            context,
            context_low,
            log_total,
            middle,
            second_factor,
            normed_two,
            both,
            hidden,
        ) = kept
        positions = block_positions(order_row, own_block * rows, rows, rows)
        cosine, sine = angle_tables(positions, head_size)
        grad_low = incoming.astype(jnp.bfloat16)
        hidden_grad = lax.dot_general(
            grad_low, down_full, contract, preferred_element_type=jnp.float32
        )
        gate_part = both[:, :hidden_units]
        up_part = both[:, hidden_units:]
        sigmoid = jax.nn.sigmoid(gate_part)
        gate_grad = hidden_grad * up_part * sigmoid * (1.0 + gate_part * (1.0 - sigmoid))
        up_grad = hidden_grad * gate_part * sigmoid
        both_grad = jnp.concatenate([gate_grad, up_grad], axis=1).astype(jnp.bfloat16)
        normed_two_grad = lax.dot_general(
            both_grad, gate_full, contract, preferred_element_type=jnp.float32
        )
        middle_grad, second_gain_grad = norm_back(
            normed_two_grad, middle, second_factor, second_gain
        )
        middle_grad = middle_grad + incoming
        middle_low = middle_grad.astype(jnp.bfloat16)
        context_grad = lax.dot_general(
            middle_low, out_full, contract, preferred_element_type=jnp.float32
        ).astype(jnp.bfloat16)
        every_key = lax.all_gather(all_keys, ("ctx", "fsdp"), axis=0, tiled=True)
        query_grad, terms = attend_back(
            every_key, queries, context_grad, context, log_total, positions, order_row, rows
        )
        key_grads = lax.psum_scatter(terms, ("ctx", "fsdp"), scatter_dimension=0, tiled=True)
        query_raw = rotate_back(
            query_grad.reshape(rows, groups * ratio, head_size), cosine, sine
        ).reshape(rows, width)
        key_raw = rotate_back(
            key_grads[:, :kv_width].reshape(rows, groups, head_size), cosine, sine
        ).reshape(rows, kv_width)
        mixed_grad = jnp.concatenate([query_raw, key_raw, key_grads[:, kv_width:]], axis=1).astype(
            jnp.bfloat16
        )
        normed_grad = lax.dot_general(
            mixed_grad, mix_full, contract, preferred_element_type=jnp.float32
        )
        start_grad, first_gain_grad = norm_back(
            normed_grad, backward_start_rows, first_factor, first_gain
        )
        products = (
            normed,
            mixed_grad,
            context_low,
            middle_low,
            normed_two,
            both_grad,
            hidden,
            grad_low,
        )
        start_grad, products, gain_grads = (
            start_grad + middle_grad,
            products,
            (first_gain_grad, second_gain_grad),
        )
        live_low = live.astype(jnp.bfloat16)
        live_float = live.astype(jnp.float32)
        pieces.append(tuple((array * live_low for array in products)))
        first_gain_sum = first_gain_sum + gain_grads[0] * live_float
        second_gain_sum = second_gain_sum + gain_grads[1] * live_float
        input_grads.append(start_grad)
        if tick + 1 < ticks:
            returned = from_behind(start_grad.astype(jnp.bfloat16), "section", -1)
    grad_rows = lax.dynamic_slice_in_dim(jnp.stack(input_grads), sections - 1 - section, micro, 0)
    columns = [jnp.concatenate([piece[index] for piece in pieces], axis=0) for index in range(8)]
    left_parts = [columns[0], columns[2], columns[4], columns[6]]
    gain_parts = [first_gain_sum, second_gain_sum]
    outer = lax.axis_size("fsdp")
    inner = lax.axis_size("ctx")
    left_parts = [spread_order(part, outer, inner) for part in left_parts]
    gain_parts = [spread_order(part, outer, inner) for part in gain_parts]
    mix_grad = lax.dot_general(
        left_parts[0], columns[1], row_contract, preferred_element_type=jnp.float32
    )
    out_grad = lax.dot_general(
        left_parts[1], columns[3], row_contract, preferred_element_type=jnp.float32
    )
    gate_grad_all = lax.dot_general(
        left_parts[2], columns[5], row_contract, preferred_element_type=jnp.float32
    )
    down_grad = lax.dot_general(
        left_parts[3], columns[7], row_contract, preferred_element_type=jnp.float32
    )
    shares = (
        lax.psum_scatter(gain_parts[0], ("ctx", "fsdp"), scatter_dimension=0, tiled=True),
        lax.psum_scatter(mix_grad, ("ctx", "fsdp"), scatter_dimension=0, tiled=True),
        lax.psum_scatter(out_grad, ("ctx", "fsdp"), scatter_dimension=0, tiled=True),
        lax.psum_scatter(gain_parts[1], ("ctx", "fsdp"), scatter_dimension=0, tiled=True),
        lax.psum_scatter(gate_grad_all, ("ctx", "fsdp"), scatter_dimension=0, tiled=True),
        lax.psum_scatter(down_grad, ("ctx", "fsdp"), scatter_dimension=0, tiled=True),
    )
    final = (
        lax.all_gather(shares[0].astype(jnp.bfloat16), "ctx", axis=0, tiled=True).astype(
            jnp.float32
        ),
        lax.all_gather(shares[1].astype(jnp.bfloat16), "ctx", axis=0, tiled=True).astype(
            jnp.float32
        ),
        lax.all_gather(shares[2].astype(jnp.bfloat16), "ctx", axis=0, tiled=True).astype(
            jnp.float32
        ),
        lax.all_gather(shares[3].astype(jnp.bfloat16), "ctx", axis=0, tiled=True).astype(
            jnp.float32
        ),
        lax.all_gather(shares[4].astype(jnp.bfloat16), "ctx", axis=0, tiled=True).astype(
            jnp.float32
        ),
        lax.all_gather(shares[5].astype(jnp.bfloat16), "ctx", axis=0, tiled=True).astype(
            jnp.float32
        ),
    )
    return (
        section_outputs[None],
        grad_rows[None],
        final[0][None],
        final[1][None],
        final[2][None],
        final[3][None],
        final[4][None],
        final[5][None],
    )


def solution(mesh):
    placed = (
        P(None, ("ctx", "fsdp"), None),
        P(None, ("ctx", "fsdp"), None),
        P("section", "fsdp"),
        P("section", "fsdp", None),
        P("section", "fsdp", None),
        P("section", "fsdp"),
        P("section", "fsdp", None),
        P("section", "fsdp", None),
        P(),
    )
    return jax.shard_map(
        on_device,
        mesh=mesh,
        in_specs=placed,
        out_specs=(
            P("section", None, ("ctx", "fsdp"), None),
            P("section", None, ("ctx", "fsdp"), None),
            P("section", "fsdp"),
            P("section", "fsdp", None),
            P("section", "fsdp", None),
            P("section", "fsdp"),
            P("section", "fsdp", None),
            P("section", "fsdp", None),
        ),
        check_vma=False,
    )
```

profile of v0, /device:TPU:0, one launch (start us, length us, event | category | flops | bytes accessed | tf_op | source)
XLA Modules:
  0.0 2511.6 jit_solution(12821682573483287355)
XLA Ops:
  21.1 55.4 %all-gather.38.cloned.1.call-done = bf16[1,1536,3072]{2,1,0:T(8,128)(2,1)} async-done(((bf16[1,384,3072]{2,1,0:T(8,128)(2,1)}), bf16[1,1536,3072]{2,1,0:T(8,128)(2,1)}) %all-gather.38.cloned.1.call-update) | async-done | bytes 9437200 | tf_op jit(solution)/shard_map/all_gather | solution.py:174
  92.9 36.0 %all-gather.24.cloned.1.call-done = bf16[1024,1536]{1,0:T(8,128)(2,1)} async-done(((bf16[64,1536]{1,0:T(8,128)(2,1)}), bf16[1024,1536]{1,0:T(8,128)(2,1)}) %all-gather.24.cloned.1.call-update) | async-done | bytes 3145744 | tf_op jit(solution)/shard_map/all_gather | solution.py:233
  141.8 24.9 all-gather.40.cloned.1.call-done
  170.8 152.2 %all-gather.42.cloned.1.call-done = bf16[1,1536,8192]{2,1,0:T(8,128)(2,1)} async-done(((bf16[1,384,8192]{2,1,0:T(8,128)(2,1)}), bf16[1,1536,8192]{2,1,0:T(8,128)(2,1)}) %all-gather.42.cloned.1.call-update) | async-done | bytes 25165840 | tf_op jit(solution)/shard_map/all_gather | solution.py:177
  334.1 72.6 %all-gather.44.cloned.1.call-done = bf16[1,4096,1536]{2,1,0:T(8,128)(2,1)} async-done(((bf16[1,1024,1536]{2,1,0:T(8,128)(2,1)}), bf16[1,4096,1536]{2,1,0:T(8,128)(2,1)}) %all-gather.44.cloned.1.call-update) | async-done | bytes 12582928 | tf_op jit(solution)/shard_map/all_gather | solution.py:178
  444.1 39.6 %all-gather.26.cloned.1.call-done = bf16[1024,1536]{1,0:T(8,128)(2,1)} async-done(((bf16[64,1536]{1,0:T(8,128)(2,1)}), bf16[1024,1536]{1,0:T(8,128)(2,1)}) %all-gather.26.cloned.1.call-update) | async-done | bytes 3145744 | tf_op jit(solution)/shard_map/all_gather | solution.py:233
  574.9 12.6 all-gather.28.cloned.1.call-done
  640.8 13.6 fusion.246
  670.6 42.5 %while.45 = (s32[]{:T(128)}, f32[64,8,2,96]{3,0,2,1:T(8,128)S(1)}, f32[8,128,1536]{2,1,0:T(8,128)}, bf16[8,128,1536]{2,1,0:T(8,128)(2,1)}, s32[8]{0:T(128)S(1)},...) while((s32[]{:T(128)}, f32[64,8,2,96]{3,0,2,1:T(8,128)S(1)}, ...), condition=%wide.region_23.24_spmd.clone, body=%wide.region_21.23_spmd.clone.sunk | while | flops 127256192 | bytes 12414463 | solution.py:149
  718.1 79.6 %reduce-scatter.8.cloned.1.call-done = f32[64,1536]{1,0:T(8,128)} async-done(((f32[1024,1536]{1,0:T(8,128)}), f32[64,1536]{1,0:T(8,128)}) %reduce-scatter.8.cloned.1.call-update) | async-done | bytes 393232 | tf_op jit(solution)/shard_map/reduce_scatter | solution.py:338
  826.8 14.3 fusion.234
  853.3 79.6 %while.46 = (s32[]{:T(128)}, f32[64,8,2,96]{3,0,2,1:T(8,128)S(1)}, f32[8,128,1536]{2,1,0:T(8,128)}, bf16[8,128,1536]{2,1,0:T(8,128)(2,1)}, s32[8]{0:T(128)}, /*i...) while((s32[]{:T(128)}, f32[64,8,2,96]{3,0,2,1:T(8,128)S(1)}, ...), condition=%wide.region_31.32_spmd.clone, body=%wide.region_29.31_spmd.clone.sunk | while | flops 127256192 | bytes 12414463 | solution.py:149
  936.3 80.9 %reduce-scatter.10.cloned.1.call-done = f32[64,1536]{1,0:T(8,128)} async-done(((f32[1024,1536]{1,0:T(8,128)}), f32[64,1536]{1,0:T(8,128)}) %reduce-scatter.10.cloned.1.call-update) | async-done | bytes 393232 | tf_op jit(solution)/shard_map/reduce_scatter | solution.py:338
  1047.6 12.8 fusion.36
  1072.4 42.6 %while.47 = (s32[]{:T(128)}, f32[64,8,2,96]{3,0,2,1:T(8,128)S(1)}, f32[8,128,1536]{2,1,0:T(8,128)}, bf16[8,128,1536]{2,1,0:T(8,128)(2,1)}, s32[8]{0:T(128)S(1)},...) while((s32[]{:T(128)}, f32[64,8,2,96]{3,0,2,1:T(8,128)S(1)}, ...), condition=%wide.region_39.40_spmd.clone, body=%wide.region_37.39_spmd.clone.sunk | while | flops 127256192 | bytes 12414463 | solution.py:149
  1130.8 68.3 %reduce-scatter.12.cloned.1.call-done = f32[64,1536]{1,0:T(8,128)} async-done(((f32[1024,1536]{1,0:T(8,128)}), f32[64,1536]{1,0:T(8,128)}) %reduce-scatter.12.cloned.1.call-update) | async-done | bytes 393232 | tf_op jit(solution)/shard_map/reduce_scatter | solution.py:338
  1243.7 20.9 fusion.87
  1264.6 50.2 %reduce-scatter.16.cloned.1.call-done = f32[96,1536]{1,0:T(8,128)} async-done(((f32[1536,1536]{1,0:T(8,128)}), f32[96,1536]{1,0:T(8,128)}) %reduce-scatter.16.cloned.1.call-update) | async-done | bytes 589840 | tf_op jit(solution)/shard_map/reduce_scatter | solution.py:400
  1316.7 196.8 %reduce-scatter.14.cloned.1.call-done = f32[96,3072]{1,0:T(8,128)} async-done(((f32[1536,3072]{1,0:T(8,128)}), f32[96,3072]{1,0:T(8,128)}) %reduce-scatter.14.cloned.1.call-update) | async-done | bytes 1179664 | tf_op jit(solution)/shard_map/reduce_scatter | solution.py:399
  1515.8 244.7 %reduce-scatter.20.cloned.1.call-done = f32[256,1536]{1,0:T(8,128)} async-done(((f32[4096,1536]{1,0:T(8,128)}), f32[256,1536]{1,0:T(8,128)}) %reduce-scatter.20.cloned.1.call-update) | async-done | bytes 1572880 | tf_op jit(solution)/shard_map/reduce_scatter | solution.py:403
  1763.0 468.6 %reduce-scatter.18.cloned.1.call-done = f32[96,8192]{1,0:T(8,128)} async-done(((f32[1536,8192]{1,0:T(8,128)}), f32[96,8192]{1,0:T(8,128)}) %reduce-scatter.18.cloned.1.call-update) | async-done | bytes 3145744 | tf_op jit(solution)/shard_map/reduce_scatter | solution.py:402
  2253.1 61.8 %all-reduce.4 = (bf16[1536]{0:T(1024)(128)(2,1)S(1)}, bf16[1536]{0:T(1024)(128)(2,1)S(1)}) all-reduce(f32[1536]{0:T(1024)S(1)} %reshape.1397, f32[1536]{0:T(1024)S(1)} %reshape.1400), channel_id=14, replica_groups=mesh['section'=2,'ctx'=4,'fsdp'=4] {'ctx','fsdp'}, use_global_device_ids=true, to_apply=%region_45.46.clone | all-reduce | flops 3072 | bytes 18432
  2333.5 45.7 %all-gather.36.cloned.1.call-done = bf16[1024,1536]{1,0:T(8,128)(2,1)} async-done(((bf16[256,1536]{1,0:T(8,128)(2,1)}), bf16[1024,1536]{1,0:T(8,128)(2,1)}) %all-gather.36.cloned.1.call-update) | async-done | bytes 3145744 | tf_op jit(solution)/shard_map/all_gather | solution.py:421
  2384.7 110.7 %all-gather.34.cloned.1.call-done = bf16[384,8192]{1,0:T(8,128)(2,1)} async-done(((bf16[96,8192]{1,0:T(8,128)(2,1)}), bf16[384,8192]{1,0:T(8,128)(2,1)}) %all-gather.34.cloned.1.call-update) | async-done | bytes 6291472 | tf_op jit(solution)/shard_map/all_gather | solution.py:418
  (1054 shorter events, 612.7 us)
Async XLA Ops:
  7.2 69.4 %all-gather.38.cloned.1.call-start = ((), (), s32[]{:S(2)}) async-start(), calls=%async_computation.21 | async-start | bytes 11796480 | tf_op jit(solution)/shard_map/all_gather | solution.py:174
  7.9 121.0 %all-gather.24.cloned.1.call-start = ((), (), s32[]{:S(2)}) async-start(), calls=%async_computation.7 | async-start | bytes 3342336 | tf_op jit(solution)/shard_map/all_gather | solution.py:233
  83.4 83.4 %all-gather.40.cloned.1.call-start = ((), (), s32[]{:S(2)}) async-start(), calls=%async_computation.22 | async-start | bytes 5898240 | tf_op jit(solution)/shard_map/all_gather | solution.py:175
  84.2 238.9 %all-gather.42.cloned.1.call-start = ((), (), s32[]{:S(2)}) async-start(), calls=%async_computation.23 | async-start | bytes 31457280 | tf_op jit(solution)/shard_map/all_gather | solution.py:177
  84.8 321.9 %all-gather.44.cloned.1.call-start = ((), (), s32[]{:S(2)}) async-start(), calls=%async_computation.24 | async-start | bytes 15728640 | tf_op jit(solution)/shard_map/all_gather | solution.py:178
  85.3 398.3 %all-gather.26.cloned.1.call-start = ((), (), s32[]{:S(2)}) async-start(), calls=%async_computation.8 | async-start | bytes 3342336 | tf_op jit(solution)/shard_map/all_gather | solution.py:233
  413.5 7.9 collective-permute-start
  437.2 150.3 %all-gather.28.cloned.1.call-start = ((), (), s32[]{:S(2)}) async-start(), calls=%async_computation.9 | async-start | bytes 3342336 | tf_op jit(solution)/shard_map/all_gather | solution.py:233
  527.8 7.9 collective-permute-start.1
  542.4 124.7 %all-gather.46.cloned.1.call-start = ((), (), s32[]{:S(2)}) async-start(), calls=%async_computation.25 | async-start | bytes 3342336 | tf_op jit(solution)/shard_map/all_gather | solution.py:334
  574.9 222.8 %reduce-scatter.8.cloned.1.call-start = ((), (), s32[]{:S(2)}) async-start(), calls=%async_computation.10 | async-start | bytes 6684672 | tf_op jit(solution)/shard_map/reduce_scatter | solution.py:338
  713.2 136.1 %all-gather.48.cloned.1.call-start = ((), (), s32[]{:S(2)}) async-start(), calls=%async_computation.26 | async-start | bytes 3342336 | tf_op jit(solution)/shard_map/all_gather | solution.py:334
  715.5 301.7 %reduce-scatter.10.cloned.1.call-start = ((), (), s32[]{:S(2)}) async-start(), calls=%async_computation.11 | async-start | bytes 6684672 | tf_op jit(solution)/shard_map/reduce_scatter | solution.py:338
  808.8 8.0 collective-permute-start.2
  933.0 135.9 %all-gather.50.cloned.1.call-start = ((), (), s32[]{:S(2)}) async-start(), calls=%async_computation.27 | async-start | bytes 3342336 | tf_op jit(solution)/shard_map/all_gather | solution.py:334
  933.6 265.6 %reduce-scatter.12.cloned.1.call-start = ((), (), s32[]{:S(2)}) async-start(), calls=%async_computation.12 | async-start | bytes 6684672 | tf_op jit(solution)/shard_map/reduce_scatter | solution.py:338
  1115.0 199.8 %reduce-scatter.16.cloned.1.call-start = ((), (), s32[]{:S(2)}) async-start(), calls=%async_computation.15 | async-start | bytes 10027008 | tf_op jit(solution)/shard_map/reduce_scatter | solution.py:400
  1125.2 388.3 %reduce-scatter.14.cloned.1.call-start = ((), (), s32[]{:S(2)}) async-start(), calls=%async_computation.13 | async-start | bytes 20054016 | tf_op jit(solution)/shard_map/reduce_scatter | solution.py:399
  1209.9 550.6 %reduce-scatter.20.cloned.1.call-start = ((), (), s32[]{:S(2)}) async-start(), calls=%async_computation.19 | async-start | bytes 26738688 | tf_op jit(solution)/shard_map/reduce_scatter | solution.py:403
  1233.2 998.3 %reduce-scatter.18.cloned.1.call-start = ((), (), s32[]{:S(2)}) async-start(), calls=%async_computation.17 | async-start | bytes 53477376 | tf_op jit(solution)/shard_map/reduce_scatter | solution.py:402
  1264.6 1061.5 %all-gather.32.cloned.1.call-start = ((), (), s32[]{:S(2)}) async-start(), calls=%async_computation.16 | async-start | bytes 1474560 | tf_op jit(solution)/shard_map/all_gather | solution.py:412
  1316.7 1012.4 %all-gather.30.cloned.1.call-start = ((), (), s32[]{:S(2)}) async-start(), calls=%async_computation.14 | async-start | bytes 2949120 | tf_op jit(solution)/shard_map/all_gather | solution.py:409
  1515.7 863.5 %all-gather.36.cloned.1.call-start = ((), (), s32[]{:S(2)}) async-start(), calls=%async_computation.20 | async-start | bytes 3932160 | tf_op jit(solution)/shard_map/all_gather | solution.py:421
  1762.9 732.5 %all-gather.34.cloned.1.call-start = ((), (), s32[]{:S(2)}) async-start(), calls=%async_computation.18 | async-start | bytes 7864320 | tf_op jit(solution)/shard_map/all_gather | solution.py:418
  (157 other events, 5188.5 us)
Sparse Core Ops, SparseCore 0:
  9.6 66.9 all-gather.37
  83.6 45.3 all-gather.23
  130.5 36.2 all-gather.39
  168.2 154.8 all-gather.41
  324.5 82.1 all-gather.43
  437.4 46.2 all-gather.25
  542.5 45.0 all-gather.27
  589.8 43.9 all-gather.45
  713.3 84.3 reduce-scatter.7
  800.1 44.7 all-gather.47
  933.1 84.0 reduce-scatter.9
  1019.3 44.4 all-gather.49
  1115.1 83.9 reduce-scatter.11
  1204.2 110.5 reduce-scatter.15
  1318.8 194.6 reduce-scatter.13
  1517.5 242.9 reduce-scatter.19
  1764.6 466.9 reduce-scatter.17
  2233.0 29.1 all-gather.31
  2264.3 50.2 all-gather.29
  2316.7 62.4 all-gather.35
  2381.3 113.9 all-gather.33
where the time goes:
time: 2520 us; the launch traced here: 2510 us
  waiting for transfers between devices  1760 us (70%)
  matrix products  299 us (12%)
  local copies, waits for them, and re-layouts  199 us (8%)
  other arithmetic  123 us (5%)
  blocking collectives  81.7 us (3%)
    reduce_scatter x1, waiting for transfers between devices, on_device(): lax.psum_scatter(gate_grad_all, ('ctx', 'fsdp'), scatter_dimension=0, til...  469 us
    reduce_scatter x1, waiting for transfers between devices, on_device(): lax.psum_scatter(down_grad, ('ctx', 'fsdp'), scatter_dimension=0, tiled=T...  245 us
    reduce_scatter x3, waiting for transfers between devices, on_device(): lax.psum_scatter(terms, ('ctx', 'fsdp'), scatter_dimension=0, tiled=True)  229 us
    reduce_scatter x1, waiting for transfers between devices, on_device(): lax.psum_scatter(mix_grad, ('ctx', 'fsdp'), scatter_dimension=0, tiled=True)  197 us
    all_gather x1, waiting for transfers between devices, on_device(): lax.all_gather(gate_up[0], 'fsdp', axis=0, tiled=True)  152 us
    all_gather x1, waiting for transfers between devices, on_device(): lax.all_gather(shares[4].astype(jnp.bfloat16), 'ctx', axis=0, tiled=True)  111 us
    all_gather x3, waiting for transfers between devices, on_device(): lax.all_gather(key_values, ('ctx', 'fsdp'), axis=0, tiled=True)  88.2 us
    all_gather x1, waiting for transfers between devices, on_device(): lax.all_gather(down_weight[0], 'fsdp', axis=0, tiled=True)  72.6 us
  transfers between devices with their start and end apart: 25, of which 20 were waited for; matrix products, arithmetic and copies ran while one was open for 14% of the time, Pallas kernels for 0%

commit v1 on v0

v1 whole, which is shorter than its diff:
```python
import jax
import jax.numpy as jnp
from jax import lax
from jax.experimental import pallas as pl
from jax.experimental.pallas import tpu as pltpu
from jax.sharding import PartitionSpec as P

MESH = pl.DeviceIdType.MESH


def greet():
    c = lax.axis_index("ctx")
    f = lax.axis_index("fsdp")
    barrier = pltpu.get_barrier_semaphore()
    inner = jnp.logical_and(c > 0, c < 3)
    for peer in (f + 2 - 4 * (f // 2), f + 1 - 2 * lax.rem(f, 2)):
        pl.semaphore_signal(barrier, inc=1, device_id={"fsdp": peer}, device_id_type=MESH)

    @pl.when(c < 3)
    def _():
        pl.semaphore_signal(barrier, inc=1, device_id={"ctx": c + 1}, device_id_type=MESH)

    @pl.when(c > 0)
    def _():
        pl.semaphore_signal(barrier, inc=1, device_id={"ctx": c - 1}, device_id_type=MESH)

    @pl.when(inner)
    def _():
        pl.semaphore_wait(barrier, 4)

    @pl.when(jnp.logical_not(inner))
    def _():
        pl.semaphore_wait(barrier, 3)


def near_order(c):
    low = c < 2
    return [c, c + 1 - 2 * lax.rem(c, 2), jnp.where(low, 2, 1), jnp.where(low, 3, 0)]


def gather_rows(own, whole, send, recv):
    c = lax.axis_index("ctx")
    f = lax.axis_index("fsdp")
    across = f + 2 - 4 * (f // 2)
    twin = f + 1 - 2 * lax.rem(f, 2)
    cross = across + 1 - 2 * lax.rem(f, 2)
    inner = jnp.logical_and(c > 0, c < 3)
    rows = own.shape[0]
    order = near_order(c)

    def at(cc, ff):
        return whole.at[pl.ds(pl.multiple_of((cc * 4 + ff) * rows, rows), rows)]

    def copy(src, dst, slot, arrival, peer):
        return pltpu.make_async_remote_copy(
            src, dst, send.at[slot], recv.at[arrival], device_id=peer, device_id_type=MESH
        )

    up = copy(own, at(c, f), 0, c, {"ctx": jnp.minimum(c + 1, 3)})
    down = copy(own, at(c, f), 1, c, {"ctx": jnp.maximum(c - 1, 0)})
    pl.when(c < 3)(up.start)
    pl.when(c > 0)(down.start)
    sent = []
    forwards = []
    first = copy(own, at(c, f), 2, 4 + c, {"fsdp": across})
    first.start()
    second = copy(own, at(c, f), 6, 8 + c, {"fsdp": twin})
    second.start()
    sent += [first, second]
    whole[pl.ds(pl.multiple_of((c * 4 + f) * rows, rows), rows), :] = own[...]

    def spread_across(step):
        d = order[step]
        block = at(d, across)
        copy(block, block, 0, 4 + d, {"fsdp": across}).wait_recv()
        one = copy(block, block, 10 + step, 12 + d, {"fsdp": twin})
        one.start()
        sent.append(one)

    for step in range(1, 4):
        d = order[step]
        block = at(d, f)
        copy(block, block, 0, d, {"fsdp": twin}).wait_recv()
        onward = jnp.where(d < c, jnp.minimum(c + 1, 3), jnp.maximum(c - 1, 0))
        forward = copy(block, block, 13 + step, d, {"ctx": onward})
        pl.when(inner)(forward.start)
        forwards.append(forward)
        one = copy(block, block, 2 + step, 4 + d, {"fsdp": across})
        one.start()
        two = copy(block, block, 6 + step, 8 + d, {"fsdp": twin})
        two.start()
        sent += [one, two]
        spread_across(step - 1)
    spread_across(3)
    for step in range(4):
        d = order[step]
        copy(at(d, twin), at(d, twin), 0, 8 + d, {"fsdp": twin}).wait_recv()
        copy(at(d, cross), at(d, cross), 0, 12 + d, {"fsdp": twin}).wait_recv()
    pl.when(c < 3)(up.wait_send)
    pl.when(c > 0)(down.wait_send)
    for forward in forwards:
        pl.when(inner)(forward.wait_send)
    for one in sent:
        one.wait_send()


GATHER_SENDS = 17
GATHER_RECVS = 16


def scatter_sum(part, total, land, send, recv):
    c = lax.axis_index("ctx")
    f = lax.axis_index("fsdp")
    across = f + 2 - 4 * (f // 2)
    twin = f + 1 - 2 * lax.rem(f, 2)
    cross = across + 1 - 2 * lax.rem(f, 2)
    inner = jnp.logical_and(c > 0, c < 3)
    rows = total.shape[0]
    order = near_order(c)[::-1]

    def rows_at(cc, ff):
        return pl.ds(pl.multiple_of((cc * 4 + ff) * rows, rows), rows)

    def at(cc, ff):
        return part.at[rows_at(cc, ff)]

    def copy(src, dst, slot, arrival, peer):
        return pltpu.make_async_remote_copy(
            src, dst, send.at[slot], recv.at[arrival], device_id=peer, device_id_type=MESH
        )

    def landed(slot):
        copy(land.at[slot], land.at[slot], 0, slot, {"fsdp": twin}).wait_recv()
        return land[slot].astype(jnp.float32)

    sent = []
    for step in range(4):
        d = order[step]
        one = copy(at(d, cross), land.at[step], step, step, {"fsdp": twin})
        one.start()
        two = copy(at(d, twin), land.at[4 + step], 4 + step, 4 + step, {"fsdp": twin})
        two.start()
        sent += [one, two]

    def over(step):
        d = order[step]
        mine = rows_at(d, across)
        part[mine, :] = (part[mine, :].astype(jnp.float32) + landed(step)).astype(part.dtype)
        one = copy(at(d, across), land.at[8 + step], 8 + step, 8 + step, {"fsdp": across})
        one.start()
        sent.append(one)

    over(0)
    lines = []
    for step in range(4):
        d = order[step]
        mine = rows_at(d, f)
        if step < 3:
            over(step + 1)
        value = part[mine, :].astype(jnp.float32) + landed(4 + step) + landed(8 + step)
        if step < 3:
            part[mine, :] = value.astype(part.dtype)

            @pl.when(inner)
            def _():
                part[mine, :] = (value + landed(12 + d)).astype(part.dtype)

            onward = jnp.where(d > c, c + 1, c - 1)
            slot = jnp.where(jnp.logical_and(d < c, d == c - 1), 16, 12 + d)
            line = copy(at(d, f), land.at[slot], 12 + step, slot, {"ctx": onward})
            line.start()
            sent.append(line)
        else:
            total[...] = value

            @pl.when(c > 0)
            def _():
                total[...] += landed(12 + c)

            @pl.when(c < 3)
            def _():
                total[...] += landed(16)
    for one in sent:
        one.wait_send()


SCATTER_SENDS = 15
SCATTER_RECVS = 17


def gather_kernel(own, whole, send, recv):
    greet()
    gather_rows(own, whole, send, recv)


def scatter_kernel(part, total, work, land, send, recv):
    greet()
    work[...] = part[...]
    scatter_sum(work, total, land, send, recv)


def gather_call(own):
    rows, w = own.shape
    return pl.pallas_call(
        gather_kernel,
        out_shape=jax.ShapeDtypeStruct((16 * rows, w), own.dtype),
        in_specs=[pl.BlockSpec(memory_space=pltpu.VMEM)],
        out_specs=pl.BlockSpec(memory_space=pltpu.VMEM),
        scratch_shapes=[pltpu.SemaphoreType.DMA((GATHER_SENDS,)), pltpu.SemaphoreType.DMA((GATHER_RECVS,))],
        compiler_params=pltpu.CompilerParams(collective_id=0, has_side_effects=True, vmem_limit_bytes=48 << 20),
    )(own)


def scatter_call(part):
    w = part.shape[1]
    rows = part.shape[0] // 16
    return pl.pallas_call(
        scatter_kernel,
        out_shape=jax.ShapeDtypeStruct((rows, w), jnp.float32),
        in_specs=[pl.BlockSpec(memory_space=pltpu.VMEM)],
        out_specs=pl.BlockSpec(memory_space=pltpu.VMEM),
        scratch_shapes=[
            pltpu.VMEM(part.shape, part.dtype),
            pltpu.VMEM((17, rows, w), part.dtype),
            pltpu.SemaphoreType.DMA((SCATTER_SENDS,)), pltpu.SemaphoreType.DMA((SCATTER_RECVS,))],
        compiler_params=pltpu.CompilerParams(collective_id=1, has_side_effects=True, vmem_limit_bytes=48 << 20),
    )(part)


KV_HEADS = 8
HEAD = 96
LANES = 128
SPAN = 64
norm_eps = 1e-05
rope_base = 100000.0
masked_value = -1e30
BF = jnp.bfloat16
F32 = jnp.float32


def on_line():
    return lax.axis_size("ctx") == 4 and lax.axis_size("fsdp") == 4


def gather(own):
    if on_line():
        return gather_call(own)
    return lax.all_gather(own, ("ctx", "fsdp"), axis=0, tiled=True)


def scatter(part):
    if on_line():
        return scatter_call(part.astype(BF))
    return lax.psum_scatter(part, ("ctx", "fsdp"), scatter_dimension=0, tiled=True)


def spread_halves(columns):
    halves = columns.reshape(columns.shape[:-1] + (2, HEAD // 2))
    halves = jnp.pad(halves, [(0, 0)] * (halves.ndim - 1) + [(0, SPAN - HEAD // 2)])
    return halves.reshape(columns.shape[:-1] + (LANES,))


def join_halves(columns):
    halves = columns.reshape(columns.shape[:-1] + (2, SPAN))[..., : HEAD // 2]
    return halves.reshape(columns.shape[:-1] + (HEAD,))


def angle_tables(positions):
    frequency = rope_base ** (-(jnp.arange(HEAD // 2, dtype=F32) * 2.0 / HEAD))
    frequency = jnp.pad(frequency, (0, SPAN - HEAD // 2))
    angles = positions.astype(F32)[:, None] * frequency[None, :]
    cosine = jnp.cos(angles)
    sine = jnp.sin(angles)
    return jnp.concatenate([cosine, cosine], axis=1), jnp.concatenate([-sine, sine], axis=1)


def rotate(values, cosine, sine):
    return values * cosine + jnp.roll(values, SPAN, axis=1) * sine


def rotate_back(grads, cosine, sine):
    return grads * cosine - jnp.roll(grads, SPAN, axis=1) * sine


def norm_rows(values):
    return lax.rsqrt(jnp.mean(values * values, axis=-1, keepdims=True) + norm_eps)


def norm_back(grad_out, values, factor, gain):
    shaped = grad_out * gain
    common = jnp.mean(shaped * values, axis=-1, keepdims=True)
    grad_in = factor * shaped - values * (factor * factor * factor) * common
    return grad_in, jnp.sum(grad_out * values * factor, axis=0)


def dot(left, right):
    return jnp.dot(left, right, preferred_element_type=F32)


def dot_nt(left, right):
    return lax.dot_general(left, right, (((1,), (1,)), ((), ())), preferred_element_type=F32)


def dot_tn(left, right):
    return lax.dot_general(left, right, (((0,), (0,)), ((), ())), preferred_element_type=F32)


class Plan:
    def __init__(self, width, hidden_units):
        self.c = lax.axis_index("ctx")
        self.f = lax.axis_index("fsdp")
        self.C = lax.axis_size("ctx")
        self.F = lax.axis_size("fsdp")
        self.heads = width // HEAD
        self.ratio = self.heads // KV_HEADS
        self.heads_f = self.heads // self.F
        self.groups_f = KV_HEADS // self.F
        self.share = self.C // self.heads_f
        self.units = hidden_units // (self.F * self.C)
        self.local_head = self.c // self.share
        self.part = self.c % self.share


def pick(array, index, axis):
    return lax.dynamic_index_in_dim(array, index, axis, keepdims=False)


def pack_weights(plan, mix, gate_up):
    depth = mix.shape[0]
    width = plan.heads * HEAD
    kv_width = KV_HEADS * HEAD
    F = plan.F
    queries = pick(mix[:, :width].reshape(depth, F, plan.heads_f, HEAD), plan.local_head, 2)
    group = plan.local_head // plan.ratio
    keys = pick(mix[:, width : width + kv_width].reshape(depth, F, plan.groups_f, HEAD), group, 2)
    values = pick(mix[:, width + kv_width :].reshape(depth, F, plan.groups_f, HEAD), group, 2)
    values = jnp.pad(values, ((0, 0), (0, 0), (0, LANES - HEAD)))
    half = gate_up.shape[1] // 2
    gate = pick(gate_up[:, :half].reshape(depth, F, plan.C, plan.units), plan.c, 2)
    up = pick(gate_up[:, half:].reshape(depth, F, plan.C, plan.units), plan.c, 2)
    packed = jnp.concatenate([spread_halves(queries), spread_halves(keys), values, gate, up], axis=2)
    return jnp.swapaxes(packed, 0, 1)


def attend(plan, q_part, k, v, positions, part_positions):
    scores = dot_nt(q_part, k) * HEAD ** (-0.5)
    allowed = positions[None, :] <= part_positions[:, None]
    scores = jnp.where(allowed, scores, masked_value)
    top = jnp.max(scores, axis=-1, keepdims=True)
    weights = jnp.exp(scores - top)
    total = jnp.sum(weights, axis=-1, keepdims=True)
    context = dot((weights / total).astype(BF), v)
    return context.astype(BF), top + jnp.log(total)


def attend_back(q_part, k, v, context_grad, context, log_total, positions, part_positions):
    scale = HEAD ** (-0.5)
    common = jnp.sum(context_grad.astype(F32) * context.astype(F32), axis=-1, keepdims=True)
    allowed = positions[None, :] <= part_positions[:, None]
    scores = dot_nt(q_part, k) * scale
    weights = jnp.exp(jnp.where(allowed, scores, masked_value) - log_total)
    weight_grad = dot_nt(context_grad, v)
    score_grad = (weights * (weight_grad - common)).astype(BF)
    value_grad = dot_tn(weights.astype(BF), context_grad)
    key_grad = dot_tn(score_grad, q_part) * scale
    query_grad = dot(score_grad, k) * scale
    return query_grad, key_grad, value_grad


def forward_layer(plan, x_own, weights, gains, positions, part_positions, tables):
    cut, out, down = weights
    cosine, sine = tables
    length = positions.shape[0]
    x_all = gather(x_own)
    x32 = x_all.astype(F32)
    factor = norm_rows(x32)
    normed = (x32 * factor * gains[0]).astype(BF)
    mixed = dot(normed, cut[:, : 3 * LANES])
    q = rotate(mixed[:, :LANES], cosine, sine).astype(BF)
    k = rotate(mixed[:, LANES : 2 * LANES], cosine, sine).astype(BF)
    v = mixed[:, 2 * LANES :].astype(BF)
    rows = length // plan.share
    start = plan.part * rows
    q_part = lax.dynamic_slice_in_dim(q, start, rows, 0)
    context, log_total = attend(plan, q_part, k, v, positions, part_positions)
    partial = dot(context[:, :HEAD], out).astype(BF)
    if plan.share > 1:
        partial = lax.dynamic_update_slice_in_dim(
            jnp.zeros((length, partial.shape[1]), BF), partial, start, 0
        )
    middle = x_own.astype(F32) + scatter(partial)
    factor_two = norm_rows(middle)
    normed_two = gather((middle * factor_two * gains[1]).astype(BF))
    both = dot(normed_two, cut[:, 3 * LANES :])
    hidden = (jax.nn.silu(both[:, : plan.units]) * both[:, plan.units :]).astype(BF)
    result = middle + scatter(dot(hidden, down).astype(BF))
    kept = (x_own, normed, q_part, k, v, context, log_total, middle, normed_two, both, hidden)
    return result.astype(BF), kept


def backward_layer(plan, grad_own, weights, gains, kept, positions, part_positions, tables, part_tables):
    cut, out, down = weights
    x_own, normed, q_part, k, v, context, log_total, middle, normed_two, both, hidden = kept
    length = positions.shape[0]
    rows = length // plan.share
    start = plan.part * rows
    grad_all = gather(grad_own)
    hidden_grad = dot_nt(grad_all, down)
    gate = both[:, : plan.units]
    up = both[:, plan.units :]
    sig = jax.nn.sigmoid(gate)
    gate_grad = hidden_grad * up * sig * (1.0 + gate * (1.0 - sig))
    up_grad = hidden_grad * gate * sig
    both_grad = jnp.concatenate([gate_grad, up_grad], axis=1).astype(BF)
    normed_two_grad = scatter(dot_nt(both_grad, cut[:, 3 * LANES :]).astype(BF))
    middle_grad, feed_gain_grad = norm_back(normed_two_grad, middle, norm_rows(middle), gains[1])
    middle_grad = middle_grad + grad_own.astype(F32)
    middle_low = gather(middle_grad.astype(BF))
    middle_part = lax.dynamic_slice_in_dim(middle_low, start, rows, 0)
    context_grad = jnp.pad(dot_nt(middle_part, out), ((0, 0), (0, LANES - HEAD))).astype(BF)
    query_grad, key_grad, value_grad = attend_back(
        q_part, k, v, context_grad, context, log_total, positions, part_positions
    )
    query_grad = rotate_back(query_grad, *part_tables).astype(BF)
    if plan.share > 1:
        query_grad = lax.dynamic_update_slice_in_dim(
            jnp.zeros((length, LANES), BF), query_grad, start, 0
        )
    key_grad = rotate_back(key_grad, *tables).astype(BF)
    mixed_grad = jnp.concatenate([query_grad, key_grad, value_grad.astype(BF)], axis=1)
    normed_grad = scatter(dot_nt(mixed_grad, cut[:, : 3 * LANES]).astype(BF))
    x32 = x_own.astype(F32)
    start_grad, attention_gain_grad = norm_back(normed_grad, x32, norm_rows(x32), gains[0])
    start_grad = start_grad + middle_grad
    cut_grad = jnp.concatenate(
        [dot_tn(normed, mixed_grad).astype(BF), dot_tn(normed_two, both_grad).astype(BF)], axis=1
    )
    out_grad = dot_tn(context, middle_part).astype(BF)[:HEAD]
    down_grad = dot_tn(hidden, grad_all).astype(BF)
    return start_grad, (cut_grad, out_grad, down_grad), (attention_gain_grad, feed_gain_grad)


def swap_sections(array):
    return lax.ppermute(array, "section", [(0, 1), (1, 0)])


def on_device(
    inputs, cotangent, attention_gain, query_key_value, output_weight, feed_gain, gate_up, down_weight, block_order
):
    section = lax.axis_index("section")
    width = inputs.shape[2]
    hidden_units = down_weight.shape[1] * lax.axis_size("fsdp")
    plan = Plan(width, hidden_units)
    rows = inputs.shape[1]
    C, F = plan.C, plan.F
    length = rows * C * F
    depth = query_key_value.shape[1]

    def by_layer(own, other):
        first = section == 0
        return jnp.where(first, own, other), jnp.where(first, other, own)

    order = pick(block_order, section, 0)
    positions = (order[:, None] * rows + jnp.arange(rows, dtype=jnp.int32)[None, :]).reshape(length)
    part_rows = length // plan.share
    part_positions = lax.dynamic_slice_in_dim(positions, plan.part * part_rows, part_rows, 0)
    tables = angle_tables(positions)
    part_tables = angle_tables(part_positions)

    gains = lax.all_gather(
        jnp.stack([attention_gain[0], feed_gain[0]]), ("section", "fsdp"), axis=0, tiled=False
    )
    gains = gains.reshape(2, F, 2, depth)
    gains = jnp.swapaxes(gains, 1, 2).reshape(2, 2, width).astype(F32)

    packed = pack_weights(plan, query_key_value[0], gate_up[0])
    own_cut = lax.all_to_all(packed, "fsdp", 0, 0).reshape(width, -1)
    own_out = lax.dynamic_slice_in_dim(output_weight[0], plan.local_head * HEAD, HEAD, 0)
    own_down = lax.dynamic_slice_in_dim(down_weight[0], plan.c * plan.units, plan.units, 0)
    cuts = by_layer(own_cut, swap_sections(own_cut))
    outs = by_layer(own_out, swap_sections(own_out))
    downs = by_layer(own_down, swap_sections(own_down))
    weights = [(cuts[s], outs[s], downs[s]) for s in range(2)]

    x = pick(inputs, section, 0)
    kept = []
    results = []
    for s in range(2):
        x, keep = forward_layer(plan, x, weights[s], gains[s], positions, part_positions, tables)
        kept.append(keep)
        results.append(x)
    grad = pick(cotangent, section, 0)
    input_grads = [None, None]
    weight_grads = [None, None]
    gain_grads = [None, None]
    for s in (1, 0):
        start_grad, weight_grads[s], gain_grads[s] = backward_layer(
            plan, grad, weights[s], gains[s], kept[s], positions, part_positions, tables, part_tables
        )
        input_grads[s] = start_grad
        grad = start_grad.astype(BF)

    def mine_and_theirs(first, second):
        return jnp.where(section == 0, first, second), jnp.where(section == 0, second, first)

    def by_batch(first, second):
        own, away = mine_and_theirs(first, second)
        return jnp.stack(by_layer(own, swap_sections(away)))

    section_outputs = by_batch(*results)
    section_input_grads = by_batch(*input_grads)

    def collected(index):
        own, away = mine_and_theirs(weight_grads[0][index], weight_grads[1][index])
        return (own.astype(F32) + swap_sections(away).astype(F32)).astype(BF)

    cut_grad = collected(0)
    cut_grad = lax.all_to_all(cut_grad.reshape(F, depth, -1), "fsdp", 0, 0)
    cut_grad = lax.all_gather(cut_grad, "ctx", axis=0, tiled=False)
    out_grad = lax.all_gather(collected(1), "ctx", axis=0, tiled=False)
    down_grad = lax.all_gather(collected(2), "ctx", axis=0, tiled=True).astype(F32)

    def heads_of(columns, count):
        folded = columns.astype(F32).reshape(count, C // count, F, depth, columns.shape[-1]).sum(axis=1)
        return jnp.transpose(folded, (2, 1, 0, 3))

    q_grad = join_halves(heads_of(cut_grad[..., :LANES], plan.heads_f)).reshape(depth, -1)
    k_grad = join_halves(heads_of(cut_grad[..., LANES : 2 * LANES], plan.groups_f)).reshape(depth, -1)
    v_grad = heads_of(cut_grad[..., 2 * LANES : 3 * LANES], plan.groups_f)[..., :HEAD].reshape(depth, -1)
    mix_grad = jnp.concatenate([q_grad, k_grad, v_grad], axis=1)
    both = jnp.transpose(cut_grad[..., 3 * LANES :], (2, 1, 0, 3)).astype(F32)
    gate_up_grad = jnp.concatenate(
        [both[..., : plan.units].reshape(depth, -1), both[..., plan.units :].reshape(depth, -1)], axis=1
    )
    out_grad = out_grad.astype(F32).reshape(plan.heads_f, plan.share, HEAD, width).sum(axis=1).reshape(-1, width)

    gain_sum = jnp.stack([jnp.stack(gain_grads[0]), jnp.stack(gain_grads[1])])
    gain_sum = lax.psum(gain_sum, ("section", "ctx", "fsdp"))
    gain_sum = lax.dynamic_slice_in_dim(pick(gain_sum, section, 0), plan.f * depth, depth, 1)
    return (
        section_outputs[None],
        section_input_grads[None],
        gain_sum[0][None],
        mix_grad[None],
        out_grad[None],
        gain_sum[1][None],
        gate_up_grad[None],
        down_grad[None],
    )


def solution(mesh):
    placed = (
        P(None, ("ctx", "fsdp"), None),
        P(None, ("ctx", "fsdp"), None),
        P("section", "fsdp"),
        P("section", "fsdp", None),
        P("section", "fsdp", None),
        P("section", "fsdp"),
        P("section", "fsdp", None),
        P("section", "fsdp", None),
        P(),
    )
    return jax.shard_map(
        on_device,
        mesh=mesh,
        in_specs=placed,
        out_specs=(
            P("section", None, ("ctx", "fsdp"), None),
            P("section", None, ("ctx", "fsdp"), None),
            P("section", "fsdp"),
            P("section", "fsdp", None),
            P("section", "fsdp", None),
            P("section", "fsdp"),
            P("section", "fsdp", None),
            P("section", "fsdp", None),
        ),
        check_vma=False,
    )
```

time: 2520 us -> 1010 us (0.40)
  waiting for transfers between devices: 1760 us -> 122 us
  Pallas kernels: 0 us -> 444 us
  matrix products: 299 us -> 65.1 us
  blocking collectives: 81.7 us -> 162 us
  local copies, waits for them, and re-layouts: 199 us -> 119 us
  other arithmetic: 123 us -> 63.5 us
    reduce_scatter x7 -> x0, waiting for transfers between devices: 1190 us -> none  [the longest x1 469 us: on_device(): lax.psum_scatter(gate_grad_all, ('ctx', 'fsdp'), scatter_dimension=0, til...]
    all_gather x14 -> x3, waiting for transfers between devices: 550 us -> 41.1 us  [the longest x1 41.1 us: on_device(): cut_grad = lax.all_gather(cut_grad, 'ctx', axis=0, tiled=False)]
    pallas_call x0 -> x16, Pallas kernels: none -> 444 us  [the longest x8 249 us: scatter_call(): pl.pallas_call(scatter_kernel, out_shape=jax.ShapeDtypeStruct((rows, w),...]
    dot_general x154 -> x36, matrix products: 299 us -> 65.1 us  [the longest x12 26 us: dot_nt(): lax.dot_general(left, right, (((1,), (1,)), ((), ())), preferred_element_...]
    all_to_all x0 -> x2, blocking collectives: none -> 74.4 us  [the longest x1 37.4 us: on_device(): cut_grad = lax.all_to_all(cut_grad.reshape(F, depth, -1), 'fsdp', 0, 0)]
    unnamed x2 -> x0, blocking collectives: 70.1 us -> none
    ppermute x4 -> x8, waiting for transfers between devices: 18.5 us -> 80.8 us  [swap_sections(): return lax.ppermute(array, 'section', [(0, 1), (1, 0)])]
    psum x0 -> x1, blocking collectives: none -> 56.1 us  [on_device(): gain_sum = lax.psum(gain_sum, ('section', 'ctx', 'fsdp'))]
  transfers between devices with their start and end apart: 25 -> 11, of which waited for: 20 -> 3; matrix products, arithmetic and copies ran while one was open for 14% -> 5% of each run, Pallas kernels for 0% -> 20%
where the time goes in v1:
time: 1010 us; the launch traced here: 1000 us
  Pallas kernels  444 us (44%)
  blocking collectives  162 us (16%)
  waiting for transfers between devices  122 us (12%)
  local copies, waits for them, and re-layouts  119 us (12%)
  matrix products  65.1 us (6%)
  other arithmetic  63.5 us (6%)
  between operations  15.8 us (2%)
    pallas_call x8, Pallas kernels, scatter_call(): pl.pallas_call(scatter_kernel, out_shape=jax.ShapeDtypeStruct((rows, w),...  249 us
    pallas_call x8, Pallas kernels, gather_call(): pl.pallas_call(gather_kernel, out_shape=jax.ShapeDtypeStruct((16 * rows,...  196 us
    ppermute x8, waiting for transfers between devices, swap_sections(): return lax.ppermute(array, 'section', [(0, 1), (1, 0)])  80.8 us
    psum x1, blocking collectives, on_device(): gain_sum = lax.psum(gain_sum, ('section', 'ctx', 'fsdp'))  56.1 us
    unnamed x169, local copies, waits for them, and re-layouts  42.9 us
    all_gather x1, waiting for transfers between devices, on_device(): cut_grad = lax.all_gather(cut_grad, 'ctx', axis=0, tiled=False)  41.1 us
    all_to_all x1, blocking collectives, on_device(): cut_grad = lax.all_to_all(cut_grad.reshape(F, depth, -1), 'fsdp', 0, 0)  37.4 us
    all_to_all x1, blocking collectives, on_device(): own_cut = lax.all_to_all(packed, 'fsdp', 0, 0).reshape(width, -1)  37 us
  transfers between devices with their start and end apart: 11, of which 3 were waited for; matrix products, arithmetic and copies ran while one was open for 5% of the time, Pallas kernels for 20%

profile of v1, /device:TPU:0, one launch (start us, length us, event | category | flops | bytes accessed | tf_op | source)
XLA Modules:
  0.0 1001.8 jit_solution(8967126731892083514)
XLA Ops:
  61.3 37.0 %all_to_all.10 = bf16[4,384,896]{1,2,0:T(8,128)(2,1)S(1)} all-to-all(bf16[4,384,896]{1,2,0:T(8,128)(2,1)} %bitcast.139), channel_id=1, replica_groups=mesh['section'=2,'ctx'=4,'fsdp'=4] {'fsdp'}, dimensions={0} | all-to-all | bytes 5505024 | tf_op jit(solution)/shard_map/all_to_all | solution.py:477
  107.3 24.1 %shard_map.160 = bf16[1024,1536]{1,0:T(8,128)(2,1)S(1)} custom-call(bf16[64,1536]{1,0:T(8,128)(2,1)S(1)} %dynamic-slice_bitcast_fusion.3.own), custom_call_target="tpu_custom_call" | custom-call | tf_op jit(solution)/shard_map/pallas_call | solution.py:204
  132.1 25.9 %shard_map.152 = bf16[1024,1536]{1,0:T(8,128)(2,1)S(1)} custom-call(bf16[64,1536]{1,0:T(8,128)(2,1)S(1)} %get-tuple-element.57.own), custom_call_target="tpu_custom_call" | custom-call | tf_op jit(solution)/shard_map/pallas_call | solution.py:204
  158.0 31.3 %all-gather.3 = bf16[8,2,384]{2,1,0:T(2,128)(2,1)S(1)} all-gather(bf16[1,2,384]{2,1,0:T(2,128)(2,1)S(1)} %maximum_bitcast_fusion.6), channel_id=2, replica_groups=mesh['section'=2,'ctx'=4,'fsdp'=4] {'section','fsdp'}, dimensions={0}, use_global_device_ids=true | all-gather | bytes 13824 | tf_op jit(solution)/shard_map/all_gather | solution.py:470
  203.5 26.7 %shard_map.153 = f32[64,1536]{1,0:T(8,128)S(1)} custom-call(bf16[1024,1536]{1,0:T(8,128)(2,1)S(1)} %convolution_convert_fusion.7.part), custom_call_target="tpu_custom_call" | custom-call | tf_op jit(solution)/shard_map/pallas_call | solution.py:217
  231.0 24.1 %shard_map.154 = bf16[1024,1536]{1,0:T(8,128)(2,1)S(1)} custom-call(bf16[64,1536]{1,0:T(8,128)(2,1)S(1)} %multiply_convert_fusion.9.own), custom_call_target="tpu_custom_call" | custom-call | tf_op jit(solution)/shard_map/pallas_call | solution.py:204
  260.7 25.3 %shard_map.155 = f32[64,1536]{1,0:T(8,128)S(1)} custom-call(bf16[1024,1536]{1,0:T(8,128)(2,1)S(1)} %convolution_convert_fusion.1.part), custom_call_target="tpu_custom_call" | custom-call | tf_op jit(solution)/shard_map/pallas_call | solution.py:217
  286.7 24.1 %shard_map.156 = bf16[1024,1536]{1,0:T(8,128)(2,1)S(1)} custom-call(bf16[64,1536]{1,0:T(8,128)(2,1)S(1)} %get-tuple-element.63.own), custom_call_target="tpu_custom_call" | custom-call | tf_op jit(solution)/shard_map/pallas_call | solution.py:204
  320.3 25.3 %shard_map.157 = f32[64,1536]{1,0:T(8,128)S(1)} custom-call(bf16[1024,1536]{1,0:T(8,128)(2,1)S(1)} %convolution_convert_fusion.6.part), custom_call_target="tpu_custom_call" | custom-call | tf_op jit(solution)/shard_map/pallas_call | solution.py:217
  345.9 24.4 %shard_map.158 = bf16[1024,1536]{1,0:T(8,128)(2,1)S(1)} custom-call(bf16[64,1536]{1,0:T(8,128)(2,1)S(1)} %multiply_convert_fusion.8.own), custom_call_target="tpu_custom_call" | custom-call | tf_op jit(solution)/shard_map/pallas_call | solution.py:204
  380.2 24.8 %shard_map.161 = f32[64,1536]{1,0:T(8,128)S(1)} custom-call(bf16[1024,1536]{1,0:T(8,128)(2,1)S(1)} %convolution_convert_fusion.5.part), custom_call_target="tpu_custom_call" | custom-call | tf_op jit(solution)/shard_map/pallas_call | solution.py:217
  405.5 24.6 %shard_map.162 = bf16[1024,1536]{1,0:T(8,128)(2,1)S(1)} custom-call(bf16[64,1536]{1,0:T(8,128)(2,1)S(1)} %get-tuple-element.64.own), custom_call_target="tpu_custom_call" | custom-call | tf_op jit(solution)/shard_map/pallas_call | solution.py:204
  444.7 25.3 %shard_map.163 = f32[64,1536]{1,0:T(8,128)S(1)} custom-call(bf16[1024,1536]{1,0:T(8,128)(2,1)S(1)} %convolution_convert_fusion.4.part), custom_call_target="tpu_custom_call" | custom-call | tf_op jit(solution)/shard_map/pallas_call | solution.py:217
  471.6 24.3 %shard_map.164 = bf16[1024,1536]{1,0:T(8,128)(2,1)S(1)} custom-call(bf16[64,1536]{1,0:T(8,128)(2,1)S(1)} %get-tuple-element.60.own), custom_call_target="tpu_custom_call" | custom-call | tf_op jit(solution)/shard_map/pallas_call | solution.py:204
  502.3 24.8 %shard_map.165 = f32[64,1536]{1,0:T(8,128)S(1)} custom-call(bf16[1024,1536]{1,0:T(8,128)(2,1)S(1)} %convolution_convert_fusion.3.part), custom_call_target="tpu_custom_call" | custom-call | tf_op jit(solution)/shard_map/pallas_call | solution.py:217
  528.8 24.1 %shard_map.166 = bf16[1024,1536]{1,0:T(8,128)(2,1)S(1)} custom-call(bf16[64,1536]{1,0:T(8,128)(2,1)S(1)} %get-tuple-element.58.own), custom_call_target="tpu_custom_call" | custom-call | tf_op jit(solution)/shard_map/pallas_call | solution.py:204
  566.3 23.0 %collective-permute-done.6 = bf16[96,1536]{1,0:T(8,128)(2,1)S(1)} collective-permute-done((bf16[96,1536]{1,0:T(8,128)(2,1)S(1)}, bf16[96,1536]{1,0:T(8,128)(2,1)S(1)}, u32[]{:S(2)}, u32[]{:S(2)}) %collective-permute-start.6) | collective-permute-done | bytes 294944 | tf_op jit(solution)/shard_map/ppermute | solution.py:444
  600.2 57.8 %collective-permute-done.5 = bf16[1536,896]{0,1:T(8,128)(2,1)} collective-permute-done((bf16[1536,896]{0,1:T(8,128)(2,1)S(1)}, bf16[1536,896]{0,1:T(8,128)(2,1)}, u32[]{:S(2)}, u32[]{:S(2)}) %collective-permute-start.5) | collective-permute-done | bytes 2752544 | tf_op jit(solution)/shard_map/ppermute | solution.py:444
  664.7 37.4 %all_to_all.11 = bf16[4,384,896]{2,1,0:T(8,128)(2,1)} all-to-all(bf16[4,384,896]{2,1,0:T(8,128)(2,1)} %bitcast.126), channel_id=1, replica_groups=mesh['section'=2,'ctx'=4,'fsdp'=4] {'fsdp'}, dimensions={0} | all-to-all | bytes 5505024 | tf_op jit(solution)/shard_map/all_to_all | solution.py:518
  704.4 44.5 %shard_map.159 = f32[64,1536]{1,0:T(8,128)S(1)} custom-call(bf16[1024,1536]{1,0:T(8,128)(2,1)S(1)} %convolution_convert_fusion.part), custom_call_target="tpu_custom_call" | custom-call | tf_op jit(solution)/shard_map/pallas_call | solution.py:217
  753.7 52.1 %shard_map.167 = f32[64,1536]{1,0:T(8,128)S(1)} custom-call(bf16[1024,1536]{1,0:T(8,128)(2,1)S(1)} %convolution_convert_fusion.2.part), custom_call_target="tpu_custom_call" | custom-call | tf_op jit(solution)/shard_map/pallas_call | solution.py:217
  806.6 56.1 %psum.7 = f32[2,2,1536]{2,1,0:T(2,128)S(1)} all-reduce(f32[2,2,1536]{2,1,0:T(2,128)S(1)} %pad_maximum_fusion.16), channel_id=1, replica_groups=mesh['section'=2,'ctx'=4,'fsdp'=4] {'section','ctx','fsdp'}, use_global_device_ids=true, to_apply=%region_20.21 | all-reduce | flops 6144 | bytes 49152 | tf_op jit(solution)/shard_map/psum | solution.py:538
  873.6 41.1 %all-gather.10.cloned.1.call-done = bf16[16,384,896]{2,1,0:T(8,128)(2,1)} async-done(((bf16[4,384,896]{2,1,0:T(8,128)(2,1)}), bf16[16,384,896]{2,1,0:T(8,128)(2,1)}) %all-gather.10.cloned.1.call-update) | async-done | bytes 11010064 | tf_op jit(solution)/shard_map/all_gather | solution.py:519
  982.1 12.7 %copy.72 = f32[1,384,8192]{2,1,0:T(8,128)} copy(f32[1,384,8192]{1,2,0:T(8,128)} %maximum_bitcast_fusion) | data formatting | bytes 25165824
  (331 shorter events, 245.2 us)
Async XLA Ops:
  7.2 96.9 %copy-start = (bf16[1,1024,1536]{2,1,0:T(8,128)(2,1)S(1)}, bf16[1,1024,1536]{2,1,0:T(8,128)(2,1)}, u32[]{:S(2)}) copy-start(bf16[1,1024,1536]{2,1,0:T(8,128)(2,1)} %param.16) | copy-start | bytes 9437188
  7.2 858.0 %all-gather.12.cloned.1.call-start = ((), (), s32[]{:S(2)}) async-start(), calls=%async_computation.4 | async-start | bytes 1474560 | tf_op jit(solution)/shard_map/all_gather | solution.py:520
  100.1 91.1 %collective-permute-start = (bf16[1536,896]{0,1:T(8,128)(2,1)}, bf16[1536,896]{0,1:T(8,128)(2,1)}, u32[]{:S(2)}, u32[]{:S(2)}) collective-permute-start(bf16[1536,896]{0,1:T(8,128)(2,1)} %bitcast.59), channel_id=1, source_target_pairs={{0,16},{16,0},{1,17},{17,1},{2,18},{18,2},{3,19},{19,3},{4,20},{20... | collective-permute-start | bytes 8257544 | tf_op jit(solution)/shard_map/ppermute | solution.py:444
  104.1 96.7 %collective-permute-start.1 = (bf16[96,1536]{1,0:T(8,128)(2,1)}, bf16[96,1536]{1,0:T(8,128)(2,1)}, u32[]{:S(2)}, u32[]{:S(2)}) collective-permute-start(bf16[96,1536]{1,0:T(8,128)(2,1)} %dynamic-slice_bitcast_fusion.1), channel_id=1, source_target_pairs={{0,16},{16,0},{1,17},{17,1},{2,18},{18,2},{3,19},{19,3},{4,20},{20... | collective-permute-start | bytes 884744 | tf_op jit(solution)/shard_map/ppermute | solution.py:444
  105.0 153.3 %collective-permute-start.2 = (bf16[256,1536]{1,0:T(8,128)(2,1)}, bf16[256,1536]{1,0:T(8,128)(2,1)}, u32[]{:S(2)}, u32[]{:S(2)}) collective-permute-start(bf16[256,1536]{1,0:T(8,128)(2,1)} %dynamic-slice_bitcast_fusion), channel_id=1, source_target_pairs={{0,16},{16,0},{1,17},{17,1},{2,18},{18,2},{3,19},{19,3},{4,20},{20... | collective-permute-start | bytes 2359304 | tf_op jit(solution)/shard_map/ppermute | solution.py:444
  107.2 50.8 %copy-start.70 = (bf16[1,384]{1,0:T(2,128)(2,1)S(1)}, bf16[1,384]{1,0:T(2,128)(2,1)}, u32[]{:S(2)}) copy-start(bf16[1,384]{1,0:T(2,128)(2,1)} %param.14) | copy-start | bytes 2308
  107.3 50.8 %copy-start.71 = (bf16[1,384]{1,0:T(2,128)(2,1)S(1)}, bf16[1,384]{1,0:T(2,128)(2,1)}, u32[]{:S(2)}) copy-start(bf16[1,384]{1,0:T(2,128)(2,1)} %param.11) | copy-start | bytes 2308
  191.2 123.2 %copy-start.14 = (f32[1024,64]{0,1:T(8,128)}, f32[1024,64]{0,1:T(8,128)S(1)}, u32[]{:S(2)}) copy-start(f32[1024,64]{0,1:T(8,128)S(1)} %get-tuple-element.115) | copy-start | bytes 786436
  191.2 123.2 %copy-start.17 = (f32[1024,64]{0,1:T(8,128)}, f32[1024,64]{0,1:T(8,128)S(1)}, u32[]{:S(2)}) copy-start(f32[1024,64]{0,1:T(8,128)S(1)} %get-tuple-element.116) | copy-start | bytes 786436
  191.2 123.2 %copy-start.20 = (f32[1024,64]{0,1:T(8,128)}, f32[1024,64]{0,1:T(8,128)S(1)}, u32[]{:S(2)}) copy-start(f32[1024,64]{0,1:T(8,128)S(1)} %get-tuple-element.117) | copy-start | bytes 786436
  230.4 55.6 %copy-start.11 = (f32[64,1536]{1,0:T(8,128)}, f32[64,1536]{1,0:T(8,128)S(1)}, u32[]{:S(2)}) copy-start(f32[64,1536]{1,0:T(8,128)S(1)} %get-tuple-element.71) | copy-start | bytes 1179652
  562.9 35.0 %collective-permute-start.7 = (bf16[256,1536]{1,0:T(8,128)(2,1)}, bf16[256,1536]{1,0:T(8,128)(2,1)}, u32[]{:S(2)}, u32[]{:S(2)}) collective-permute-start(bf16[256,1536]{1,0:T(8,128)(2,1)} %get-tuple-element.130), channel_id=1, source_target_pairs={{0,16},{16,0},{1,17},{17,1},{2,18},{18,2},{3,19},{19,3},{4,20},{20... | collective-permute-start | bytes 2359304 | tf_op jit(solution)/shard_map/ppermute | solution.py:444
  564.2 25.1 %collective-permute-start.6 = (bf16[96,1536]{1,0:T(8,128)(2,1)S(1)}, bf16[96,1536]{1,0:T(8,128)(2,1)S(1)}, u32[]{:S(2)}, u32[]{:S(2)}) collective-permute-start(bf16[96,1536]{1,0:T(8,128)(2,1)S(1)} %broadcast_select_fusion.10), channel_id=1, source_target_pairs={{0,16},{16,0},{1,17},{17,1},{2,18},{18,2},{3,19},{19,3},{4,20},{20... | collective-permute-start | bytes 884744 | tf_op jit(solution)/shard_map/ppermute | solution.py:444
  590.2 278.0 %all-gather.8.cloned.1.call-start = ((), (), s32[]{:S(2)}) async-start(), calls=%async_computation.2 | async-start | bytes 3932160 | tf_op jit(solution)/shard_map/all_gather | solution.py:521
  596.7 61.4 %collective-permute-start.5 = (bf16[1536,896]{0,1:T(8,128)(2,1)S(1)}, bf16[1536,896]{0,1:T(8,128)(2,1)}, u32[]{:S(2)}, u32[]{:S(2)}) collective-permute-start(bf16[1536,896]{0,1:T(8,128)(2,1)S(1)} %broadcast_select_fusion), channel_id=1, source_target_pairs={{0,16},{16,0},{1,17},{17,1},{2,18},{18,2},{3,19},{19,3},{4,20},{20... | collective-permute-start | bytes 8257544 | tf_op jit(solution)/shard_map/ppermute | solution.py:444
  600.2 314.6 %all-gather.10.cloned.1.call-start = ((), (), s32[]{:S(2)}) async-start(), calls=%async_computation.3 | async-start | bytes 13762560 | tf_op jit(solution)/shard_map/all_gather | solution.py:519
  704.4 46.1 %copy-start.66 = (f32[1536]{0:T(1024)S(1)}, f32[1536]{0:T(1024)}, u32[]{:S(2)}) copy-start(f32[1536]{0:T(1024)} %get-tuple-element.42) | copy-start | bytes 18436
  704.4 46.1 %copy-start.61 = (bf16[1024,128]{0,1:T(8,128)(2,1)S(1)}, bf16[1024,128]{0,1:T(8,128)(2,1)}, u32[]{:S(2)}) copy-start(bf16[1024,128]{0,1:T(8,128)(2,1)} %get-tuple-element.99) | copy-start | bytes 786436
  704.4 46.1 %copy-start.62 = (bf16[1024,128]{0,1:T(8,128)(2,1)S(1)}, bf16[1024,128]{0,1:T(8,128)(2,1)}, u32[]{:S(2)}) copy-start(bf16[1024,128]{0,1:T(8,128)(2,1)} %get-tuple-element.100) | copy-start | bytes 786436
  704.4 46.1 %copy-start.63 = (bf16[1024,128]{0,1:T(8,128)(2,1)S(1)}, bf16[1024,128]{0,1:T(8,128)(2,1)}, u32[]{:S(2)}) copy-start(bf16[1024,128]{0,1:T(8,128)(2,1)} %fusion.24) | copy-start | bytes 786436
  749.0 114.4 %collective-permute-start.3 = (bf16[64,1536]{1,0:T(8,128)(2,1)S(1)}, bf16[64,1536]{1,0:T(8,128)(2,1)S(1)}, u32[]{:S(2)}, u32[]{:S(2)}) collective-permute-start(bf16[64,1536]{1,0:T(8,128)(2,1)S(1)} %get-tuple-element.66), channel_id=1, source_target_pairs={{0,16},{16,0},{1,17},{17,1},{2,18},{18,2},{3,19},{19,3},{4,20},{20... | collective-permute-start | bytes 589832 | tf_op jit(solution)/shard_map/ppermute | solution.py:444
  753.6 52.3 %copy-start.29 = (f32[64,1536]{1,0:T(8,128)S(1)}, f32[64,1536]{1,0:T(8,128)}, u32[]{:S(2)}) copy-start(f32[64,1536]{1,0:T(8,128)} %get-tuple-element.61) | copy-start | bytes 1179652
  753.7 52.3 %copy-start.50 = (f32[64,1536]{1,0:T(8,128)S(1)}, f32[64,1536]{1,0:T(8,128)}, u32[]{:S(2)}) copy-start(f32[64,1536]{1,0:T(8,128)} %get-tuple-element.59) | copy-start | bytes 1179652
  806.1 58.0 %collective-permute-start.4 = (f32[64,1536]{1,0:T(8,128)S(1)}, f32[64,1536]{1,0:T(8,128)S(1)}, u32[]{:S(2)}, u32[]{:S(2)}) collective-permute-start(f32[64,1536]{1,0:T(8,128)S(1)} %get-tuple-element.54), channel_id=1, source_target_pairs={{0,16},{16,0},{1,17},{17,1},{2,18},{18,2},{3,19},{19,3},{4,20},{20... | collective-permute-start | bytes 1179656 | tf_op jit(solution)/shard_map/ppermute | solution.py:444
  (67 other events, 577.7 us)
Sparse Core Ops, SparseCore 0:
  590.3 29.2 all-gather.11
  621.8 62.6 all-gather.7
  702.2 212.4 all-gather.9

commit v2 on v1

v2 whole, which is shorter than its diff:
```python
import functools

import jax
import jax.numpy as jnp
from jax import lax
from jax.experimental import pallas as pl
from jax.experimental.pallas import tpu as pltpu
from jax.sharding import PartitionSpec as P

KV_HEADS = 8
HEAD = 96
LANES = 128
SPAN = 64
norm_eps = 1e-05
rope_base = 100000.0
masked_value = -1e30
BF = jnp.bfloat16
F32 = jnp.float32

MESH = pl.DeviceIdType.MESH


def greet():
    c = lax.axis_index("ctx")
    f = lax.axis_index("fsdp")
    barrier = pltpu.get_barrier_semaphore()
    inner = jnp.logical_and(c > 0, c < 3)
    for peer in (f + 2 - 4 * (f // 2), f + 1 - 2 * lax.rem(f, 2)):
        pl.semaphore_signal(barrier, inc=1, device_id={"fsdp": peer}, device_id_type=MESH)

    @pl.when(c < 3)
    def _():
        pl.semaphore_signal(barrier, inc=1, device_id={"ctx": c + 1}, device_id_type=MESH)

    @pl.when(c > 0)
    def _():
        pl.semaphore_signal(barrier, inc=1, device_id={"ctx": c - 1}, device_id_type=MESH)

    @pl.when(inner)
    def _():
        pl.semaphore_wait(barrier, 4)

    @pl.when(jnp.logical_not(inner))
    def _():
        pl.semaphore_wait(barrier, 3)


def near_order(c):
    low = c < 2
    return [c, c + 1 - 2 * lax.rem(c, 2), jnp.where(low, 2, 1), jnp.where(low, 3, 0)]


def gather_rows(whole, rows, send, recv, ready=None):
    c = lax.axis_index("ctx")
    f = lax.axis_index("fsdp")
    across = f + 2 - 4 * (f // 2)
    twin = f + 1 - 2 * lax.rem(f, 2)
    cross = across + 1 - 2 * lax.rem(f, 2)
    inner = jnp.logical_and(c > 0, c < 3)
    outer = jnp.logical_not(inner)
    order = near_order(c)
    pair = order[1]
    half = rows // 2
    sent = []

    def at(cc, ff, h):
        return whole.at[pl.ds(pl.multiple_of((cc * 4 + ff) * rows + h * half, half), half)]

    def copy(src, slot, arrival, peer):
        return pltpu.make_async_remote_copy(
            src, src, send.at[slot], recv.at[arrival], device_id=peer, device_id_type=MESH
        )

    def go(src, slot, arrival, peer, when=None):
        one = copy(src, slot, arrival, peer)
        if when is None:
            one.start()
        else:
            pl.when(when)(one.start)
        sent.append((one, when))

    def arrived(ref, arrival):
        copy(ref, 0, arrival, {"fsdp": twin}).wait_recv()

    up_to = {"ctx": jnp.minimum(c + 1, 3)}
    down_to = {"ctx": jnp.maximum(c - 1, 0)}
    for h in range(2):
        go(at(c, f, h), h, 2 * c + h, up_to, c < 3)
        go(at(c, f, h), 2 + h, 2 * c + h, down_to, c > 0)
        go(at(c, f, h), 4 + h, 8 + 2 * c + h, {"fsdp": across})
    for h in range(2):
        go(at(c, f, h), 12 + h, 16 + 2 * c + h, {"fsdp": twin})

    def along(step, h):
        d = order[step]
        block = at(d, f, h)
        arrived(block, 2 * d + h)
        go(block, 28 + 2 * step + h, 2 * d + h, {"ctx": jnp.where(d < c, jnp.minimum(c + 1, 3), jnp.maximum(c - 1, 0))}, inner)
        if (step, h) != (1, 0):
            go(block, 4 + 2 * step + h, 8 + 2 * d + h, {"fsdp": across})
        go(block, 12 + 2 * step + h, 16 + 2 * d + h, {"fsdp": twin})

    def over(step, h):
        d = order[step]
        block = at(d, across, h)
        arrived(block, 32 if (step, h) == (1, 0) else 8 + 2 * d + h)
        go(block, 20 + 2 * step + h, 24 + 2 * d + h, {"fsdp": twin})

    def complete(step):
        d = order[step]
        for h in range(2):
            arrived(at(d, twin, h), 16 + 2 * d + h)
            arrived(at(d, cross, h), 24 + 2 * d + h)
        if ready is not None:
            ready(d)

    along(1, 0)
    over(0, 0)
    go(at(c, across, 0), 36, 32, {"ctx": pair}, outer)
    along(1, 1)
    over(0, 1)
    along(2, 0)
    along(2, 1)
    complete(0)
    over(1, 1)
    along(3, 0)
    over(2, 0)
    along(3, 1)
    go(at(c, across, 0), 37, 32, {"ctx": pair}, inner)
    over(2, 1)
    complete(2)
    over(3, 0)
    over(1, 0)
    complete(1)
    over(3, 1)
    complete(3)
    for one, when in sent:
        if when is None:
            one.wait_send()
        else:
            pl.when(when)(one.wait_send)


GATHER_SENDS = 38
GATHER_RECVS = 33


def scatter_sum(part, total, land, send, recv, produce=None, meanwhile=None):
    c = lax.axis_index("ctx")
    f = lax.axis_index("fsdp")
    across = f + 2 - 4 * (f // 2)
    twin = f + 1 - 2 * lax.rem(f, 2)
    cross = across + 1 - 2 * lax.rem(f, 2)
    inner = jnp.logical_and(c > 0, c < 3)
    rows = total.shape[0]
    half = rows // 2
    order = near_order(c)[::-1]
    pair = order[2]
    sent = []

    def rows_at(cc, ff, h=None):
        start = (cc * 4 + ff) * rows
        if h is None:
            return pl.ds(pl.multiple_of(start, rows), rows)
        return pl.ds(pl.multiple_of(start + h * half, half), half)

    def copy(src, dst, slot, arrival, peer):
        return pltpu.make_async_remote_copy(
            src, dst, send.at[slot], recv.at[arrival], device_id=peer, device_id_type=MESH
        )

    def go(src, dst, slot, arrival, peer):
        one = copy(src, dst, slot, arrival, peer)
        one.start()
        sent.append(one)

    def piece(slot, h):
        return land.at[slot, pl.ds(h * half, half)]

    def landed(ref, arrival):
        copy(ref, ref, 0, arrival, {"fsdp": twin}).wait_recv()
        return ref[...].astype(F32)

    def begin(step):
        d = order[step]
        if produce is not None:
            produce(d)
        go(part.at[rows_at(d, cross)], land.at[step], step, step, {"fsdp": twin})
        go(part.at[rows_at(d, twin)], land.at[4 + step], 4 + step, 4 + step, {"fsdp": twin})

    def over(step, h):
        d = order[step]
        mine = rows_at(d, across, h)
        if h == 0:
            copy(land.at[step], land.at[step], 0, step, {"fsdp": twin}).wait_recv()
        value = part[mine, :].astype(F32) + land[step, h * half : (h + 1) * half, :].astype(F32)
        if (step, h) == (3, 0):
            value = value + landed(piece(17, 0), 26)
        part[mine, :] = value.astype(BF)
        if (step, h) == (2, 0):
            go(part.at[mine], piece(17, 0), 16, 26, {"ctx": pair})
        else:
            go(part.at[mine], piece(8 + step, h), 8 + 2 * step + h, 8 + 2 * step + h, {"fsdp": across})

    def onward(step, h):
        d = order[step]
        mine = rows_at(d, f, h)
        if h == 0:
            copy(land.at[4 + step], land.at[4 + step], 0, 4 + step, {"fsdp": twin}).wait_recv()
        value = part[mine, :].astype(F32) + land[4 + step, h * half : (h + 1) * half, :].astype(F32)
        if (step, h) != (2, 0):
            value = value + landed(piece(8 + step, h), 8 + 2 * step + h)
        if step == 3:
            total[h * half : (h + 1) * half, :] = value
            return
        part[mine, :] = value.astype(BF)

        @pl.when(inner)
        def _():
            part[mine, :] = (part[mine, :].astype(F32) + landed(piece(12 + d, h), 16 + 2 * d + h)).astype(BF)

        target = jnp.where(d > c, c + 1, c - 1)
        here = jnp.logical_and(d < c, d == c - 1)
        go(part.at[mine], piece(jnp.where(here, 16, 12 + d), h), 17 + 2 * step + h,
           jnp.where(here, 24, 16 + 2 * d) + h, {"ctx": target})

    begin(0)
    over(0, 0)
    over(0, 1)
    begin(1)
    begin(2)
    over(2, 0)
    over(1, 0)
    onward(0, 0)
    over(1, 1)
    onward(0, 1)
    begin(3)
    over(2, 1)
    onward(1, 0)
    over(3, 0)
    onward(1, 1)
    over(3, 1)
    onward(2, 0)
    onward(2, 1)
    if meanwhile is not None:
        meanwhile()
    for h in range(2):
        onward(3, h)

        @pl.when(c > 0)
        def _():
            total[h * half : (h + 1) * half, :] += landed(piece(12 + c, h), 16 + 2 * c + h)

        @pl.when(c < 3)
        def _():
            total[h * half : (h + 1) * half, :] += landed(piece(16, h), 24 + h)

    for one in sent:
        one.wait_send()


SCATTER_SENDS = 23
SCATTER_RECVS = 27


def kernel_dot(left, right):
    return jnp.dot(left, right, preferred_element_type=F32)


def kernel_dot_nt(left, right):
    return lax.dot_general(left, right, (((1,), (1,)), ((), ())), preferred_element_type=F32)


def kernel_dot_tn(left, right):
    return lax.dot_general(left, right, (((0,), (0,)), ((), ())), preferred_element_type=F32)


def turn(values):
    return pltpu.roll(values, SPAN, axis=1)


def mean_square(values):
    return lax.rsqrt(jnp.mean(values * values, axis=-1, keepdims=True) + norm_eps)


class Loads:
    def __init__(self, sems):
        self.sems = sems
        self.copies = []

    def start(self, src, dst):
        one = pltpu.make_async_copy(src, dst, self.sems.at[len(self.copies)])
        one.start()
        self.copies.append(one)
        return one


def plane_rows(d, rows):
    return pl.ds(pl.multiple_of(d * 4 * rows, 4 * rows), 4 * rows)


def forward_kernel(layer, x_own, w_mix, w_gate, w_out, w_down, w_gains, cosine, sine, place_col, place_row,
                   normed_o, q_o, k_o, v_o, context_o, log_o, middle_o, normed_two_o, both_o, result_o,
                   x_v, normed_v, q_v, k_v, v_v, context_v, log_v, middle_v, two_v, both_v, hidden_v, result_v,
                   mix_v, gate_v, out_v, down_v, gains_v, part_v, land_a, land_b, total_v, local, save,
                   send_a, recv_a, send_b, recv_b, send_c, recv_c, send_d, recv_d):
    c = lax.axis_index("ctx")
    f = lax.axis_index("fsdp")
    rows = x_own.shape[0]
    units = down_v.shape[0]
    own_rows = pl.ds(pl.multiple_of((c * 4 + f) * rows, rows), rows)
    loads = Loads(local)
    saves = Loads(save)
    load_x = loads.start(x_own, x_v.at[own_rows])
    load_gains = loads.start(w_gains.at[layer], gains_v)
    load_mix = loads.start(w_mix.at[layer], mix_v)
    out_v[...] = jnp.zeros_like(out_v)
    greet()
    load_x.wait()
    load_gains.wait()
    load_mix.wait()
    load_out = loads.start(w_out.at[layer], out_v.at[pl.ds(0, HEAD)])
    load_gate = loads.start(w_gate.at[layer], gate_v)
    load_down = loads.start(w_down.at[layer], down_v)

    def project(d):
        here = plane_rows(d, rows)
        x = x_v[here, :].astype(F32)
        normed = (x * mean_square(x) * gains_v[0:1, :].astype(F32)).astype(BF)
        normed_v[here, :] = normed
        mixed = kernel_dot(normed, mix_v[...])
        cos = cosine[here, :]
        sin = sine[here, :]
        q = mixed[:, :LANES]
        k = mixed[:, LANES : 2 * LANES]
        q_v[here, :] = (q * cos + turn(q) * sin).astype(BF)
        k_v[here, :] = (k * cos + turn(k) * sin).astype(BF)
        v_v[here, :] = mixed[:, 2 * LANES :].astype(BF)

    gather_rows(x_v, rows, send_a, recv_a, project)
    for src, dst in ((normed_v, normed_o), (q_v, q_o), (k_v, k_o), (v_v, v_o)):
        saves.start(src, dst)
    load_out.wait()
    scale = HEAD ** (-0.5)

    def attention(d):
        here = plane_rows(d, rows)
        scores = kernel_dot_nt(q_v[here, :], k_v[...]) * scale
        allowed = place_row[...] <= place_col[here, :]
        scores = jnp.where(allowed, scores, masked_value)
        top = jnp.max(scores, axis=-1, keepdims=True)
        weights = jnp.exp(scores - top)
        amount = jnp.sum(weights, axis=-1, keepdims=True)
        context = (kernel_dot(weights.astype(BF), v_v[...]) / amount).astype(BF)
        context_v[here, :] = context
        log_v[here, :] = jnp.broadcast_to(top + jnp.log(amount), (4 * rows, LANES))
        part_v[here, :] = kernel_dot(context, out_v[...]).astype(BF)

    scatter_sum(part_v, total_v, land_a, send_b, recv_b, attention)
    saves.start(context_v, context_o)
    saves.start(log_v, log_o)
    middle = x_v[own_rows, :].astype(F32) + total_v[...]
    middle_v[...] = middle
    saves.start(middle_v, middle_o)
    two_v[own_rows, :] = (middle * mean_square(middle) * gains_v[1:2, :].astype(F32)).astype(BF)
    load_gate.wait()

    def feed(d):
        here = plane_rows(d, rows)
        both = kernel_dot(two_v[here, :], gate_v[...])
        both_v[here, :] = both
        gate = both[:, :units]
        hidden_v[here, :] = (gate * jax.nn.sigmoid(gate) * both[:, units:]).astype(BF)

    gather_rows(two_v, rows, send_c, recv_c, feed)
    saves.start(two_v, normed_two_o)
    saves.start(both_v, both_o)
    load_down.wait()

    def lower(d):
        here = plane_rows(d, rows)
        part_v[here, :] = kernel_dot(hidden_v[here, :], down_v[...]).astype(BF)

    scatter_sum(part_v, total_v, land_b, send_d, recv_d, lower)
    result_v[...] = (middle_v[...] + total_v[...]).astype(BF)
    saves.start(result_v, result_o)
    for one in saves.copies:
        one.wait()


def backward_kernel(layer, grad_own, w_mix, w_gate, w_out, w_down, w_gains, cosine, sine, place_col, place_row,
                    x_own, normed, q, k, v, context, log, middle, normed_two, both,
                    start_o, low_o, mix_grad_o, gate_grad_o, out_grad_o, down_grad_o, gain_grad_o,
                    grad_v, x_v, normed_v, q_v, k_v, v_v, context_v, log_v, middle_v, two_v, both_v, both_grad_v, hidden_v,
                    low_v, mixed_v, key_grad_v, value_grad_v, start_v, start_low_v,
                    mix_grad_v, gate_grad_v, out_grad_v, down_grad_v, gain_grad_v,
                    mix_v, gate_v, out_v, down_v, gains_v, part_v, land_a, land_b, total_v, local, save,
                    send_a, recv_a, send_b, recv_b, send_c, recv_c, send_d, recv_d):
    c = lax.axis_index("ctx")
    f = lax.axis_index("fsdp")
    rows = grad_own.shape[0]
    length, width = grad_v.shape
    units = down_v.shape[0]
    own_rows = pl.ds(pl.multiple_of((c * 4 + f) * rows, rows), rows)
    loads = Loads(local)
    saves = Loads(save)
    load_grad = loads.start(grad_own, grad_v.at[own_rows])
    load_down = loads.start(w_down.at[layer], down_v)
    load_both = loads.start(both, both_v)
    load_gate = loads.start(w_gate.at[layer], gate_v)
    out_v[...] = jnp.zeros_like(out_v)
    key_grad_v[...] = jnp.zeros_like(key_grad_v)
    value_grad_v[...] = jnp.zeros_like(value_grad_v)
    greet()
    load_grad.wait()
    later = [
        loads.start(src, dst)
        for src, dst in (
            (normed_two, two_v), (middle, middle_v), (w_gains.at[layer], gains_v),
            (w_out.at[layer], out_v.at[pl.ds(0, HEAD)]), (q, q_v), (k, k_v), (v, v_v),
            (context, context_v), (log, log_v), (w_mix.at[layer], mix_v), (normed, normed_v), (x_own, x_v),
        )
    ]
    load_down.wait()
    load_both.wait()

    def feed(d):
        here = plane_rows(d, rows)
        hidden_grad = kernel_dot_nt(grad_v[here, :], down_v[...])
        gate = both_v[here, :units]
        up = both_v[here, units:]
        sig = jax.nn.sigmoid(gate)
        silu = gate * sig
        hidden_v[here, :] = (silu * up).astype(BF)
        both_grad_v[here, :units] = (hidden_grad * up * sig * (1.0 + gate * (1.0 - sig))).astype(BF)
        both_grad_v[here, units:] = (hidden_grad * silu).astype(BF)

    gather_rows(grad_v, rows, send_a, recv_a, feed)
    load_gate.wait()

    def spread(d):
        here = plane_rows(d, rows)
        part_v[here, :] = kernel_dot_nt(both_grad_v[here, :], gate_v[...]).astype(BF)

    def feed_weights():
        later[0].wait()
        down_grad_v[...] = kernel_dot_tn(hidden_v[...], grad_v[...]).astype(BF)
        for part in range(2):
            gate_grad_v[part] = kernel_dot_tn(
                two_v[...], both_grad_v[:, part * units : (part + 1) * units]
            ).astype(BF)
        saves.start(down_grad_v, down_grad_o)
        saves.start(gate_grad_v, gate_grad_o)

    scatter_sum(part_v, total_v, land_a, send_b, recv_b, spread, feed_weights)
    for one in later[1:]:
        one.wait()

    def norm_grads(error, value, gain, row):
        factor = mean_square(value)
        shaped = error * gain
        common = jnp.mean(shaped * value, axis=-1, keepdims=True)
        gain_grad_v[row : row + 1, :] = jnp.sum(error * value * factor, axis=0, keepdims=True)
        return factor * shaped - value * (factor * factor * factor) * common

    gain_grad_v[...] = jnp.zeros_like(gain_grad_v)
    middle_grad = norm_grads(total_v[...], middle_v[...], gains_v[1:2, :].astype(F32), 1)
    middle_grad = middle_grad + grad_v[own_rows, :].astype(F32)
    middle_v[...] = middle_grad
    low_v[own_rows, :] = middle_grad.astype(BF)
    scale = HEAD ** (-0.5)

    def attention(d):
        here = plane_rows(d, rows)
        context_grad = kernel_dot_nt(low_v[here, :], out_v[...])
        common = jnp.sum(context_grad * context_v[here, :].astype(F32), axis=-1, keepdims=True)
        context_grad = context_grad.astype(BF)
        queries = q_v[here, :]
        scores = kernel_dot_nt(queries, k_v[...]) * scale
        allowed = place_row[...] <= place_col[here, :]
        weights = jnp.exp(jnp.where(allowed, scores, masked_value) - log_v[here, 0:1])
        weight_grad = kernel_dot_nt(context_grad, v_v[...])
        score_grad = (weights * (weight_grad - common)).astype(BF)
        value_grad_v[...] += kernel_dot_tn(weights.astype(BF), context_grad)
        key_grad_v[...] += kernel_dot_tn(score_grad, queries)
        query_grad = kernel_dot(score_grad, k_v[...]) * scale
        mixed_v[here, :LANES] = (query_grad * cosine[here, :] - turn(query_grad) * sine[here, :]).astype(BF)

    gather_rows(low_v, rows, send_c, recv_c, attention)
    key_grad = key_grad_v[...] * scale
    mixed_v[:, LANES : 2 * LANES] = (key_grad * cosine[...] - turn(key_grad) * sine[...]).astype(BF)
    mixed_v[:, 2 * LANES :] = value_grad_v[...].astype(BF)

    def spread_two(d):
        here = plane_rows(d, rows)
        part_v[here, :] = kernel_dot_nt(mixed_v[here, :], mix_v[...]).astype(BF)

    def mix_weights():
        out_grad_v[...] = kernel_dot_tn(context_v[...], low_v[...])[:HEAD].astype(BF)
        for part in range(3):
            mix_grad_v[part] = kernel_dot_tn(
                normed_v[...], mixed_v[:, part * LANES : (part + 1) * LANES]
            ).astype(BF)
        saves.start(out_grad_v, out_grad_o)
        saves.start(mix_grad_v, mix_grad_o)

    scatter_sum(part_v, total_v, land_b, send_d, recv_d, spread_two, mix_weights)
    start_grad = norm_grads(total_v[...], x_v[...].astype(F32), gains_v[0:1, :].astype(F32), 0) + middle_v[...]
    start_v[...] = start_grad
    start_low_v[...] = start_grad.astype(BF)
    saves.start(start_v, start_o)
    saves.start(start_low_v, low_o)
    saves.start(gain_grad_v, gain_grad_o)
    for one in saves.copies:
        one.wait()


def link_sems():
    dma = pltpu.SemaphoreType.DMA
    return [dma((GATHER_SENDS,)), dma((GATHER_RECVS,)), dma((SCATTER_SENDS,)), dma((SCATTER_RECVS,))] * 2


def forward_call(layer, x_own, shared, tables, places):
    rows, width = x_own.shape
    length = 16 * rows
    units = shared[3].shape[1]
    anywhere = pl.BlockSpec(memory_space=pl.ANY)
    inside = pl.BlockSpec(memory_space=pltpu.VMEM)

    def low(*shape):
        return (shape, BF)

    def full(*shape):
        return (shape, F32)

    kept = [low(length, width)] + [low(length, LANES)] * 4 + [
        full(length, LANES), full(rows, width), low(length, width), full(length, 2 * units), low(rows, width)]
    inner = [low(length, width), low(length, width)] + [low(length, LANES)] * 4 + [
        full(length, LANES), full(rows, width), low(length, width), full(length, 2 * units), low(length, units),
        low(rows, width), low(width, 3 * LANES), low(width, 2 * units), low(LANES, width), low(units, width),
        low(16, width), low(length, width), low(18, rows, width), low(18, rows, width), full(rows, width)]
    return pl.pallas_call(
        functools.partial(forward_kernel, layer),
        out_shape=[jax.ShapeDtypeStruct(*one) for one in kept],
        in_specs=[anywhere] * 6 + [inside] * 4,
        out_specs=[anywhere] * len(kept),
        scratch_shapes=[pltpu.VMEM(*one) for one in inner]
        + [pltpu.SemaphoreType.DMA((6,)), pltpu.SemaphoreType.DMA((10,))] + link_sems(),
        compiler_params=pltpu.CompilerParams(
            collective_id=4 + layer, has_side_effects=True, vmem_limit_bytes=60 << 20),
    )(x_own, *shared, *tables, *places)


def backward_call(layer, grad_own, shared, tables, places, x_own, kept):
    rows, width = grad_own.shape
    length = 16 * rows
    units = shared[3].shape[1]
    anywhere = pl.BlockSpec(memory_space=pl.ANY)
    inside = pl.BlockSpec(memory_space=pltpu.VMEM)

    def low(*shape):
        return (shape, BF)

    def full(*shape):
        return (shape, F32)

    grads = [low(3, width, LANES), low(2, width, units), low(HEAD, width), low(units, width), full(2, width)]
    outs = [full(rows, width), low(rows, width)] + grads
    inner = [low(length, width), low(rows, width), low(length, width)] + [low(length, LANES)] * 4 + [
        full(length, LANES), full(rows, width), low(length, width), full(length, 2 * units), low(length, 2 * units),
        low(length, units), low(length, width), low(length, 3 * LANES), full(length, LANES), full(length, LANES),
        full(rows, width), low(rows, width)] + grads + [
        low(width, 3 * LANES), low(width, 2 * units), low(LANES, width), low(units, width),
        low(16, width), low(length, width), low(18, rows, width), low(18, rows, width), full(rows, width)]
    return pl.pallas_call(
        functools.partial(backward_kernel, layer),
        out_shape=[jax.ShapeDtypeStruct(*one) for one in outs],
        in_specs=[anywhere] * 6 + [inside] * 4 + [anywhere] * 10,
        out_specs=[anywhere] * len(outs),
        scratch_shapes=[pltpu.VMEM(*one) for one in inner]
        + [pltpu.SemaphoreType.DMA((16,)), pltpu.SemaphoreType.DMA((7,))] + link_sems(),
        compiler_params=pltpu.CompilerParams(
            collective_id=6 + layer, has_side_effects=True, vmem_limit_bytes=60 << 20),
    )(grad_own, *shared, *tables, *places, x_own, *kept)


def greet_all(peers):
    barrier = pltpu.get_barrier_semaphore()
    for peer in peers:
        pl.semaphore_signal(barrier, inc=1, device_id=peer, device_id_type=MESH)
    pl.semaphore_wait(barrier, len(peers))


def head_choice(value_part):
    source = lax.broadcasted_iota(jnp.int32, (4 * HEAD, 4 * LANES), 0)
    lane = lax.broadcasted_iota(jnp.int32, (4 * HEAD, 4 * LANES), 1)
    head = lane // LANES
    inside = lane - head * LANES
    if value_part:
        wanted = jnp.where(inside < HEAD, head * HEAD + inside, -1)
    else:
        half = inside // SPAN
        place = inside - half * SPAN
        wanted = jnp.where(place < HEAD // 2, head * HEAD + half * (HEAD // 2) + place, -1)
    return jnp.where(source == wanted, 1.0, 0.0).astype(BF)


def share_kernel(mix, out, gate_up, down, gains, w_mix, w_gate, w_out, w_down, w_gains,
                 mix_v, heads_v, local, send, recv):
    s = lax.axis_index("section")
    c = lax.axis_index("ctx")
    f = lax.axis_index("fsdp")
    depth = mix.shape[1]
    units = w_down.shape[1]
    hidden_units = gate_up.shape[2] // 2
    other = 1 - s
    peers = [lax.rem(f + k, 4) for k in range(1, 4)]
    greet_all([{"fsdp": peer} for peer in peers] + [{"section": other}]
              + [{"section": other, "fsdp": peer} for peer in peers])
    load = pltpu.make_async_copy(mix.at[0], mix_v, local.at[0])
    load.start()
    rows = pl.ds(pl.multiple_of(f * depth, depth), depth)
    pending = []

    def copy(src, dst, slot, arrival, peer):
        return pltpu.make_async_remote_copy(
            src, dst, send.at[slot], recv.at[arrival], device_id=peer, device_id_type=MESH
        )

    def go(src, dst, slot, arrival, peer):
        one = copy(src, dst, slot, arrival, peer)
        one.start()
        pending.append(one)

    mine = w_gains.at[s, :, pl.ds(pl.multiple_of(f * depth, depth), depth)]
    for k, peer in enumerate(peers):
        go(gains, mine, 20 + k, 16 + 4 * s + f, {"fsdp": peer})
        go(gains, mine, 23 + k, 16 + 4 * s + f, {"section": other, "fsdp": peer})
    go(gains, mine, 26, 16 + 4 * s + f, {"section": other})
    keep_gains = pltpu.make_async_copy(gains, mine, local.at[1])
    keep_gains.start()

    load.wait()
    for g in range(8):
        choice = head_choice(g >= 6)
        heads_v[:, g * 512 : (g + 1) * 512] = jnp.dot(
            mix_v[:, g * 384 : (g + 1) * 384], choice, preferred_element_type=F32
        ).astype(BF)

    def lanes(peer, part):
        head = peer * 4 + c
        start = head * LANES if part == 0 else (16 + 8 * (part - 1) + head // 2) * LANES
        return heads_v.at[:, pl.ds(pl.multiple_of(start, LANES), LANES)]

    def put(peer, part):
        return w_mix.at[s, rows, pl.ds(part * LANES, LANES)]

    for k, peer in enumerate(peers):
        for part in range(3):
            copy(lanes(peer, part), put(peer, part), k, f, {"fsdp": peer}).start()
    own_mix = [pltpu.make_async_copy(lanes(f, part), put(f, part), local.at[2 + part]) for part in range(3)]
    for one in own_mix:
        one.start()

    def gate_piece(peer, part):
        start = pl.multiple_of(part * hidden_units + (peer * 4 + c) * units, units)
        return gate_up.at[0, :, pl.ds(start, units)]

    def gate_put(part):
        return w_gate.at[s, rows, pl.ds(part * units, units)]

    for k, peer in enumerate(peers):
        for part in range(2):
            copy(gate_piece(peer, part), gate_put(part), 3 + k, 4 + f, {"fsdp": peer}).start()
    own_gate = [pltpu.make_async_copy(gate_piece(f, part), gate_put(part), local.at[5 + part]) for part in range(2)]
    for one in own_gate:
        one.start()
    out_rows = out.at[0, pl.ds(pl.multiple_of(c * HEAD, HEAD), HEAD)]
    down_rows = down.at[0, pl.ds(pl.multiple_of(c * units, units), units)]
    own_out = pltpu.make_async_copy(out_rows, w_out.at[s], local.at[7])
    own_out.start()
    own_down = pltpu.make_async_copy(down_rows, w_down.at[s], local.at[8])
    own_down.start()

    def slab(ref, origin):
        return ref.at[s, pl.ds(pl.multiple_of(origin * depth, depth), depth)]

    for one in own_mix:
        one.wait()
    go(slab(w_mix, f), slab(w_mix, f), 6, 8 + f, {"section": other})
    for k in range(3):
        origin = lax.rem(f + 3 - k, 4)
        copy(slab(w_mix, origin), slab(w_mix, origin), 0, origin, {"fsdp": origin}).wait_recv()
        go(slab(w_mix, origin), slab(w_mix, origin), 7 + k, 8 + origin, {"section": other})
    go(out_rows, w_out.at[s], 10, 24, {"section": other})
    for one in own_gate:
        one.wait()
    go(slab(w_gate, f), slab(w_gate, f), 11, 12 + f, {"section": other})
    for k in range(3):
        origin = lax.rem(f + 3 - k, 4)
        copy(slab(w_gate, origin), slab(w_gate, origin), 0, 4 + origin, {"fsdp": origin}).wait_recv()
        go(slab(w_gate, origin), slab(w_gate, origin), 12 + k, 12 + origin, {"section": other})
    go(down_rows, w_down.at[s], 15, 25, {"section": other})

    def from_there(ref, arrival):
        copy(ref, ref, 0, arrival, {"section": other}).wait_recv()

    for origin in range(4):
        theirs = pl.ds(origin * depth, depth)
        from_there(w_mix.at[other, theirs], 8 + origin)
        from_there(w_gate.at[other, theirs], 12 + origin)
    from_there(w_out.at[other], 24)
    from_there(w_down.at[other], 25)
    for origin in range(4):
        from_there(w_gains.at[other, :, pl.ds(origin * depth, depth)], 16 + 4 * other + origin)
    for k in range(3):
        origin = lax.rem(f + 3 - k, 4)
        from_there(w_gains.at[s, :, pl.ds(pl.multiple_of(origin * depth, depth), depth)], 16 + 4 * s + origin)
    keep_gains.wait()
    own_out.wait()
    own_down.wait()
    for k, peer in enumerate(peers):
        copy(slab(w_mix, f), slab(w_mix, f), k, 0, {"fsdp": peer}).wait_send()
        copy(slab(w_gate, f), slab(w_gate, f), 3 + k, 0, {"fsdp": peer}).wait_send()
    for one in pending:
        one.wait_send()


def share_call(mix, out, gate_up, down, gains):
    depth = mix.shape[1]
    width = 4 * depth
    units = gate_up.shape[2] // 32
    anywhere = pl.BlockSpec(memory_space=pl.ANY)
    return pl.pallas_call(
        share_kernel,
        out_shape=(
            jax.ShapeDtypeStruct((2, width, 3 * LANES), BF),
            jax.ShapeDtypeStruct((2, width, 2 * units), BF),
            jax.ShapeDtypeStruct((2, HEAD, width), BF),
            jax.ShapeDtypeStruct((2, units, width), BF),
            jax.ShapeDtypeStruct((2, 16, width), BF),
        ),
        in_specs=[anywhere] * 5,
        out_specs=(anywhere,) * 5,
        scratch_shapes=[
            pltpu.VMEM((depth, mix.shape[2]), BF),
            pltpu.VMEM((depth, 32 * LANES), BF),
            pltpu.SemaphoreType.DMA((9,)),
            pltpu.SemaphoreType.DMA((27,)),
            pltpu.SemaphoreType.DMA((26,)),
        ],
        compiler_params=pltpu.CompilerParams(collective_id=2, has_side_effects=True, vmem_limit_bytes=48 << 20),
    )(mix, out, gate_up, down, gains)


def return_kernel(mix_0, mix_1, gate_0, gate_1, out_0, out_1, down_0, down_1, gains,
                  mix_out, gate_out, out_out, down_out, gain_out,
                  mix_v, gate_v, out_v, down_v, mix_x, gate_x, out_x, down_x, gain_v, gain_x,
                  local, send, recv, line_send, line_recv):
    s = lax.axis_index("section")
    c = lax.axis_index("ctx")
    f = lax.axis_index("fsdp")
    other = 1 - s
    units = down_0.shape[0]
    depth = mix_out.shape[1]
    inner = jnp.logical_and(c > 0, c < 3)
    peers = [lax.rem(f + k, 4) for k in range(1, 4)]
    pair = c + 1 - 2 * lax.rem(c, 2)
    far = lax.rem(c + 2, 4)
    barrier = pltpu.get_barrier_semaphore()
    for peer in [{"fsdp": peer} for peer in peers] + [{"section": other}, {"ctx": pair}, {"ctx": far}]:
        pl.semaphore_signal(barrier, inc=1, device_id=peer, device_id_type=MESH)

    @pl.when(inner)
    def _():
        pl.semaphore_signal(barrier, inc=1, device_id={"ctx": 3 - c}, device_id_type=MESH)
        pl.semaphore_wait(barrier, 7)

    @pl.when(jnp.logical_not(inner))
    def _():
        pl.semaphore_wait(barrier, 6)

    def copy(src, dst, slot, arrival, peer):
        return pltpu.make_async_remote_copy(
            src, dst, send.at[slot], recv.at[arrival], device_id=peer, device_id_type=MESH
        )

    def rows_of(k):
        return pl.ds(k * depth, depth)

    def away(mix, gate, out, down):
        copy(down, down_x, 8, 8, {"section": other}).start()
        for k in range(4):
            copy(gate.at[:, rows_of(k)], gate_x.at[:, rows_of(k)], k, k, {"section": other}).start()
        copy(out, out_x, 9, 9, {"section": other}).start()
        for k in range(4):
            copy(mix.at[:, rows_of(k)], mix_x.at[:, rows_of(k)], 4 + k, 4 + k, {"section": other}).start()

    def home(mix, gate, out, down):
        for k, (src, dst) in enumerate(((down, down_v), (gate, gate_v), (out, out_v), (mix, mix_v))):
            pltpu.make_async_copy(src, dst, local.at[k]).start()

    @pl.when(s == 0)
    def _():
        away(mix_1, gate_1, out_1, down_1)
        home(mix_0, gate_0, out_0, down_0)

    @pl.when(s == 1)
    def _():
        away(mix_0, gate_0, out_0, down_0)
        home(mix_1, gate_1, out_1, down_1)

    def home_wait(k, dst):
        pltpu.make_async_copy(dst, dst, local.at[k]).wait()

    def arrived(ref, arrival):
        copy(ref, ref, 0, arrival, {"section": other}).wait_recv()

    def gate_at(cc, ff):
        return gate_out.at[:, :, pl.ds(pl.multiple_of((ff * 4 + cc) * units, units), units)]

    def mix_at(cc, ff):
        return mix_out.at[:, :, pl.ds(pl.multiple_of((ff * 4 + cc) * LANES, LANES), LANES)]

    def out_at(cc, ff):
        return out_out.at[pl.ds(pl.multiple_of(cc * HEAD, HEAD), HEAD)]

    def down_at(cc, ff):
        return down_out.at[pl.ds(pl.multiple_of(cc * units, units), units)]

    items = [(down_at, f)] + [(gate_at, lax.rem(f + k, 4)) for k in (0, 3, 2, 1)] + [(out_at, f)] + [
        (mix_at, lax.rem(f + k, 4)) for k in (0, 3, 2, 1)
    ]

    def line(place, origin, index, cc, slot, target):
        key = cc * 10 + index
        return pltpu.make_async_remote_copy(
            place(cc, origin), place(cc, origin), line_send.at[slot], line_recv.at[key],
            device_id={"ctx": target}, device_id_type=MESH,
        )

    above = jnp.minimum(c + 1, 3)
    below = jnp.maximum(c - 1, 0)

    def start_line(index):
        place, origin = items[index]
        pl.when(c < 3)(line(place, origin, index, c, index, above).start)
        pl.when(c > 0)(line(place, origin, index, c, 10 + index, below).start)

    def fold(mine, theirs, arrival):
        arrived(theirs, arrival)
        mine[...] = (mine[...].astype(F32) + theirs[...].astype(F32)).astype(BF)

    def keep(src, dst, k):
        one = pltpu.make_async_copy(src, dst, local.at[k])
        one.start()
        one.wait()

    home_wait(0, down_v)
    fold(down_v, down_x, 8)
    keep(down_v, down_at(c, f), 4)
    start_line(0)

    def to_owners(mine, theirs, place, arrival_x, arrival_y, slot):
        for k in (1, 2, 3, 0):
            owner = lax.rem(f + k, 4)
            rows = pl.ds(pl.multiple_of(owner * depth, depth), depth)
            fold(mine.at[:, rows], theirs.at[:, rows], arrival_x + owner)
            if k:
                copy(mine.at[:, rows], place(c, f), slot + k, arrival_y + f, {"fsdp": owner}).start()
            else:
                keep(mine.at[:, rows], place(c, f), 4)

    home_wait(1, gate_v)
    to_owners(gate_v, gate_x, gate_at, 0, 10, 10)
    start_line(1)
    home_wait(2, out_v)
    fold(out_v, out_x, 9)
    keep(out_v, out_at(c, f), 4)
    start_line(5)
    for k in range(3):
        origin = items[2 + k][1]
        arrived(gate_at(c, origin), 10 + origin)
        start_line(2 + k)
    home_wait(3, mix_v)
    to_owners(mix_v, mix_x, mix_at, 4, 14, 14)
    start_line(6)
    for k in range(3):
        origin = items[7 + k][1]
        arrived(mix_at(c, origin), 14 + origin)
        start_line(7 + k)

    gain_v[0] = gains[...]
    twin = f + 1 - 2 * lax.rem(f, 2)
    across = f + 2 - 4 * (f // 2)
    targets = [{"section": other}, {"fsdp": twin}, {"fsdp": across}, {"ctx": pair}, {"ctx": far}]
    gain_copies = []
    for k, target in enumerate(targets):
        one = copy(gain_v.at[k], gain_x.at[k], 18 + k, 18 + k, target)
        one.start()
        one.wait_recv()
        gain_copies.append(one)
        if k < 4:
            gain_v[k + 1] = gain_v[k] + gain_x[k]
        else:
            gain_out[...] = gain_v[k] + gain_x[k]

    order = near_order(c)
    forwards = []
    for step in range(1, 4):
        d = order[step]
        onward = jnp.where(d < c, above, below)
        for index, (place, origin) in enumerate(items):
            one = line(place, origin, index, d, 20 + (step - 1) * 10 + index, onward)
            one.wait_recv()
            pl.when(inner)(one.start)
            forwards.append(one)
    for index, (place, origin) in enumerate(items):
        pl.when(c < 3)(line(place, origin, index, c, index, above).wait_send)
        pl.when(c > 0)(line(place, origin, index, c, 10 + index, below).wait_send)
    for one in forwards:
        pl.when(inner)(one.wait_send)
    for one in gain_copies:
        one.wait_send()
    for k in range(4):
        copy(gate_x.at[:, rows_of(k)], gate_x.at[:, rows_of(k)], k, 0, {"section": other}).wait_send()
        copy(mix_x.at[:, rows_of(k)], mix_x.at[:, rows_of(k)], 4 + k, 0, {"section": other}).wait_send()
        if k:
            copy(gate_x.at[:, rows_of(k)], gate_x.at[:, rows_of(k)], 10 + k, 0, {"section": other}).wait_send()
            copy(mix_x.at[:, rows_of(k)], mix_x.at[:, rows_of(k)], 14 + k, 0, {"section": other}).wait_send()
    copy(down_x, down_x, 8, 0, {"section": other}).wait_send()
    copy(out_x, out_x, 9, 0, {"section": other}).wait_send()


def return_call(first, second, gains):
    mix, gate, out, down = first
    units, width = down.shape
    depth = width // 4
    anywhere = pl.BlockSpec(memory_space=pl.ANY)
    inside = pl.BlockSpec(memory_space=pltpu.VMEM)
    return pl.pallas_call(
        return_kernel,
        out_shape=(
            jax.ShapeDtypeStruct((3, depth, 16 * LANES), BF),
            jax.ShapeDtypeStruct((2, depth, 16 * units), BF),
            jax.ShapeDtypeStruct((4 * HEAD, width), BF),
            jax.ShapeDtypeStruct((4 * units, width), BF),
            jax.ShapeDtypeStruct(gains.shape, F32),
        ),
        in_specs=[anywhere] * 8 + [inside],
        out_specs=(anywhere,) * 4 + (inside,),
        scratch_shapes=[
            pltpu.VMEM(mix.shape, BF), pltpu.VMEM(gate.shape, BF), pltpu.VMEM(out.shape, BF), pltpu.VMEM(down.shape, BF),
            pltpu.VMEM(mix.shape, BF), pltpu.VMEM(gate.shape, BF), pltpu.VMEM(out.shape, BF), pltpu.VMEM(down.shape, BF),
            pltpu.VMEM((5,) + gains.shape, F32), pltpu.VMEM((5,) + gains.shape, F32),
            pltpu.SemaphoreType.DMA((5,)),
            pltpu.SemaphoreType.DMA((23,)),
            pltpu.SemaphoreType.DMA((23,)),
            pltpu.SemaphoreType.DMA((50,)),
            pltpu.SemaphoreType.DMA((40,)),
        ],
        compiler_params=pltpu.CompilerParams(collective_id=3, has_side_effects=True, vmem_limit_bytes=56 << 20),
    )(mix, second[0], gate, second[1], out, second[2], down, second[3], gains)


def on_line():
    return lax.axis_size("ctx") == 4 and lax.axis_size("fsdp") == 4


def gather(own):
    return lax.all_gather(own, ("ctx", "fsdp"), axis=0, tiled=True)


def scatter(part):
    return lax.psum_scatter(part, ("ctx", "fsdp"), scatter_dimension=0, tiled=True)


def spread_halves(columns):
    halves = columns.reshape(columns.shape[:-1] + (2, HEAD // 2))
    halves = jnp.pad(halves, [(0, 0)] * (halves.ndim - 1) + [(0, SPAN - HEAD // 2)])
    return halves.reshape(columns.shape[:-1] + (LANES,))


def join_halves(columns):
    halves = columns.reshape(columns.shape[:-1] + (2, SPAN))[..., : HEAD // 2]
    return halves.reshape(columns.shape[:-1] + (HEAD,))


def angle_tables(positions):
    frequency = rope_base ** (-(jnp.arange(HEAD // 2, dtype=F32) * 2.0 / HEAD))
    frequency = jnp.pad(frequency, (0, SPAN - HEAD // 2))
    angles = positions.astype(F32)[:, None] * frequency[None, :]
    cosine = jnp.cos(angles)
    sine = jnp.sin(angles)
    return jnp.concatenate([cosine, cosine], axis=1), jnp.concatenate([-sine, sine], axis=1)


def rotate(values, cosine, sine):
    return values * cosine + jnp.roll(values, SPAN, axis=1) * sine


def rotate_back(grads, cosine, sine):
    return grads * cosine - jnp.roll(grads, SPAN, axis=1) * sine


def norm_rows(values):
    return lax.rsqrt(jnp.mean(values * values, axis=-1, keepdims=True) + norm_eps)


def norm_back(grad_out, values, factor, gain):
    shaped = grad_out * gain
    common = jnp.mean(shaped * values, axis=-1, keepdims=True)
    grad_in = factor * shaped - values * (factor * factor * factor) * common
    return grad_in, jnp.sum(grad_out * values * factor, axis=0)


def dot(left, right):
    return jnp.dot(left, right, preferred_element_type=F32)


def dot_nt(left, right):
    return lax.dot_general(left, right, (((1,), (1,)), ((), ())), preferred_element_type=F32)


def dot_tn(left, right):
    return lax.dot_general(left, right, (((0,), (0,)), ((), ())), preferred_element_type=F32)


class Plan:
    def __init__(self, width, hidden_units):
        self.c = lax.axis_index("ctx")
        self.f = lax.axis_index("fsdp")
        self.C = lax.axis_size("ctx")
        self.F = lax.axis_size("fsdp")
        self.heads = width // HEAD
        self.ratio = self.heads // KV_HEADS
        self.heads_f = self.heads // self.F
        self.groups_f = KV_HEADS // self.F
        self.share = self.C // self.heads_f
        self.units = hidden_units // (self.F * self.C)
        self.local_head = self.c // self.share
        self.part = self.c % self.share


def pick(array, index, axis):
    return lax.dynamic_index_in_dim(array, index, axis, keepdims=False)


def pack_weights(plan, mix, gate_up):
    depth = mix.shape[0]
    width = plan.heads * HEAD
    kv_width = KV_HEADS * HEAD
    F = plan.F
    queries = pick(mix[:, :width].reshape(depth, F, plan.heads_f, HEAD), plan.local_head, 2)
    group = plan.local_head // plan.ratio
    keys = pick(mix[:, width : width + kv_width].reshape(depth, F, plan.groups_f, HEAD), group, 2)
    values = pick(mix[:, width + kv_width :].reshape(depth, F, plan.groups_f, HEAD), group, 2)
    values = jnp.pad(values, ((0, 0), (0, 0), (0, LANES - HEAD)))
    half = gate_up.shape[1] // 2
    gate = pick(gate_up[:, :half].reshape(depth, F, plan.C, plan.units), plan.c, 2)
    up = pick(gate_up[:, half:].reshape(depth, F, plan.C, plan.units), plan.c, 2)
    packed = jnp.concatenate([spread_halves(queries), spread_halves(keys), values, gate, up], axis=2)
    return jnp.swapaxes(packed, 0, 1)


def attend(plan, q_part, k, v, positions, part_positions):
    scores = dot_nt(q_part, k) * HEAD ** (-0.5)
    allowed = positions[None, :] <= part_positions[:, None]
    scores = jnp.where(allowed, scores, masked_value)
    top = jnp.max(scores, axis=-1, keepdims=True)
    weights = jnp.exp(scores - top)
    total = jnp.sum(weights, axis=-1, keepdims=True)
    context = dot((weights / total).astype(BF), v)
    return context.astype(BF), top + jnp.log(total)


def attend_back(q_part, k, v, context_grad, context, log_total, positions, part_positions):
    scale = HEAD ** (-0.5)
    common = jnp.sum(context_grad.astype(F32) * context.astype(F32), axis=-1, keepdims=True)
    allowed = positions[None, :] <= part_positions[:, None]
    scores = dot_nt(q_part, k) * scale
    weights = jnp.exp(jnp.where(allowed, scores, masked_value) - log_total)
    weight_grad = dot_nt(context_grad, v)
    score_grad = (weights * (weight_grad - common)).astype(BF)
    value_grad = dot_tn(weights.astype(BF), context_grad)
    key_grad = dot_tn(score_grad, q_part) * scale
    query_grad = dot(score_grad, k) * scale
    return query_grad, key_grad, value_grad


def forward_layer(plan, x_own, weights, gains, positions, part_positions, tables):
    mix_cut, gate_cut, out, down = weights
    cosine, sine = tables
    length = positions.shape[0]
    x_all = gather(x_own)
    x32 = x_all.astype(F32)
    factor = norm_rows(x32)
    normed = (x32 * factor * gains[0]).astype(BF)
    mixed = dot(normed, mix_cut)
    q = rotate(mixed[:, :LANES], cosine, sine).astype(BF)
    k = rotate(mixed[:, LANES : 2 * LANES], cosine, sine).astype(BF)
    v = mixed[:, 2 * LANES :].astype(BF)
    rows = length // plan.share
    start = plan.part * rows
    q_part = lax.dynamic_slice_in_dim(q, start, rows, 0)
    context, log_total = attend(plan, q_part, k, v, positions, part_positions)
    partial = dot(context[:, :HEAD], out).astype(BF)
    if plan.share > 1:
        partial = lax.dynamic_update_slice_in_dim(
            jnp.zeros((length, partial.shape[1]), BF), partial, start, 0
        )
    middle = x_own.astype(F32) + scatter(partial)
    factor_two = norm_rows(middle)
    normed_two = gather((middle * factor_two * gains[1]).astype(BF))
    both = dot(normed_two, gate_cut)
    hidden = (jax.nn.silu(both[:, : plan.units]) * both[:, plan.units :]).astype(BF)
    result = middle + scatter(dot(hidden, down).astype(BF))
    kept = (x_own, normed, q_part, k, v, context, log_total, middle, normed_two, both, hidden)
    return result.astype(BF), kept


def backward_layer(plan, grad_own, weights, gains, kept, positions, part_positions, tables, part_tables):
    mix_cut, gate_cut, out, down = weights
    x_own, normed, q_part, k, v, context, log_total, middle, normed_two, both, hidden = kept
    length = positions.shape[0]
    rows = length // plan.share
    start = plan.part * rows
    grad_all = gather(grad_own)
    hidden_grad = dot_nt(grad_all, down)
    gate = both[:, : plan.units]
    up = both[:, plan.units :]
    sig = jax.nn.sigmoid(gate)
    gate_grad = hidden_grad * up * sig * (1.0 + gate * (1.0 - sig))
    up_grad = hidden_grad * gate * sig
    both_grad = jnp.concatenate([gate_grad, up_grad], axis=1).astype(BF)
    normed_two_grad = scatter(dot_nt(both_grad, gate_cut).astype(BF))
    middle_grad, feed_gain_grad = norm_back(normed_two_grad, middle, norm_rows(middle), gains[1])
    middle_grad = middle_grad + grad_own.astype(F32)
    middle_low = gather(middle_grad.astype(BF))
    middle_part = lax.dynamic_slice_in_dim(middle_low, start, rows, 0)
    context_grad = jnp.pad(dot_nt(middle_part, out), ((0, 0), (0, LANES - HEAD))).astype(BF)
    query_grad, key_grad, value_grad = attend_back(
        q_part, k, v, context_grad, context, log_total, positions, part_positions
    )
    query_grad = rotate_back(query_grad, *part_tables).astype(BF)
    if plan.share > 1:
        query_grad = lax.dynamic_update_slice_in_dim(
            jnp.zeros((length, LANES), BF), query_grad, start, 0
        )
    key_grad = rotate_back(key_grad, *tables).astype(BF)
    mixed_grad = jnp.concatenate([query_grad, key_grad, value_grad.astype(BF)], axis=1)
    normed_grad = scatter(dot_nt(mixed_grad, mix_cut).astype(BF))
    x32 = x_own.astype(F32)
    start_grad, attention_gain_grad = norm_back(normed_grad, x32, norm_rows(x32), gains[0])
    start_grad = start_grad + middle_grad
    mix_grad = jnp.stack(
        [dot_tn(normed, part).astype(BF) for part in (query_grad, key_grad, value_grad.astype(BF))]
    )
    gate_cut_grad = jnp.stack(
        [dot_tn(normed_two, part.astype(BF)).astype(BF) for part in (gate_grad, up_grad)]
    )
    out_grad = dot_tn(context, middle_part).astype(BF)[:HEAD]
    down_grad = dot_tn(hidden, grad_all).astype(BF)
    return start_grad, (mix_grad, gate_cut_grad, out_grad, down_grad), jnp.stack([attention_gain_grad, feed_gain_grad])


def swap_sections(array):
    return lax.ppermute(array, "section", [(0, 1), (1, 0)])


def by_layer_of(section, own, other):
    first = section == 0
    return jnp.where(first, own, other), jnp.where(first, other, own)


def shared_weights(plan, section, attention_gain, query_key_value, output_weight, feed_gain, gate_up, down_weight):
    depth = query_key_value.shape[1]
    width = depth * plan.F
    gains = lax.all_gather(
        jnp.stack([attention_gain[0], feed_gain[0]]), ("section", "fsdp"), axis=0, tiled=False
    )
    gains = gains.reshape(2, plan.F, 2, depth)
    gains = jnp.swapaxes(gains, 1, 2).reshape(2, 2, width).astype(F32)
    packed = pack_weights(plan, query_key_value[0], gate_up[0])
    own_cut = lax.all_to_all(packed, "fsdp", 0, 0).reshape(width, -1)
    own_out = lax.dynamic_slice_in_dim(output_weight[0], plan.local_head * HEAD, HEAD, 0)
    own_down = lax.dynamic_slice_in_dim(down_weight[0], plan.c * plan.units, plan.units, 0)
    cuts = by_layer_of(section, own_cut, swap_sections(own_cut))
    outs = by_layer_of(section, own_out, swap_sections(own_out))
    downs = by_layer_of(section, own_down, swap_sections(own_down))
    weights = [(cuts[s][:, : 3 * LANES], cuts[s][:, 3 * LANES :], outs[s], downs[s]) for s in range(2)]
    return weights, gains


def returned_grads(plan, section, weight_grads, gain_grads, depth):
    C, F = plan.C, plan.F
    gain_sum = jnp.concatenate([gain_grads[0], gain_grads[1]])
    if on_line():
        mixes, both, out_grad, down_grad, gain_sum = return_call(
            weight_grads[0], weight_grads[1], jnp.pad(gain_sum, ((0, 4), (0, 0)))
        )
        slots = mixes.astype(F32).reshape(3, depth, 16, LANES)
        q_grad = join_halves(slots[0]).reshape(depth, -1)
        pairs = slots[1:].reshape(2, depth, KV_HEADS, 2, LANES).sum(axis=3)
        k_grad = join_halves(pairs[0]).reshape(depth, -1)
        v_grad = pairs[1][..., :HEAD].reshape(depth, -1)
        mix_grad = jnp.concatenate([q_grad, k_grad, v_grad], axis=1)
        gate_up_grad = jnp.concatenate([both[0], both[1]], axis=1).astype(F32)
        out_grad = out_grad.astype(F32)
        down_grad = down_grad.astype(F32)
        gain_sum = gain_sum[:4]
    else:
        def collected(index):
            first, second = weight_grads[0][index], weight_grads[1][index]
            own = jnp.where(section == 0, first, second)
            away = jnp.where(section == 0, second, first)
            return (own.astype(F32) + swap_sections(away).astype(F32)).astype(BF)

        cut_grad = jnp.concatenate(list(collected(0)) + list(collected(1)), axis=1)
        cut_grad = lax.all_to_all(cut_grad.reshape(F, depth, -1), "fsdp", 0, 0)
        cut_grad = lax.all_gather(cut_grad, "ctx", axis=0, tiled=False)
        out_grad = lax.all_gather(collected(2), "ctx", axis=0, tiled=False)
        down_grad = lax.all_gather(collected(3), "ctx", axis=0, tiled=True).astype(F32)

        def heads_of(columns, count):
            folded = columns.astype(F32).reshape(count, C // count, F, depth, columns.shape[-1]).sum(axis=1)
            return jnp.transpose(folded, (2, 1, 0, 3))

        q_grad = join_halves(heads_of(cut_grad[..., :LANES], plan.heads_f)).reshape(depth, -1)
        k_grad = join_halves(heads_of(cut_grad[..., LANES : 2 * LANES], plan.groups_f)).reshape(depth, -1)
        v_grad = heads_of(cut_grad[..., 2 * LANES : 3 * LANES], plan.groups_f)[..., :HEAD].reshape(depth, -1)
        mix_grad = jnp.concatenate([q_grad, k_grad, v_grad], axis=1)
        both = jnp.transpose(cut_grad[..., 3 * LANES :], (2, 1, 0, 3)).astype(F32)
        gate_up_grad = jnp.concatenate(
            [both[..., : plan.units].reshape(depth, -1), both[..., plan.units :].reshape(depth, -1)], axis=1
        )
        out_grad = out_grad.astype(F32).reshape(plan.heads_f, plan.share, HEAD, depth * F).sum(axis=1).reshape(-1, depth * F)

        gain_sum = lax.psum(gain_sum, ("section", "ctx", "fsdp"))
    gain_sum = lax.dynamic_slice_in_dim(gain_sum, 2 * section, 2, 0)
    gain_sum = lax.dynamic_slice_in_dim(gain_sum, plan.f * depth, depth, 1)
    return mix_grad, gate_up_grad, out_grad, down_grad, gain_sum


def on_device(
    inputs, cotangent, attention_gain, query_key_value, output_weight, feed_gain, gate_up, down_weight, block_order
):
    section = lax.axis_index("section")
    width = inputs.shape[2]
    hidden_units = down_weight.shape[1] * lax.axis_size("fsdp")
    plan = Plan(width, hidden_units)
    rows = inputs.shape[1]
    C, F = plan.C, plan.F
    length = rows * C * F
    depth = query_key_value.shape[1]

    def by_layer(own, other):
        first = section == 0
        return jnp.where(first, own, other), jnp.where(first, other, own)

    order = pick(block_order, section, 0)
    positions = (order[:, None] * rows + jnp.arange(rows, dtype=jnp.int32)[None, :]).reshape(length)
    part_rows = length // plan.share
    part_positions = lax.dynamic_slice_in_dim(positions, plan.part * part_rows, part_rows, 0)
    tables = angle_tables(positions)
    part_tables = angle_tables(part_positions)

    x = pick(inputs, section, 0)
    grad = pick(cotangent, section, 0)
    results = []
    input_grads = [None, None]
    weight_grads = [None, None]
    gain_grads = [None, None]
    kept = []
    if on_line():
        own_gains = jnp.pad(jnp.concatenate([attention_gain, feed_gain]), ((0, 14), (0, 0)))
        shared = share_call(query_key_value, output_weight, gate_up, down_weight, own_gains)
        places = (positions[:, None], positions[None, :])
        for s in range(2):
            *keep, result = forward_call(s, x, shared, tables, places)
            kept.append((x, keep))
            results.append(result)
            x = result
        for s in (1, 0):
            input_grads[s], grad, *weight_grads[s], gain_grads[s] = backward_call(
                s, grad, shared, tables, places, *kept[s]
            )
    else:
        weights, gains = shared_weights(
            plan, section, attention_gain, query_key_value, output_weight, feed_gain, gate_up, down_weight
        )
        for s in range(2):
            x, keep = forward_layer(plan, x, weights[s], gains[s], positions, part_positions, tables)
            kept.append(keep)
            results.append(x)
        for s in (1, 0):
            input_grads[s], weight_grads[s], gain_grads[s] = backward_layer(
                plan, grad, weights[s], gains[s], kept[s], positions, part_positions, tables, part_tables
            )
            grad = input_grads[s].astype(BF)

    def mine_and_theirs(first, second):
        return jnp.where(section == 0, first, second), jnp.where(section == 0, second, first)

    def by_batch(first, second):
        own, away = mine_and_theirs(first, second)
        return jnp.stack(by_layer(own, swap_sections(away)))

    section_outputs = by_batch(*results)
    section_input_grads = by_batch(*input_grads)

    shard_grads = returned_grads(plan, section, weight_grads, gain_grads, depth)
    mix_grad, gate_up_grad, out_grad, down_grad, gain_sum = shard_grads
    return (
        section_outputs[None],
        section_input_grads[None],
        gain_sum[0][None],
        mix_grad[None],
        out_grad[None],
        gain_sum[1][None],
        gate_up_grad[None],
        down_grad[None],
    )


def solution(mesh):
    placed = (
        P(None, ("ctx", "fsdp"), None),
        P(None, ("ctx", "fsdp"), None),
        P("section", "fsdp"),
        P("section", "fsdp", None),
        P("section", "fsdp", None),
        P("section", "fsdp"),
        P("section", "fsdp", None),
        P("section", "fsdp", None),
        P(),
    )
    return jax.shard_map(
        on_device,
        mesh=mesh,
        in_specs=placed,
        out_specs=(
            P("section", None, ("ctx", "fsdp"), None),
            P("section", None, ("ctx", "fsdp"), None),
            P("section", "fsdp"),
            P("section", "fsdp", None),
            P("section", "fsdp", None),
            P("section", "fsdp"),
            P("section", "fsdp", None),
            P("section", "fsdp", None),
        ),
        check_vma=False,
    )
```

time: 1010 us -> 872 us (0.86)
  Pallas kernels: 444 us -> 775 us
  blocking collectives: 162 us -> 0 us
  waiting for transfers between devices: 122 us -> 0.01 us
  local copies, waits for them, and re-layouts: 119 us -> 44.3 us
  matrix products: 65.1 us -> 0 us
  other arithmetic: 63.5 us -> 38.7 us
  between operations: 15.8 us -> 1.36 us
    pallas_call x16 -> x6, Pallas kernels: 444 us -> 775 us  [the longest x1 295 us: return_call(): pl.pallas_call(return_kernel, out_shape=(jax.ShapeDtypeStruct((3, depth,...]
    ppermute x8 -> x2, waiting for transfers between devices: 80.8 us -> 0.01 us  [swap_sections(): return lax.ppermute(array, 'section', [(0, 1), (1, 0)])]
    all_to_all x2 -> x0, blocking collectives: 74.4 us -> none  [the longest x1 37.4 us: on_device(): cut_grad = lax.all_to_all(cut_grad.reshape(F, depth, -1), 'fsdp', 0, 0)]
    dot_general x36 -> x0, matrix products: 65.1 us -> none  [the longest x12 26 us: dot_nt(): lax.dot_general(left, right, (((1,), (1,)), ((), ())), preferred_element_...]
    psum x1 -> x0, blocking collectives: 56.1 us -> none  [on_device(): gain_sum = lax.psum(gain_sum, ('section', 'ctx', 'fsdp'))]
    all_gather x3 -> x0, waiting for transfers between devices: 41.1 us -> none  [the longest x1 41.1 us: on_device(): cut_grad = lax.all_gather(cut_grad, 'ctx', axis=0, tiled=False)]
    unnamed x169 -> x47, local copies, waits for them, and re-layouts: 42.9 us -> 11.1 us
    all_gather x1 -> x0, blocking collectives: 31.3 us -> none  [on_device(): lax.all_gather(jnp.stack([attention_gain[0], feed_gain[0]]), ('section',...]
  transfers between devices with their start and end apart: 11 -> 2, of which waited for: 3 -> 0; matrix products, arithmetic and copies ran while one was open for 5% -> 8% of each run, Pallas kernels for 20% -> 57%
where the time goes in v2:
time: 872 us; the launch traced here: 862 us
  Pallas kernels  775 us (89%)
  local copies, waits for them, and re-layouts  44.3 us (5%)
  other arithmetic  38.7 us (4%)
    pallas_call x1, Pallas kernels, return_call(): pl.pallas_call(return_kernel, out_shape=(jax.ShapeDtypeStruct((3, depth,...  295 us
    pallas_call x2, Pallas kernels, backward_call(): pl.pallas_call(functools.partial(backward_kernel, layer), out_shape=[jax....  195 us
    pallas_call x2, Pallas kernels, forward_call(): pl.pallas_call(functools.partial(forward_kernel, layer), out_shape=[jax.S...  194 us
    pallas_call x1, Pallas kernels, share_call(): pl.pallas_call(share_kernel, out_shape=(jax.ShapeDtypeStruct((2, width, 3...  91.2 us
  transfers between devices with their start and end apart: 2, of which 0 were waited for; matrix products, arithmetic and copies ran while one was open for 8% of the time, Pallas kernels for 57%

profile of v2, /device:TPU:0, one launch (start us, length us, event | category | flops | bytes accessed | tf_op | source)
XLA Modules:
  0.0 862.3 jit_solution(12677534690376760067)
XLA Ops:
  5.0 1.9 fusion
  8.2 91.2 %shard_map.152 = (bf16[2,1536,384]{2,1,0:T(8,128)(2,1)S(1)}, bf16[2,1536,512]{2,1,0:T(8,128)(2,1)}, bf16[2,96,1536]{2,1,0:T(8,128)(2,1)S(1)}, bf16[2,256,1536]{2,1,0:T(8,128)(2,1)S(1)}, bf16[2,16,1536]{2,1,0:T(8,128)(2,1)S(1)}) custom-call(bf16[1,384,3072]{2,1,0:T(8,128)(2,1)} %mix.1, bf16[1,384,1536]{2,1,0:T(8,128)(2,1)S(1)} %copy-done.6, ...), custom_call_target="tpu_custom_call" | custom-call | tf_op jit(solution)/shard_map/pallas_call | solution.py:734
  99.5 1.4 copy-done.2
  103.4 98.2 %shard_map.153 = (bf16[1024,1536]{1,0:T(8,128)(2,1)}, bf16[1024,128]{1,0:T(8,128)(2,1)}, bf16[1024,128]{1,0:T(8,128)(2,1)}, bf16[1024,128]{1,0:T(8,128)(2,1)}, b...) custom-call(bf16[64,1536]{1,0:T(8,128)(2,1)} %dynamic-slice_bitcast_, ...), custom_call_target="tpu_custom_call" | custom-call | tf_op jit(solution)/shard_map/pallas_call | solution.py:542
  201.7 95.4 %shard_map.154 = (bf16[1024,1536]{1,0:T(8,128)(2,1)}, bf16[1024,128]{1,0:T(8,128)(2,1)}, bf16[1024,128]{1,0:T(8,128)(2,1)}, bf16[1024,128]{1,0:T(8,128)(2,1)}, b...) custom-call(bf16[64,1536]{1,0:T(8,128)(2,1)} %get-tuple-element.56.x, ...), custom_call_target="tpu_custom_call" | custom-call | tf_op jit(solution)/shard_map/pallas_call | solution.py:542
  297.1 1.7 broadcast_select_fusion.2
  300.4 97.9 %shard_map.155 = (f32[64,1536]{1,0:T(8,128)}, bf16[64,1536]{1,0:T(8,128)(2,1)}, bf16[3,1536,128]{2,1,0:T(8,128)(2,1)}, bf16[2,1536,256]{2,1,0:T(8,128)(2,1)}, bf...) custom-call(bf16[64,1536]{1,0:T(8,128)(2,1)} %dynamic-slice_bitcast_fusion.grad_own, ...), custom_call_target="tpu_custom_call" | custom-call | tf_op jit(solution)/shard_map/pallas_call | solution.py:575
  398.3 96.9 %shard_map.156 = (f32[64,1536]{1,0:T(8,128)}, bf16[64,1536]{1,0:T(8,128)(2,1)}, bf16[3,1536,128]{2,1,0:T(8,128)(2,1)}, bf16[2,1536,256]{2,1,0:T(8,128)(2,1)}, bf...) custom-call(bf16[64,1536]{1,0:T(8,128)(2,1)} %get-tuple-element.67.grad_own, ...), custom_call_target="tpu_custom_call" | custom-call | tf_op jit(solution)/shard_map/pallas_call | solution.py:575
  496.1 2.0 collective-permute-start.1
  499.4 295.2 %shard_map.157 = (bf16[3,384,2048]{2,1,0:T(8,128)(2,1)}, bf16[2,384,4096]{2,1,0:T(8,128)(2,1)}, bf16[384,1536]{1,0:T(8,128)(2,1)}, bf16[1024,1536]{1,0:T(8,128)(2,1)}, f32[8,1536]{1,0:T(8,128)}) custom-call(bf16[3,1536,128]{2,1,0:T(8,128)(2,1)} %get-tuple-element.79.mix_0, bf16[3,1536,128]{2,1,0:T(8,128)(2,1)} %get-tuple-element.80.mix_1, ...), custom_call_target="tpu_custom_call" | custom-call | tf_op jit(solution)/shard_map/pallas_call | solution.py:941
  794.7 1.9 slice.50
  797.5 3.6 slice.52
  801.0 1.7 bitcast_convert_fusion.1
  802.7 2.4 copy.27
  805.1 3.3 slice.51
  808.4 9.4 %reshape.119 = f32[2,384,8,2,128]{4,3,2,1,0:T(2,128)} reshape(f32[2,384,2048]{2,1,0:T(8,128)} %slice.52) | data formatting | bytes 12582912 | tf_op jit(solution)/shard_map/reshape | solution.py:1204
  817.7 10.3 %reduce_sum.9 = f32[2,384,8,128]{3,2,1,0:T(8,128)S(1)} reduce(f32[2,384,8,2,128]{4,3,2,1,0:T(2,128)} %reshape.119, f32[]{:T(128)} %constant.49.clone.1), dimensions={3}, to_apply=%region_0.1 | reduce | flops 786432 | bytes 9437188 | tf_op jit(solution)/shard_map/reduce_sum | solution.py:1204
  828.0 1.9 fusion.8
  829.9 1.9 copy.28
  832.9 3.0 copy.29
  835.9 5.6 bitcast_convert_fusion
  842.4 6.3 maximum_convert_fusion
  848.7 2.5 maximum_bitcast_fusion
  851.2 6.2 copy.30
  (70 shorter events, 19.3 us)
Async XLA Ops:
  0.6 2.9 copy-start
  0.6 7.5 copy-start.6
  99.4 1.4 copy-start.2
  100.8 1.1 copy-start.3
  102.0 0.8 copy-start.4
  201.7 95.4 %copy-start.11 = (bf16[64,1536]{1,0:T(8,128)(2,1)S(1)}, bf16[64,1536]{1,0:T(8,128)(2,1)}, u32[]{:S(2)}) copy-start(bf16[64,1536]{1,0:T(8,128)(2,1)} %get-tuple-element.56.x_own) | copy-start | bytes 589828
  201.7 98.0 %copy-start.18 = (bf16[2,64,1536]{2,1,0:T(8,128)(2,1)S(1)}, bf16[2,64,1536]{2,1,0:T(8,128)(2,1)}, u32[]{:S(2)}) copy-start(bf16[2,64,1536]{2,1,0:T(8,128)(2,1)} %param.10) | copy-start | bytes 1179652
  298.8 559.3 %collective-permute-start = (bf16[64,1536]{1,0:T(8,128)(2,1)}, bf16[64,1536]{1,0:T(8,128)(2,1)}, u32[]{:S(2)}, u32[]{:S(2)}) collective-permute-start(bf16[64,1536]{1,0:T(8,128)(2,1)} %broadcast_select_fusion.2), channel_id=1, source_target_pairs={{0,16},{16,0},{1,17},{17,1},{2,18},{18,2},{3,19},{19,3},{4,20},{20... | collective-permute-start | bytes 589832 | tf_op jit(solution)/shard_map/ppermute | solution.py:1168
  398.3 97.0 %copy-start.13 = (f32[64,1536]{1,0:T(8,128)S(1)}, f32[64,1536]{1,0:T(8,128)}, u32[]{:S(2)}) copy-start(f32[64,1536]{1,0:T(8,128)} %get-tuple-element.78) | copy-start | bytes 1179652
  398.3 99.8 %copy-start.19 = (f32[2,1536]{1,0:T(2,128)S(1)}, f32[2,1536]{1,0:T(2,128)}, u32[]{:S(2)}) copy-start(f32[2,1536]{1,0:T(2,128)} %get-tuple-element.88) | copy-start | bytes 36868
  496.1 363.7 %collective-permute-start.1 = (f32[64,1536]{1,0:T(8,128)}, f32[64,1536]{1,0:T(8,128)}, u32[]{:S(2)}, u32[]{:S(2)}) collective-permute-start(f32[64,1536]{1,0:T(8,128)} %broadcast_select_fusion), channel_id=1, source_target_pairs={{0,16},{16,0},{1,17},{17,1},{2,18},{18,2},{3,19},{19,3},{4,20},{20... | collective-permute-start | bytes 1179656 | tf_op jit(solution)/shard_map/ppermute | solution.py:1168
  794.6 2.8 copy-start.7
  797.5 3.6 copy-start.16
  832.9 8.7 %slice-start = ((s8[6291456]{0:T(1024)(128)(4,1)}), s8[2097152]{0:T(1024)(128)(4,1)S(1)}, s32[]{:S(2)}) async-start(s8[6291456]{0:T(1024)(128)(4,1)} %bitcast.36), calls=%async_computation | async-start | bytes 4194304
  835.9 5.6 slice-start.1
  842.3 6.4 copy-start.8
  842.3 6.4 copy-start.9
  842.4 6.4 copy-start.10
  848.7 2.5 copy-start.20
  851.2 6.9 copy-start.12
  851.2 6.9 copy-start.17
  851.2 8.6 copy-start.14
  851.2 8.6 copy-start.15
  851.2 10.6 %copy-start.1 = (bf16[2,64,1536]{2,1,0:T(8,128)(2,1)S(1)}, bf16[2,64,1536]{2,1,0:T(8,128)(2,1)}, u32[]{:S(2)}) copy-start(bf16[2,64,1536]{2,1,0:T(8,128)(2,1)} %param.9) | copy-start | bytes 1179652
  (1 other events, 0.6 us)

commit v3 on v2

--- a/solution.py
+++ b/solution.py
@@ -50,7 +50,7 @@
     return [c, c + 1 - 2 * lax.rem(c, 2), jnp.where(low, 2, 1), jnp.where(low, 3, 0)]
 
 
-def gather_rows(whole, rows, send, recv, ready=None):
+def gather_rows(whole, rows, send, recv, ready=None, started=None):
     c = lax.axis_index("ctx")
     f = lax.axis_index("fsdp")
     across = f + 2 - 4 * (f // 2)
@@ -90,6 +90,8 @@
         go(at(c, f, h), 4 + h, 8 + 2 * c + h, {"fsdp": across})
     for h in range(2):
         go(at(c, f, h), 12 + h, 16 + 2 * c + h, {"fsdp": twin})
+    if started is not None:
+        started()
 
     def along(step, h):
         d = order[step]
@@ -145,7 +147,7 @@
 GATHER_RECVS = 33
 
 
-def scatter_sum(part, total, land, send, recv, produce=None, meanwhile=None):
+def scatter_sum(part, total, land, send, recv, produce=None, meanwhile=None, tick=None):
     c = lax.axis_index("ctx")
     f = lax.axis_index("fsdp")
     across = f + 2 - 4 * (f // 2)
@@ -237,9 +239,13 @@
     begin(3)
     over(2, 1)
     onward(1, 0)
+    if tick is not None:
+        tick()
     over(3, 0)
     onward(1, 1)
     over(3, 1)
+    if tick is not None:
+        tick()
     onward(2, 0)
     onward(2, 1)
     if meanwhile is not None:
@@ -283,6 +289,196 @@
     return lax.rsqrt(jnp.mean(values * values, axis=-1, keepdims=True) + norm_eps)
 
 
+def greet_all(peers):
+    barrier = pltpu.get_barrier_semaphore()
+    for peer in peers:
+        pl.semaphore_signal(barrier, inc=1, device_id=peer, device_id_type=MESH)
+    return len(peers)
+
+
+def greet_more(peers):
+    c = lax.axis_index("ctx")
+    barrier = pltpu.get_barrier_semaphore()
+    count = greet_all(peers)
+    inner = jnp.logical_and(c > 0, c < 3)
+
+    @pl.when(c < 3)
+    def _():
+        pl.semaphore_signal(barrier, inc=1, device_id={"ctx": c + 1}, device_id_type=MESH)
+
+    @pl.when(c > 0)
+    def _():
+        pl.semaphore_signal(barrier, inc=1, device_id={"ctx": c - 1}, device_id_type=MESH)
+
+    @pl.when(inner)
+    def _():
+        pl.semaphore_wait(barrier, count + 2)
+
+    @pl.when(jnp.logical_not(inner))
+    def _():
+        pl.semaphore_wait(barrier, count + 1)
+
+
+def head_choice(value_part):
+    source = lax.broadcasted_iota(jnp.int32, (4 * HEAD, 4 * LANES), 0)
+    lane = lax.broadcasted_iota(jnp.int32, (4 * HEAD, 4 * LANES), 1)
+    head = lane // LANES
+    inside = lane - head * LANES
+    if value_part:
+        wanted = jnp.where(inside < HEAD, head * HEAD + inside, -1)
+    else:
+        half = inside // SPAN
+        place = inside - half * SPAN
+        wanted = jnp.where(place < HEAD // 2, head * HEAD + half * (HEAD // 2) + place, -1)
+    return jnp.where(source == wanted, 1.0, 0.0).astype(BF)
+
+
+class Share:
+    def __init__(self, sources, targets, scratch, sems):
+        self.mix, self.out, self.gate_up, self.down, self.gains = sources
+        self.w_mix, self.w_gate, self.w_out, self.w_down, self.w_gains = targets
+        self.mix_v, self.heads_v = scratch
+        self.local, self.send, self.recv = sems
+        self.s = lax.axis_index("section")
+        self.c = lax.axis_index("ctx")
+        self.f = lax.axis_index("fsdp")
+        self.other = 1 - self.s
+        self.depth = self.mix.shape[1]
+        self.units = self.w_down.shape[1]
+        self.peers = [lax.rem(self.f + k, 4) for k in range(1, 4)]
+        self.rows = pl.ds(pl.multiple_of(self.f * self.depth, self.depth), self.depth)
+        self.pending = []
+
+    def greeted(self):
+        return (
+            [{"fsdp": peer} for peer in self.peers]
+            + [{"section": self.other}]
+            + [{"section": self.other, "fsdp": peer} for peer in self.peers]
+        )
+
+    def copy(self, src, dst, slot, arrival, peer):
+        return pltpu.make_async_remote_copy(
+            src, dst, self.send.at[slot], self.recv.at[arrival], device_id=peer, device_id_type=MESH
+        )
+
+    def go(self, src, dst, slot, arrival, peer):
+        one = self.copy(src, dst, slot, arrival, peer)
+        one.start()
+        self.pending.append(one)
+
+    def keep(self, src, dst, slot):
+        one = pltpu.make_async_copy(src, dst, self.local.at[slot])
+        one.start()
+        return one
+
+    def load(self):
+        self.loaded = self.keep(self.mix.at[0], self.mix_v, 0)
+
+    def lanes(self, peer, part):
+        head = peer * 4 + self.c
+        start = head * LANES if part == 0 else (16 + 8 * (part - 1) + head // 2) * LANES
+        return self.heads_v.at[:, pl.ds(pl.multiple_of(start, LANES), LANES)]
+
+    def put(self, part):
+        return self.w_mix.at[self.s, self.rows, pl.ds(part * LANES, LANES)]
+
+    def send_mix(self):
+        self.loaded.wait()
+        for g in range(8):
+            self.heads_v[:, g * 4 * LANES : (g + 1) * 4 * LANES] = kernel_dot(
+                self.mix_v[:, g * 4 * HEAD : (g + 1) * 4 * HEAD], head_choice(g >= 6)
+            ).astype(BF)
+        for k, peer in enumerate(self.peers):
+            for part in range(3):
+                self.copy(self.lanes(peer, part), self.put(part), k, self.f, {"fsdp": peer}).start()
+        self.own_mix = [self.keep(self.lanes(self.f, part), self.put(part), 2 + part) for part in range(3)]
+        out_rows = self.out.at[0, pl.ds(pl.multiple_of(self.c * HEAD, HEAD), HEAD)]
+        down_rows = self.down.at[0, pl.ds(pl.multiple_of(self.c * self.units, self.units), self.units)]
+        self.own_out = self.keep(out_rows, self.w_out.at[self.s], 7)
+        self.own_down = self.keep(down_rows, self.w_down.at[self.s], 8)
+        mine = self.w_gains.at[self.s, :, pl.ds(pl.multiple_of(self.f * self.depth, self.depth), self.depth)]
+        for k, peer in enumerate(self.peers):
+            self.go(self.gains, mine, 20 + k, 16 + 4 * self.s + self.f, {"fsdp": peer})
+            self.go(self.gains, mine, 23 + k, 16 + 4 * self.s + self.f, {"section": self.other, "fsdp": peer})
+        self.go(self.gains, mine, 26, 16 + 4 * self.s + self.f, {"section": self.other})
+        self.own_gains = self.keep(self.gains, mine, 1)
+
+    def gate_piece(self, peer, part):
+        hidden_units = self.gate_up.shape[2] // 2
+        start = pl.multiple_of(part * hidden_units + (peer * 4 + self.c) * self.units, self.units)
+        return self.gate_up.at[0, :, pl.ds(start, self.units)]
+
+    def gate_put(self, part):
+        return self.w_gate.at[self.s, self.rows, pl.ds(part * self.units, self.units)]
+
+    def send_gate(self):
+        for k, peer in enumerate(self.peers):
+            for part in range(2):
+                self.copy(self.gate_piece(peer, part), self.gate_put(part), 3 + k, 4 + self.f, {"fsdp": peer}).start()
+
+    def keep_gate(self):
+        self.own_gate = [self.keep(self.gate_piece(self.f, part), self.gate_put(part), 5 + part) for part in range(2)]
+
+    def slab(self, ref, origin):
+        return ref.at[self.s, pl.ds(pl.multiple_of(origin * self.depth, self.depth), self.depth)]
+
+    def cross_own(self, ref, copies, slot, base):
+        for one in copies:
+            one.wait()
+        self.go(self.slab(ref, self.f), self.slab(ref, self.f), slot, base + self.f, {"section": self.other})
+
+    def cross_slab(self, ref, k, slot, arrival, base):
+        origin = lax.rem(self.f + 3 - k, 4)
+        block = self.slab(ref, origin)
+        self.copy(block, block, 0, arrival + origin, {"fsdp": origin}).wait_recv()
+        self.go(block, block, slot + k, base + origin, {"section": self.other})
+
+    def cross_mix(self):
+        self.cross_own(self.w_mix, self.own_mix, 6, 8)
+        for k in range(3):
+            self.cross_slab(self.w_mix, k, 7, 0, 8)
+        self.own_out.wait()
+        self.go(self.w_out.at[self.s], self.w_out.at[self.s], 10, 24, {"section": self.other})
+        self.cross_own(self.w_gate, self.own_gate, 11, 12)
+
+    def cross_gate(self):
+        for k in range(3):
+            self.cross_slab(self.w_gate, k, 12, 4, 12)
+        self.own_down.wait()
+        self.go(self.w_down.at[self.s], self.w_down.at[self.s], 15, 25, {"section": self.other})
+
+    def there(self, ref, arrival):
+        self.copy(ref, ref, 0, arrival, {"section": self.other}).wait_recv()
+
+    def mix_there(self):
+        self.own_gains.wait()
+        for origin in range(4):
+            rows = pl.ds(origin * self.depth, self.depth)
+            self.there(self.w_mix.at[self.other, rows], 8 + origin)
+            self.there(self.w_gains.at[self.other, :, rows], 16 + 4 * self.other + origin)
+        for k in range(3):
+            origin = lax.rem(self.f + 3 - k, 4)
+            columns = pl.ds(pl.multiple_of(origin * self.depth, self.depth), self.depth)
+            self.there(self.w_gains.at[self.s, :, columns], 16 + 4 * self.s + origin)
+        self.there(self.w_out.at[self.other], 24)
+
+    def gate_there(self):
+        for origin in range(4):
+            self.there(self.w_gate.at[self.other, pl.ds(origin * self.depth, self.depth)], 12 + origin)
+
+    def down_there(self):
+        self.there(self.w_down.at[self.other], 25)
+
+    def finish(self):
+        for k, peer in enumerate(self.peers):
+            block = self.slab(self.w_mix, self.f)
+            self.copy(block, block, k, 0, {"fsdp": peer}).wait_send()
+            block = self.slab(self.w_gate, self.f)
+            self.copy(block, block, 3 + k, 0, {"fsdp": peer}).wait_send()
+        for one in self.pending:
+            one.wait_send()
+
+
 class Loads:
     def __init__(self, sems):
         self.sems = sems
@@ -299,11 +495,13 @@
     return pl.ds(pl.multiple_of(d * 4 * rows, 4 * rows), 4 * rows)
 
 
-def forward_kernel(layer, x_own, w_mix, w_gate, w_out, w_down, w_gains, cosine, sine, place_col, place_row,
-                   normed_o, q_o, k_o, v_o, context_o, log_o, middle_o, normed_two_o, both_o, result_o,
-                   x_v, normed_v, q_v, k_v, v_v, context_v, log_v, middle_v, two_v, both_v, hidden_v, result_v,
-                   mix_v, gate_v, out_v, down_v, gains_v, part_v, land_a, land_b, total_v, local, save,
-                   send_a, recv_a, send_b, recv_b, send_c, recv_c, send_d, recv_d):
+def forward_body(layer, share, x_own, weights, tables, kept, scratch, sems):
+    w_mix, w_gate, w_out, w_down, w_gains = weights
+    cosine, sine, place_col, place_row = tables
+    normed_o, q_o, k_o, v_o, context_o, log_o, middle_o, normed_two_o, both_o, result_o = kept
+    (x_v, normed_v, q_v, k_v, v_v, context_v, log_v, middle_v, two_v, both_v, hidden_v, result_v,
+     mix_v, gate_v, out_v, down_v, gains_v, part_v, land_a, land_b, total_v) = scratch
+    local, save, send_a, recv_a, send_b, recv_b, send_c, recv_c, send_d, recv_d = sems
     c = lax.axis_index("ctx")
     f = lax.axis_index("fsdp")
     rows = x_own.shape[0]
@@ -312,16 +510,14 @@
     loads = Loads(local)
     saves = Loads(save)
     load_x = loads.start(x_own, x_v.at[own_rows])
-    load_gains = loads.start(w_gains.at[layer], gains_v)
-    load_mix = loads.start(w_mix.at[layer], mix_v)
     out_v[...] = jnp.zeros_like(out_v)
-    greet()
-    load_x.wait()
-    load_gains.wait()
-    load_mix.wait()
-    load_out = loads.start(w_out.at[layer], out_v.at[pl.ds(0, HEAD)])
-    load_gate = loads.start(w_gate.at[layer], gate_v)
-    load_down = loads.start(w_down.at[layer], down_v)
+
+    def load_first():
+        return [
+            loads.start(w_gains.at[layer], gains_v),
+            loads.start(w_mix.at[layer], mix_v),
+            loads.start(w_out.at[layer], out_v.at[pl.ds(0, HEAD)]),
+        ]
 
     def project(d):
         here = plane_rows(d, rows)
@@ -337,10 +533,32 @@
         k_v[here, :] = (k * cos + turn(k) * sin).astype(BF)
         v_v[here, :] = mixed[:, 2 * LANES :].astype(BF)
 
-    gather_rows(x_v, rows, send_a, recv_a, project)
+    if share is None:
+        first = load_first()
+        load_gate = loads.start(w_gate.at[layer], gate_v)
+        load_down = loads.start(w_down.at[layer], down_v)
+        greet()
+        load_x.wait()
+        for one in first:
+            one.wait()
+        gather_rows(x_v, rows, send_a, recv_a, project)
+    else:
+        share.load()
+        share.keep_gate()
+        greet_more(share.greeted())
+        load_x.wait()
+        share.send_mix()
+        gather_rows(x_v, rows, send_a, recv_a, started=share.cross_mix)
+        share.send_gate()
+        share.mix_there()
+        first = load_first()
+        for one in first:
+            one.wait()
+        for d in range(4):
+            project(d)
+        share.cross_gate()
     for src, dst in ((normed_v, normed_o), (q_v, q_o), (k_v, k_o), (v_v, v_o)):
         saves.start(src, dst)
-    load_out.wait()
     scale = HEAD ** (-0.5)
 
     def attention(d):
@@ -363,7 +581,13 @@
     middle_v[...] = middle
     saves.start(middle_v, middle_o)
     two_v[own_rows, :] = (middle * mean_square(middle) * gains_v[1:2, :].astype(F32)).astype(BF)
-    load_gate.wait()
+
+    def gate_ready():
+        if share is None:
+            load_gate.wait()
+        else:
+            share.gate_there()
+            loads.start(w_gate.at[layer], gate_v).wait()
 
     def feed(d):
         here = plane_rows(d, rows)
@@ -372,10 +596,14 @@
         gate = both[:, :units]
         hidden_v[here, :] = (gate * jax.nn.sigmoid(gate) * both[:, units:]).astype(BF)
 
-    gather_rows(two_v, rows, send_c, recv_c, feed)
+    gather_rows(two_v, rows, send_c, recv_c, feed, gate_ready)
     saves.start(two_v, normed_two_o)
     saves.start(both_v, both_o)
-    load_down.wait()
+    if share is None:
+        load_down.wait()
+    else:
+        share.down_there()
+        loads.start(w_down.at[layer], down_v).wait()
 
     def lower(d):
         here = plane_rows(d, rows)
@@ -386,20 +614,45 @@
     saves.start(result_v, result_o)
     for one in saves.copies:
         one.wait()
-
-
-def backward_kernel(layer, grad_own, w_mix, w_gate, w_out, w_down, w_gains, cosine, sine, place_col, place_row,
-                    x_own, normed, q, k, v, context, log, middle, normed_two, both,
-                    start_o, low_o, mix_grad_o, gate_grad_o, out_grad_o, down_grad_o, gain_grad_o,
-                    grad_v, x_v, normed_v, q_v, k_v, v_v, context_v, log_v, middle_v, two_v, both_v, both_grad_v, hidden_v,
-                    low_v, mixed_v, key_grad_v, value_grad_v, start_v, start_low_v,
-                    mix_grad_v, gate_grad_v, out_grad_v, down_grad_v, gain_grad_v,
-                    mix_v, gate_v, out_v, down_v, gains_v, part_v, land_a, land_b, total_v, local, save,
-                    send_a, recv_a, send_b, recv_b, send_c, recv_c, send_d, recv_d):
+    if share is not None:
+        share.finish()
+
+
+def forward_kernel(layer, *refs):
+    x_own, *refs = refs
+    weights, refs = refs[:5], refs[5:]
+    tables, refs = refs[:4], refs[4:]
+    kept, refs = refs[:10], refs[10:]
+    scratch, sems = refs[:21], refs[21:]
+    forward_body(layer, None, x_own, weights, tables, kept, scratch, sems)
+
+
+def forward_share_kernel(*refs):
+    x_own, *refs = refs
+    sources, refs = refs[:5], refs[5:]
+    tables, refs = refs[:4], refs[4:]
+    kept, refs = refs[:10], refs[10:]
+    weights, refs = refs[:5], refs[5:]
+    scratch, refs = refs[:21], refs[21:]
+    packing, refs = refs[:2], refs[2:]
+    sems, share_sems = refs[:10], refs[10:]
+    share = Share(sources, weights, packing, share_sems)
+    forward_body(0, share, x_own, weights, tables, kept, scratch, sems)
+
+
+def backward_body(layer, grad_own, weights, tables, saved, outs, scratch, sems, returning):
+    w_mix, w_gate, w_out, w_down, w_gains = weights
+    cosine, sine, place_col, place_row = tables
+    x_own, normed, q, k, v, context, log, middle, normed_two, both = saved
+    (grad_v, x_v, normed_v, q_v, k_v, v_v, context_v, log_v, middle_v, two_v, both_v, both_grad_v, hidden_v,
+     low_v, mixed_v, kv_land, kv_v, key_grad_v, value_grad_v, start_v, start_low_v,
+     mix_grad_v, gate_grad_v, out_grad_v, down_grad_v, gain_grad_v,
+     mix_v, gate_v, out_v, down_v, gains_v, part_v, land_a, land_b, total_v) = scratch
+    local, save, pair_sems, send_a, recv_a, send_b, recv_b, send_c, recv_c, send_d, recv_d = sems
     c = lax.axis_index("ctx")
     f = lax.axis_index("fsdp")
+    odd = lax.rem(c, 2)
     rows = grad_own.shape[0]
-    length, width = grad_v.shape
     units = down_v.shape[0]
     own_rows = pl.ds(pl.multiple_of((c * 4 + f) * rows, rows), rows)
     loads = Loads(local)
@@ -411,7 +664,12 @@
     out_v[...] = jnp.zeros_like(out_v)
     key_grad_v[...] = jnp.zeros_like(key_grad_v)
     value_grad_v[...] = jnp.zeros_like(value_grad_v)
-    greet()
+    gain_grad_v[...] = jnp.zeros_like(gain_grad_v)
+    if returning is None:
+        greet()
+    else:
+        peers = [{"fsdp": lax.rem(f + k, 4)} for k in range(1, 4)]
+        greet_more(peers + [{"section": 1 - lax.axis_index("section")}, {"ctx": lax.rem(c + 2, 4)}])
     load_grad.wait()
     later = [
         loads.start(src, dst)
@@ -423,6 +681,9 @@
     ]
     load_down.wait()
     load_both.wait()
+    if returning is not None:
+        begin_feed, begin_mix, feed_steps, mix_steps, sum_gains, along_line = returning
+        steps = feed_steps()
 
     def feed(d):
         here = plane_rows(d, rows)
@@ -449,8 +710,11 @@
             gate_grad_v[part] = kernel_dot_tn(
                 two_v[...], both_grad_v[:, part * units : (part + 1) * units]
             ).astype(BF)
-        saves.start(down_grad_v, down_grad_o)
-        saves.start(gate_grad_v, gate_grad_o)
+        if returning is None:
+            saves.start(down_grad_v, outs[4])
+            saves.start(gate_grad_v, outs[2])
+        else:
+            begin_feed()
 
     scatter_sum(part_v, total_v, land_a, send_b, recv_b, spread, feed_weights)
     for one in later[1:]:
@@ -463,7 +727,6 @@
         gain_grad_v[row : row + 1, :] = jnp.sum(error * value * factor, axis=0, keepdims=True)
         return factor * shaped - value * (factor * factor * factor) * common
 
-    gain_grad_v[...] = jnp.zeros_like(gain_grad_v)
     middle_grad = norm_grads(total_v[...], middle_v[...], gains_v[1:2, :].astype(F32), 1)
     middle_grad = middle_grad + grad_v[own_rows, :].astype(F32)
     middle_v[...] = middle_grad
@@ -490,6 +753,16 @@
     key_grad = key_grad_v[...] * scale
     mixed_v[:, LANES : 2 * LANES] = (key_grad * cosine[...] - turn(key_grad) * sine[...]).astype(BF)
     mixed_v[:, 2 * LANES :] = value_grad_v[...].astype(BF)
+    pair = {"ctx": c + 1 - 2 * odd}
+
+    def pair_copy(part):
+        return pltpu.make_async_remote_copy(
+            mixed_v.at[:, pl.ds(part * LANES, LANES)], kv_land, pair_sems.at[0], pair_sems.at[1],
+            device_id=pair, device_id_type=MESH,
+        )
+
+    pl.when(odd == 0)(pair_copy(2).start)
+    pl.when(odd == 1)(pair_copy(1).start)
 
     def spread_two(d):
         here = plane_rows(d, rows)
@@ -497,22 +770,82 @@
 
     def mix_weights():
         out_grad_v[...] = kernel_dot_tn(context_v[...], low_v[...])[:HEAD].astype(BF)
-        for part in range(3):
-            mix_grad_v[part] = kernel_dot_tn(
-                normed_v[...], mixed_v[:, part * LANES : (part + 1) * LANES]
-            ).astype(BF)
-        saves.start(out_grad_v, out_grad_o)
-        saves.start(mix_grad_v, mix_grad_o)
-
-    scatter_sum(part_v, total_v, land_b, send_d, recv_d, spread_two, mix_weights)
+        mix_grad_v[0] = kernel_dot_tn(normed_v[...], mixed_v[:, :LANES]).astype(BF)
+        pair_copy(1).wait_recv()
+        mine = jnp.where(odd == 0, mixed_v[:, LANES : 2 * LANES].astype(F32), mixed_v[:, 2 * LANES :].astype(F32))
+        kv_v[...] = (mine + kv_land[...].astype(F32)).astype(BF)
+        mix_grad_v[1] = kernel_dot_tn(normed_v[...], kv_v[...]).astype(BF)
+        if returning is None:
+            saves.start(out_grad_v, outs[3])
+            saves.start(mix_grad_v, outs[1])
+        else:
+            begin_mix()
+
+    def next_step():
+        if returning is not None:
+            next(steps)()
+
+    scatter_sum(part_v, total_v, land_b, send_d, recv_d, spread_two, mix_weights, next_step)
     start_grad = norm_grads(total_v[...], x_v[...].astype(F32), gains_v[0:1, :].astype(F32), 0) + middle_v[...]
     start_v[...] = start_grad
-    start_low_v[...] = start_grad.astype(BF)
-    saves.start(start_v, start_o)
-    saves.start(start_low_v, low_o)
-    saves.start(gain_grad_v, gain_grad_o)
+    saves.start(start_v, outs[0])
+    if returning is None:
+        start_low_v[...] = start_grad.astype(BF)
+        saves.start(start_low_v, outs[6])
+        saves.start(gain_grad_v, outs[5])
+    else:
+        for step in steps:
+            step()
+        for step in mix_steps():
+            step()
+        sum_gains(gain_grad_v)
+        along_line()
+    pair_copy(1).wait_send()
     for one in saves.copies:
         one.wait()
+
+
+SAVED = 10
+BACK_SCRATCH = 35
+
+
+def backward_kernel(layer, *refs):
+    grad_own, *refs = refs
+    weights, refs = refs[:5], refs[5:]
+    tables, refs = refs[:4], refs[4:]
+    saved, refs = refs[:SAVED], refs[SAVED:]
+    outs, refs = refs[:7], refs[7:]
+    scratch, sems = refs[:BACK_SCRATCH], refs[BACK_SCRATCH:]
+    backward_body(layer, grad_own, weights, tables, saved, outs, scratch, sems, None)
+
+
+def backward_return_kernel(*refs):
+    grad_own, *refs = refs
+    weights, refs = refs[:5], refs[5:]
+    tables, refs = refs[:4], refs[4:]
+    saved, refs = refs[:SAVED], refs[SAVED:]
+    (mix_old, gate_old, out_old, down_old, gain_old), refs = refs[:5], refs[5:]
+    outs, refs = refs[:1], refs[1:]
+    finals, refs = refs[:5], refs[5:]
+    scratch, refs = refs[:BACK_SCRATCH], refs[BACK_SCRATCH:]
+    own, refs = refs[:10], refs[10:]
+    sems, return_sems = refs[:11], refs[11:]
+    mix_new, gate_new, out_new, down_new, gain_new = scratch[21:26]
+    gain_v = own[8]
+    *steps, sum_gains, along_line = returner(
+        tuple(finals) + tuple(own), return_sems,
+        gate_new, down_new, mix_new, out_new, gate_old, down_old, mix_old, out_old,
+    )
+
+    def all_gains(gain_grad_v):
+        gain_v[0] = jnp.zeros(gain_v.shape[1:], F32)
+        gain_v[0, 0:2, :] = gain_grad_v[...]
+        gain_v[0, 2:4, :] = gain_old[...]
+        sum_gains()
+
+    backward_body(
+        0, grad_own, weights, tables, saved, outs, scratch, sems, tuple(steps) + (all_gains, along_line)
+    )
 
 
 def link_sems():
@@ -520,301 +853,144 @@
     return [dma((GATHER_SENDS,)), dma((GATHER_RECVS,)), dma((SCATTER_SENDS,)), dma((SCATTER_RECVS,))] * 2
 
 
-def forward_call(layer, x_own, shared, tables, places):
+def low(*shape):
+    return (shape, BF)
+
+
+def full(*shape):
+    return (shape, F32)
+
+
+def shapes(specs):
+    return [jax.ShapeDtypeStruct(*one) for one in specs]
+
+
+def rooms(specs):
+    return [pltpu.VMEM(*one) for one in specs]
+
+
+def signals(*counts):
+    return [pltpu.SemaphoreType.DMA((count,)) for count in counts]
+
+
+def forward_call(layer, x_own, weights, tables):
     rows, width = x_own.shape
     length = 16 * rows
-    units = shared[3].shape[1]
+    sharing = layer == 0
+    if sharing:
+        depth = weights[0].shape[1]
+        units = weights[2].shape[2] // 32
+        packing = [low(depth, weights[0].shape[2]), low(depth, 32 * LANES)]
+    else:
+        units = weights[3].shape[1]
+        packing = []
     anywhere = pl.BlockSpec(memory_space=pl.ANY)
     inside = pl.BlockSpec(memory_space=pltpu.VMEM)
-
-    def low(*shape):
-        return (shape, BF)
-
-    def full(*shape):
-        return (shape, F32)
-
     kept = [low(length, width)] + [low(length, LANES)] * 4 + [
         full(length, LANES), full(rows, width), low(length, width), full(length, 2 * units), low(rows, width)]
-    inner = [low(length, width), low(length, width)] + [low(length, LANES)] * 4 + [
+    shared = [low(2, width, 3 * LANES), low(2, width, 2 * units), low(2, HEAD, width), low(2, units, width), low(2, 16, width)]
+    scratch = [low(length, width), low(length, width)] + [low(length, LANES)] * 4 + [
         full(length, LANES), full(rows, width), low(length, width), full(length, 2 * units), low(length, units),
         low(rows, width), low(width, 3 * LANES), low(width, 2 * units), low(LANES, width), low(units, width),
         low(16, width), low(length, width), low(18, rows, width), low(18, rows, width), full(rows, width)]
+    outs = kept + shared if sharing else kept
     return pl.pallas_call(
-        functools.partial(forward_kernel, layer),
-        out_shape=[jax.ShapeDtypeStruct(*one) for one in kept],
+        forward_share_kernel if sharing else functools.partial(forward_kernel, layer),
+        out_shape=shapes(outs),
         in_specs=[anywhere] * 6 + [inside] * 4,
-        out_specs=[anywhere] * len(kept),
-        scratch_shapes=[pltpu.VMEM(*one) for one in inner]
-        + [pltpu.SemaphoreType.DMA((6,)), pltpu.SemaphoreType.DMA((10,))] + link_sems(),
+        out_specs=[anywhere] * len(outs),
+        scratch_shapes=rooms(scratch + packing) + signals(6, 10) + link_sems() + (signals(9, 27, 26) if sharing else []),
         compiler_params=pltpu.CompilerParams(
-            collective_id=4 + layer, has_side_effects=True, vmem_limit_bytes=60 << 20),
-    )(x_own, *shared, *tables, *places)
-
-
-def backward_call(layer, grad_own, shared, tables, places, x_own, kept):
+            collective_id=layer, has_side_effects=True, vmem_limit_bytes=60 << 20),
+    )(x_own, *weights, *tables)
+
+
+def backward_call(layer, grad_own, weights, tables, saved, old=()):
     rows, width = grad_own.shape
     length = 16 * rows
-    units = shared[3].shape[1]
+    units = weights[3].shape[1]
+    depth = width // 4
+    returning = layer == 0
     anywhere = pl.BlockSpec(memory_space=pl.ANY)
     inside = pl.BlockSpec(memory_space=pltpu.VMEM)
-
-    def low(*shape):
-        return (shape, BF)
-
-    def full(*shape):
-        return (shape, F32)
-
-    grads = [low(3, width, LANES), low(2, width, units), low(HEAD, width), low(units, width), full(2, width)]
-    outs = [full(rows, width), low(rows, width)] + grads
-    inner = [low(length, width), low(rows, width), low(length, width)] + [low(length, LANES)] * 4 + [
+    grads = [low(2, width, LANES), low(2, width, units), low(HEAD, width), low(units, width), full(2, width)]
+    scratch = [low(length, width), low(rows, width), low(length, width)] + [low(length, LANES)] * 4 + [
         full(length, LANES), full(rows, width), low(length, width), full(length, 2 * units), low(length, 2 * units),
-        low(length, units), low(length, width), low(length, 3 * LANES), full(length, LANES), full(length, LANES),
+        low(length, units), low(length, width), low(length, 3 * LANES), low(length, LANES), low(length, LANES),
+        full(length, LANES), full(length, LANES),
         full(rows, width), low(rows, width)] + grads + [
         low(width, 3 * LANES), low(width, 2 * units), low(LANES, width), low(units, width),
         low(16, width), low(length, width), low(18, rows, width), low(18, rows, width), full(rows, width)]
+    sems = signals(16, 7, 2) + link_sems()
+    if returning:
+        outs = [full(rows, width), low(2, depth, 16 * LANES), low(2, depth, 16 * units), low(4 * HEAD, width),
+                low(4 * units, width), full(8, width)]
+        out_specs = [anywhere] * 5 + [inside]
+        scratch += grads[:4] + grads[:4] + [full(5, 8, width), full(5, 8, width)]
+        sems += signals(5, 23, 23, 50, 40)
+    else:
+        outs = [full(rows, width)] + grads + [low(rows, width)]
+        out_specs = [anywhere] * len(outs)
     return pl.pallas_call(
-        functools.partial(backward_kernel, layer),
-        out_shape=[jax.ShapeDtypeStruct(*one) for one in outs],
-        in_specs=[anywhere] * 6 + [inside] * 4 + [anywhere] * 10,
-        out_specs=[anywhere] * len(outs),
-        scratch_shapes=[pltpu.VMEM(*one) for one in inner]
-        + [pltpu.SemaphoreType.DMA((16,)), pltpu.SemaphoreType.DMA((7,))] + link_sems(),
+        backward_return_kernel if returning else functools.partial(backward_kernel, layer),
+        out_shape=shapes(outs),
+        in_specs=[anywhere] * 6 + [inside] * 4 + [anywhere] * SAVED + ([anywhere] * 4 + [inside] if returning else []),
+        out_specs=out_specs,
+        scratch_shapes=rooms(scratch) + sems,
         compiler_params=pltpu.CompilerParams(
-            collective_id=6 + layer, has_side_effects=True, vmem_limit_bytes=60 << 20),
-    )(grad_own, *shared, *tables, *places, x_own, *kept)
-
-
-def greet_all(peers):
-    barrier = pltpu.get_barrier_semaphore()
-    for peer in peers:
-        pl.semaphore_signal(barrier, inc=1, device_id=peer, device_id_type=MESH)
-    pl.semaphore_wait(barrier, len(peers))
-
-
-def head_choice(value_part):
-    source = lax.broadcasted_iota(jnp.int32, (4 * HEAD, 4 * LANES), 0)
-    lane = lax.broadcasted_iota(jnp.int32, (4 * HEAD, 4 * LANES), 1)
-    head = lane // LANES
-    inside = lane - head * LANES
-    if value_part:
-        wanted = jnp.where(inside < HEAD, head * HEAD + inside, -1)
-    else:
-        half = inside // SPAN
-        place = inside - half * SPAN
-        wanted = jnp.where(place < HEAD // 2, head * HEAD + half * (HEAD // 2) + place, -1)
-    return jnp.where(source == wanted, 1.0, 0.0).astype(BF)
-
-
-def share_kernel(mix, out, gate_up, down, gains, w_mix, w_gate, w_out, w_down, w_gains,
-                 mix_v, heads_v, local, send, recv):
+            collective_id=2 + layer, has_side_effects=True, vmem_limit_bytes=60 << 20),
+    )(grad_own, *weights, *tables, *saved, *old)
+
+
+def returner(refs, sems, gate_new, down_new, mix_new, out_new, gate_old, down_old, mix_old, out_old):
+    (mix_out, gate_out, out_out, down_out, gain_out,
+     mix_v, gate_v, out_v, down_v, mix_x, gate_x, out_x, down_x, gain_v, gain_x) = refs
+    local, send, recv, line_send, line_recv = sems
     s = lax.axis_index("section")
     c = lax.axis_index("ctx")
     f = lax.axis_index("fsdp")
-    depth = mix.shape[1]
-    units = w_down.shape[1]
-    hidden_units = gate_up.shape[2] // 2
-    other = 1 - s
-    peers = [lax.rem(f + k, 4) for k in range(1, 4)]
-    greet_all([{"fsdp": peer} for peer in peers] + [{"section": other}]
-              + [{"section": other, "fsdp": peer} for peer in peers])
-    load = pltpu.make_async_copy(mix.at[0], mix_v, local.at[0])
-    load.start()
-    rows = pl.ds(pl.multiple_of(f * depth, depth), depth)
-    pending = []
+    other = {"section": 1 - s}
+    units = down_v.shape[0]
+    depth = mix_out.shape[1]
+    inner = jnp.logical_and(c > 0, c < 3)
+    above = jnp.minimum(c + 1, 3)
+    below = jnp.maximum(c - 1, 0)
 
     def copy(src, dst, slot, arrival, peer):
         return pltpu.make_async_remote_copy(
             src, dst, send.at[slot], recv.at[arrival], device_id=peer, device_id_type=MESH
         )
 
-    def go(src, dst, slot, arrival, peer):
-        one = copy(src, dst, slot, arrival, peer)
-        one.start()
-        pending.append(one)
-
-    mine = w_gains.at[s, :, pl.ds(pl.multiple_of(f * depth, depth), depth)]
-    for k, peer in enumerate(peers):
-        go(gains, mine, 20 + k, 16 + 4 * s + f, {"fsdp": peer})
-        go(gains, mine, 23 + k, 16 + 4 * s + f, {"section": other, "fsdp": peer})
-    go(gains, mine, 26, 16 + 4 * s + f, {"section": other})
-    keep_gains = pltpu.make_async_copy(gains, mine, local.at[1])
-    keep_gains.start()
-
-    load.wait()
-    for g in range(8):
-        choice = head_choice(g >= 6)
-        heads_v[:, g * 512 : (g + 1) * 512] = jnp.dot(
-            mix_v[:, g * 384 : (g + 1) * 384], choice, preferred_element_type=F32
-        ).astype(BF)
-
-    def lanes(peer, part):
-        head = peer * 4 + c
-        start = head * LANES if part == 0 else (16 + 8 * (part - 1) + head // 2) * LANES
-        return heads_v.at[:, pl.ds(pl.multiple_of(start, LANES), LANES)]
-
-    def put(peer, part):
-        return w_mix.at[s, rows, pl.ds(part * LANES, LANES)]
-
-    for k, peer in enumerate(peers):
-        for part in range(3):
-            copy(lanes(peer, part), put(peer, part), k, f, {"fsdp": peer}).start()
-    own_mix = [pltpu.make_async_copy(lanes(f, part), put(f, part), local.at[2 + part]) for part in range(3)]
-    for one in own_mix:
-        one.start()
-
-    def gate_piece(peer, part):
-        start = pl.multiple_of(part * hidden_units + (peer * 4 + c) * units, units)
-        return gate_up.at[0, :, pl.ds(start, units)]
-
-    def gate_put(part):
-        return w_gate.at[s, rows, pl.ds(part * units, units)]
-
-    for k, peer in enumerate(peers):
-        for part in range(2):
-            copy(gate_piece(peer, part), gate_put(part), 3 + k, 4 + f, {"fsdp": peer}).start()
-    own_gate = [pltpu.make_async_copy(gate_piece(f, part), gate_put(part), local.at[5 + part]) for part in range(2)]
-    for one in own_gate:
-        one.start()
-    out_rows = out.at[0, pl.ds(pl.multiple_of(c * HEAD, HEAD), HEAD)]
-    down_rows = down.at[0, pl.ds(pl.multiple_of(c * units, units), units)]
-    own_out = pltpu.make_async_copy(out_rows, w_out.at[s], local.at[7])
-    own_out.start()
-    own_down = pltpu.make_async_copy(down_rows, w_down.at[s], local.at[8])
-    own_down.start()
-
-    def slab(ref, origin):
-        return ref.at[s, pl.ds(pl.multiple_of(origin * depth, depth), depth)]
-
-    for one in own_mix:
-        one.wait()
-    go(slab(w_mix, f), slab(w_mix, f), 6, 8 + f, {"section": other})
-    for k in range(3):
-        origin = lax.rem(f + 3 - k, 4)
-        copy(slab(w_mix, origin), slab(w_mix, origin), 0, origin, {"fsdp": origin}).wait_recv()
-        go(slab(w_mix, origin), slab(w_mix, origin), 7 + k, 8 + origin, {"section": other})
-    go(out_rows, w_out.at[s], 10, 24, {"section": other})
-    for one in own_gate:
-        one.wait()
-    go(slab(w_gate, f), slab(w_gate, f), 11, 12 + f, {"section": other})
-    for k in range(3):
-        origin = lax.rem(f + 3 - k, 4)
-        copy(slab(w_gate, origin), slab(w_gate, origin), 0, 4 + origin, {"fsdp": origin}).wait_recv()
-        go(slab(w_gate, origin), slab(w_gate, origin), 12 + k, 12 + origin, {"section": other})
-    go(down_rows, w_down.at[s], 15, 25, {"section": other})
-
-    def from_there(ref, arrival):
-        copy(ref, ref, 0, arrival, {"section": other}).wait_recv()
-
-    for origin in range(4):
-        theirs = pl.ds(origin * depth, depth)
-        from_there(w_mix.at[other, theirs], 8 + origin)
-        from_there(w_gate.at[other, theirs], 12 + origin)
-    from_there(w_out.at[other], 24)
-    from_there(w_down.at[other], 25)
-    for origin in range(4):
-        from_there(w_gains.at[other, :, pl.ds(origin * depth, depth)], 16 + 4 * other + origin)
-    for k in range(3):
-        origin = lax.rem(f + 3 - k, 4)
-        from_there(w_gains.at[s, :, pl.ds(pl.multiple_of(origin * depth, depth), depth)], 16 + 4 * s + origin)
-    keep_gains.wait()
-    own_out.wait()
-    own_down.wait()
-    for k, peer in enumerate(peers):
-        copy(slab(w_mix, f), slab(w_mix, f), k, 0, {"fsdp": peer}).wait_send()
-        copy(slab(w_gate, f), slab(w_gate, f), 3 + k, 0, {"fsdp": peer}).wait_send()
-    for one in pending:
-        one.wait_send()
-
-
-def share_call(mix, out, gate_up, down, gains):
-    depth = mix.shape[1]
-    width = 4 * depth
-    units = gate_up.shape[2] // 32
-    anywhere = pl.BlockSpec(memory_space=pl.ANY)
-    return pl.pallas_call(
-        share_kernel,
-        out_shape=(
-            jax.ShapeDtypeStruct((2, width, 3 * LANES), BF),
-            jax.ShapeDtypeStruct((2, width, 2 * units), BF),
-            jax.ShapeDtypeStruct((2, HEAD, width), BF),
-            jax.ShapeDtypeStruct((2, units, width), BF),
-            jax.ShapeDtypeStruct((2, 16, width), BF),
-        ),
-        in_specs=[anywhere] * 5,
-        out_specs=(anywhere,) * 5,
-        scratch_shapes=[
-            pltpu.VMEM((depth, mix.shape[2]), BF),
-            pltpu.VMEM((depth, 32 * LANES), BF),
-            pltpu.SemaphoreType.DMA((9,)),
-            pltpu.SemaphoreType.DMA((27,)),
-            pltpu.SemaphoreType.DMA((26,)),
-        ],
-        compiler_params=pltpu.CompilerParams(collective_id=2, has_side_effects=True, vmem_limit_bytes=48 << 20),
-    )(mix, out, gate_up, down, gains)
-
-
-def return_kernel(mix_0, mix_1, gate_0, gate_1, out_0, out_1, down_0, down_1, gains,
-                  mix_out, gate_out, out_out, down_out, gain_out,
-                  mix_v, gate_v, out_v, down_v, mix_x, gate_x, out_x, down_x, gain_v, gain_x,
-                  local, send, recv, line_send, line_recv):
-    s = lax.axis_index("section")
-    c = lax.axis_index("ctx")
-    f = lax.axis_index("fsdp")
-    other = 1 - s
-    units = down_0.shape[0]
-    depth = mix_out.shape[1]
-    inner = jnp.logical_and(c > 0, c < 3)
-    peers = [lax.rem(f + k, 4) for k in range(1, 4)]
-    pair = c + 1 - 2 * lax.rem(c, 2)
-    far = lax.rem(c + 2, 4)
-    barrier = pltpu.get_barrier_semaphore()
-    for peer in [{"fsdp": peer} for peer in peers] + [{"section": other}, {"ctx": pair}, {"ctx": far}]:
-        pl.semaphore_signal(barrier, inc=1, device_id=peer, device_id_type=MESH)
-
-    @pl.when(inner)
-    def _():
-        pl.semaphore_signal(barrier, inc=1, device_id={"ctx": 3 - c}, device_id_type=MESH)
-        pl.semaphore_wait(barrier, 7)
-
-    @pl.when(jnp.logical_not(inner))
-    def _():
-        pl.semaphore_wait(barrier, 6)
-
-    def copy(src, dst, slot, arrival, peer):
-        return pltpu.make_async_remote_copy(
-            src, dst, send.at[slot], recv.at[arrival], device_id=peer, device_id_type=MESH
-        )
-
     def rows_of(k):
         return pl.ds(k * depth, depth)
 
-    def away(mix, gate, out, down):
-        copy(down, down_x, 8, 8, {"section": other}).start()
+    def cross_feed(gate_away, down_away, gate_home, down_home):
+        copy(down_away, down_x, 8, 8, other).start()
         for k in range(4):
-            copy(gate.at[:, rows_of(k)], gate_x.at[:, rows_of(k)], k, k, {"section": other}).start()
-        copy(out, out_x, 9, 9, {"section": other}).start()
+            copy(gate_away.at[:, rows_of(k)], gate_x.at[:, rows_of(k)], k, k, other).start()
+        pltpu.make_async_copy(down_home, down_v, local.at[0]).start()
+        pltpu.make_async_copy(gate_home, gate_v, local.at[1]).start()
+
+    def cross_mix(mix_away, out_away, mix_home, out_home):
+        copy(out_away, out_x, 9, 9, other).start()
         for k in range(4):
-            copy(mix.at[:, rows_of(k)], mix_x.at[:, rows_of(k)], 4 + k, 4 + k, {"section": other}).start()
-
-    def home(mix, gate, out, down):
-        for k, (src, dst) in enumerate(((down, down_v), (gate, gate_v), (out, out_v), (mix, mix_v))):
-            pltpu.make_async_copy(src, dst, local.at[k]).start()
-
-    @pl.when(s == 0)
-    def _():
-        away(mix_1, gate_1, out_1, down_1)
-        home(mix_0, gate_0, out_0, down_0)
-
-    @pl.when(s == 1)
-    def _():
-        away(mix_0, gate_0, out_0, down_0)
-        home(mix_1, gate_1, out_1, down_1)
+            copy(mix_away.at[:, rows_of(k)], mix_x.at[:, rows_of(k)], 4 + k, 4 + k, other).start()
+        pltpu.make_async_copy(out_home, out_v, local.at[2]).start()
+        pltpu.make_async_copy(mix_home, mix_v, local.at[3]).start()
+
+    def begin_feed():
+        pl.when(s == 0)(lambda: cross_feed(gate_old, down_old, gate_new, down_new))
+        pl.when(s == 1)(lambda: cross_feed(gate_new, down_new, gate_old, down_old))
+
+    def begin_mix():
+        pl.when(s == 0)(lambda: cross_mix(mix_old, out_old, mix_new, out_new))
+        pl.when(s == 1)(lambda: cross_mix(mix_new, out_new, mix_old, out_old))
 
     def home_wait(k, dst):
         pltpu.make_async_copy(dst, dst, local.at[k]).wait()
 
     def arrived(ref, arrival):
-        copy(ref, ref, 0, arrival, {"section": other}).wait_recv()
+        copy(ref, ref, 0, arrival, other).wait_recv()
 
     def gate_at(cc, ff):
         return gate_out.at[:, :, pl.ds(pl.multiple_of((ff * 4 + cc) * units, units), units)]
@@ -828,139 +1004,180 @@
     def down_at(cc, ff):
         return down_out.at[pl.ds(pl.multiple_of(cc * units, units), units)]
 
-    items = [(down_at, f)] + [(gate_at, lax.rem(f + k, 4)) for k in (0, 3, 2, 1)] + [(out_at, f)] + [
-        (mix_at, lax.rem(f + k, 4)) for k in (0, 3, 2, 1)
-    ]
-
-    def line(place, origin, index, cc, slot, target):
-        key = cc * 10 + index
+    origins = [lax.rem(f + k, 4) for k in (0, 3, 2, 1)]
+    items = [(down_at, f)] + [(gate_at, one) for one in origins] + [(out_at, f)] + [(mix_at, one) for one in origins]
+
+    def line(index, cc, slot, target):
+        place, origin = items[index]
         return pltpu.make_async_remote_copy(
-            place(cc, origin), place(cc, origin), line_send.at[slot], line_recv.at[key],
+            place(cc, origin), place(cc, origin), line_send.at[slot], line_recv.at[cc * 10 + index],
             device_id={"ctx": target}, device_id_type=MESH,
         )
 
-    above = jnp.minimum(c + 1, 3)
-    below = jnp.maximum(c - 1, 0)
-
     def start_line(index):
-        place, origin = items[index]
-        pl.when(c < 3)(line(place, origin, index, c, index, above).start)
-        pl.when(c > 0)(line(place, origin, index, c, 10 + index, below).start)
+        pl.when(c < 3)(line(index, c, index, above).start)
+        pl.when(c > 0)(line(index, c, 10 + index, below).start)
 
     def fold(mine, theirs, arrival):
         arrived(theirs, arrival)
         mine[...] = (mine[...].astype(F32) + theirs[...].astype(F32)).astype(BF)
 
-    def keep(src, dst, k):
-        one = pltpu.make_async_copy(src, dst, local.at[k])
+    def keep(src, dst):
+        one = pltpu.make_async_copy(src, dst, local.at[4])
         one.start()
         one.wait()
 
-    home_wait(0, down_v)
-    fold(down_v, down_x, 8)
-    keep(down_v, down_at(c, f), 4)
-    start_line(0)
-
-    def to_owners(mine, theirs, place, arrival_x, arrival_y, slot):
-        for k in (1, 2, 3, 0):
-            owner = lax.rem(f + k, 4)
-            rows = pl.ds(pl.multiple_of(owner * depth, depth), depth)
-            fold(mine.at[:, rows], theirs.at[:, rows], arrival_x + owner)
+    def whole_item(k, mine, theirs, arrival, place, index):
+        home_wait(k, mine)
+        fold(mine, theirs, arrival)
+        keep(mine, place(c, f))
+        start_line(index)
+
+    def to_owner(k, mine, theirs, place, arrival_x, arrival_y, slot, index):
+        owner = lax.rem(f + k, 4)
+        rows = pl.ds(pl.multiple_of(owner * depth, depth), depth)
+        fold(mine.at[:, rows], theirs.at[:, rows], arrival_x + owner)
+        if k:
+            copy(mine.at[:, rows], place(c, f), slot + k, arrival_y + f, {"fsdp": owner}).start()
+        else:
+            keep(mine.at[:, rows], place(c, f))
+            start_line(index)
+
+    def from_owner(k, place, arrival, index):
+        arrived(place(c, origins[k]), arrival + origins[k])
+        start_line(index)
+
+    def feed_steps():
+        yield lambda: whole_item(0, down_v, down_x, 8, down_at, 0)
+
+        def first():
+            home_wait(1, gate_v)
+            to_owner(1, gate_v, gate_x, gate_at, 0, 10, 10, 1)
+
+        yield first
+        for k in (2, 3, 0):
+            yield functools.partial(to_owner, k, gate_v, gate_x, gate_at, 0, 10, 10, 1)
+        for k in range(1, 4):
+            yield functools.partial(from_owner, k, gate_at, 10, 1 + k)
+
+    def mix_steps():
+        yield lambda: whole_item(2, out_v, out_x, 9, out_at, 5)
+
+        def first():
+            home_wait(3, mix_v)
+            to_owner(1, mix_v, mix_x, mix_at, 4, 14, 14, 6)
+
+        yield first
+        for k in (2, 3, 0):
+            yield functools.partial(to_owner, k, mix_v, mix_x, mix_at, 4, 14, 14, 6)
+        for k in range(1, 4):
+            yield functools.partial(from_owner, k, mix_at, 14, 6 + k)
+
+    def sum_gains():
+        targets = [other, {"fsdp": f + 1 - 2 * lax.rem(f, 2)}, {"fsdp": f + 2 - 4 * (f // 2)},
+                   {"ctx": c + 1 - 2 * lax.rem(c, 2)}, {"ctx": lax.rem(c + 2, 4)}]
+        copies = []
+        for k, target in enumerate(targets):
+            one = copy(gain_v.at[k], gain_x.at[k], 18 + k, 18 + k, target)
+            one.start()
+            one.wait_recv()
+            copies.append(one)
+            if k < 4:
+                gain_v[k + 1] = gain_v[k] + gain_x[k]
+            else:
+                gain_out[...] = gain_v[k] + gain_x[k]
+        for one in copies:
+            one.wait_send()
+
+    def along_line():
+        order = near_order(c)
+        forwards = []
+        for step in range(1, 4):
+            d = order[step]
+            for index in range(10):
+                one = line(index, d, 20 + (step - 1) * 10 + index, jnp.where(d < c, above, below))
+                one.wait_recv()
+                pl.when(inner)(one.start)
+                forwards.append(one)
+        for index in range(10):
+            pl.when(c < 3)(line(index, c, index, above).wait_send)
+            pl.when(c > 0)(line(index, c, 10 + index, below).wait_send)
+        for one in forwards:
+            pl.when(inner)(one.wait_send)
+        for k in range(4):
+            gate_rows = gate_x.at[:, rows_of(k)]
+            mix_rows = mix_x.at[:, rows_of(k)]
+            copy(gate_rows, gate_rows, k, 0, other).wait_send()
+            copy(mix_rows, mix_rows, 4 + k, 0, other).wait_send()
             if k:
-                copy(mine.at[:, rows], place(c, f), slot + k, arrival_y + f, {"fsdp": owner}).start()
-            else:
-                keep(mine.at[:, rows], place(c, f), 4)
-
-    home_wait(1, gate_v)
-    to_owners(gate_v, gate_x, gate_at, 0, 10, 10)
-    start_line(1)
-    home_wait(2, out_v)
-    fold(out_v, out_x, 9)
-    keep(out_v, out_at(c, f), 4)
-    start_line(5)
-    for k in range(3):
-        origin = items[2 + k][1]
-        arrived(gate_at(c, origin), 10 + origin)
-        start_line(2 + k)
-    home_wait(3, mix_v)
-    to_owners(mix_v, mix_x, mix_at, 4, 14, 14)
-    start_line(6)
-    for k in range(3):
-        origin = items[7 + k][1]
-        arrived(mix_at(c, origin), 14 + origin)
-        start_line(7 + k)
-
-    gain_v[0] = gains[...]
-    twin = f + 1 - 2 * lax.rem(f, 2)
-    across = f + 2 - 4 * (f // 2)
-    targets = [{"section": other}, {"fsdp": twin}, {"fsdp": across}, {"ctx": pair}, {"ctx": far}]
-    gain_copies = []
-    for k, target in enumerate(targets):
-        one = copy(gain_v.at[k], gain_x.at[k], 18 + k, 18 + k, target)
-        one.start()
-        one.wait_recv()
-        gain_copies.append(one)
-        if k < 4:
-            gain_v[k + 1] = gain_v[k] + gain_x[k]
-        else:
-            gain_out[...] = gain_v[k] + gain_x[k]
-
-    order = near_order(c)
-    forwards = []
-    for step in range(1, 4):
-        d = order[step]
-        onward = jnp.where(d < c, above, below)
-        for index, (place, origin) in enumerate(items):
-            one = line(place, origin, index, d, 20 + (step - 1) * 10 + index, onward)
-            one.wait_recv()
-            pl.when(inner)(one.start)
-            forwards.append(one)
-    for index, (place, origin) in enumerate(items):
-        pl.when(c < 3)(line(place, origin, index, c, index, above).wait_send)
-        pl.when(c > 0)(line(place, origin, index, c, 10 + index, below).wait_send)
-    for one in forwards:
-        pl.when(inner)(one.wait_send)
-    for one in gain_copies:
-        one.wait_send()
-    for k in range(4):
-        copy(gate_x.at[:, rows_of(k)], gate_x.at[:, rows_of(k)], k, 0, {"section": other}).wait_send()
-        copy(mix_x.at[:, rows_of(k)], mix_x.at[:, rows_of(k)], 4 + k, 0, {"section": other}).wait_send()
-        if k:
-            copy(gate_x.at[:, rows_of(k)], gate_x.at[:, rows_of(k)], 10 + k, 0, {"section": other}).wait_send()
-            copy(mix_x.at[:, rows_of(k)], mix_x.at[:, rows_of(k)], 14 + k, 0, {"section": other}).wait_send()
-    copy(down_x, down_x, 8, 0, {"section": other}).wait_send()
-    copy(out_x, out_x, 9, 0, {"section": other}).wait_send()
-
-
-def return_call(first, second, gains):
-    mix, gate, out, down = first
-    units, width = down.shape
-    depth = width // 4
-    anywhere = pl.BlockSpec(memory_space=pl.ANY)
-    inside = pl.BlockSpec(memory_space=pltpu.VMEM)
+                copy(gate_rows, gate_rows, 10 + k, 0, other).wait_send()
+                copy(mix_rows, mix_rows, 14 + k, 0, other).wait_send()
+        copy(down_x, down_x, 8, 0, other).wait_send()
+        copy(out_x, out_x, 9, 0, other).wait_send()
+
+    return begin_feed, begin_mix, feed_steps, mix_steps, sum_gains, along_line
+
+
+def widen_kernel(mix, gate, out, down, mix_f, gate_f, out_f, down_f):
+    rows = mix.shape[1]
+
+    def choice(count, wanted):
+        lane = lax.broadcasted_iota(jnp.int32, (count, 4 * HEAD), 0)
+        column = lax.broadcasted_iota(jnp.int32, (count, 4 * HEAD), 1)
+        return jnp.where(lane == wanted(column // HEAD, lax.rem(column, HEAD)), 1.0, 0.0).astype(BF)
+
+    def halves(place):
+        half = place // (HEAD // 2)
+        return half * SPAN + place - half * (HEAD // 2)
+
+    queries = choice(4 * LANES, lambda head, place: head * LANES + halves(place))
+    keys = choice(8 * LANES, lambda head, place: 2 * head * LANES + halves(place))
+    values = choice(8 * LANES, lambda head, place: (2 * head + 1) * LANES + place)
+    width = 4 * 4 * HEAD
+    for g in range(4):
+        mix_f[:, g * 4 * HEAD : (g + 1) * 4 * HEAD] = kernel_dot(mix[0, :, g * 4 * LANES : (g + 1) * 4 * LANES], queries)
+    for g in range(2):
+        slots = mix[1, :, g * 8 * LANES : (g + 1) * 8 * LANES]
+        at = width + g * 4 * HEAD
+        mix_f[:, at : at + 4 * HEAD] = kernel_dot(slots, keys)
+        at = width + (g + 2) * 4 * HEAD
+        mix_f[:, at : at + 4 * HEAD] = kernel_dot(slots, values)
+    half = gate.shape[2]
+    gate_f[:, :half] = gate[0].astype(F32)
+    gate_f[:, half:] = gate[1].astype(F32)
+    out_f[...] = out[...].astype(F32)
+    down_f[...] = down[...].astype(F32)
+
+
+def widen_call(mix, gate, out, down):
+    steps = 8
+    depth = mix.shape[1]
+    width = out.shape[1]
+    rows = depth // steps
+    down_rows = down.shape[0] // steps
     return pl.pallas_call(
-        return_kernel,
+        widen_kernel,
+        grid=(steps,),
         out_shape=(
-            jax.ShapeDtypeStruct((3, depth, 16 * LANES), BF),
-            jax.ShapeDtypeStruct((2, depth, 16 * units), BF),
-            jax.ShapeDtypeStruct((4 * HEAD, width), BF),
-            jax.ShapeDtypeStruct((4 * units, width), BF),
-            jax.ShapeDtypeStruct(gains.shape, F32),
+            jax.ShapeDtypeStruct((depth, 2 * width), F32),
+            jax.ShapeDtypeStruct((depth, 2 * gate.shape[2]), F32),
+            jax.ShapeDtypeStruct(out.shape, F32),
+            jax.ShapeDtypeStruct(down.shape, F32),
         ),
-        in_specs=[anywhere] * 8 + [inside],
-        out_specs=(anywhere,) * 4 + (inside,),
-        scratch_shapes=[
-            pltpu.VMEM(mix.shape, BF), pltpu.VMEM(gate.shape, BF), pltpu.VMEM(out.shape, BF), pltpu.VMEM(down.shape, BF),
-            pltpu.VMEM(mix.shape, BF), pltpu.VMEM(gate.shape, BF), pltpu.VMEM(out.shape, BF), pltpu.VMEM(down.shape, BF),
-            pltpu.VMEM((5,) + gains.shape, F32), pltpu.VMEM((5,) + gains.shape, F32),
-            pltpu.SemaphoreType.DMA((5,)),
-            pltpu.SemaphoreType.DMA((23,)),
-            pltpu.SemaphoreType.DMA((23,)),
-            pltpu.SemaphoreType.DMA((50,)),
-            pltpu.SemaphoreType.DMA((40,)),
+        in_specs=[
+            pl.BlockSpec((2, rows, mix.shape[2]), lambda i: (0, i, 0)),
+            pl.BlockSpec((2, rows, gate.shape[2]), lambda i: (0, i, 0)),
+            pl.BlockSpec((rows, width), lambda i: (i, 0)),
+            pl.BlockSpec((down_rows, width), lambda i: (i, 0)),
         ],
-        compiler_params=pltpu.CompilerParams(collective_id=3, has_side_effects=True, vmem_limit_bytes=56 << 20),
-    )(mix, second[0], gate, second[1], out, second[2], down, second[3], gains)
+        out_specs=(
+            pl.BlockSpec((rows, 2 * width), lambda i: (i, 0)),
+            pl.BlockSpec((rows, 2 * gate.shape[2]), lambda i: (i, 0)),
+            pl.BlockSpec((rows, width), lambda i: (i, 0)),
+            pl.BlockSpec((down_rows, width), lambda i: (i, 0)),
+        ),
+        compiler_params=pltpu.CompilerParams(vmem_limit_bytes=48 << 20),
+    )(mix, gate, out, down)
 
 
 def on_line():
@@ -1192,54 +1409,43 @@
     return weights, gains
 
 
+def own_gain_sums(plan, section, gain_sum, depth):
+    gain_sum = lax.dynamic_slice_in_dim(gain_sum, 2 * section, 2, 0)
+    return lax.dynamic_slice_in_dim(gain_sum, plan.f * depth, depth, 1)
+
+
 def returned_grads(plan, section, weight_grads, gain_grads, depth):
     C, F = plan.C, plan.F
     gain_sum = jnp.concatenate([gain_grads[0], gain_grads[1]])
-    if on_line():
-        mixes, both, out_grad, down_grad, gain_sum = return_call(
-            weight_grads[0], weight_grads[1], jnp.pad(gain_sum, ((0, 4), (0, 0)))
-        )
-        slots = mixes.astype(F32).reshape(3, depth, 16, LANES)
-        q_grad = join_halves(slots[0]).reshape(depth, -1)
-        pairs = slots[1:].reshape(2, depth, KV_HEADS, 2, LANES).sum(axis=3)
-        k_grad = join_halves(pairs[0]).reshape(depth, -1)
-        v_grad = pairs[1][..., :HEAD].reshape(depth, -1)
-        mix_grad = jnp.concatenate([q_grad, k_grad, v_grad], axis=1)
-        gate_up_grad = jnp.concatenate([both[0], both[1]], axis=1).astype(F32)
-        out_grad = out_grad.astype(F32)
-        down_grad = down_grad.astype(F32)
-        gain_sum = gain_sum[:4]
-    else:
-        def collected(index):
-            first, second = weight_grads[0][index], weight_grads[1][index]
-            own = jnp.where(section == 0, first, second)
-            away = jnp.where(section == 0, second, first)
-            return (own.astype(F32) + swap_sections(away).astype(F32)).astype(BF)
-
-        cut_grad = jnp.concatenate(list(collected(0)) + list(collected(1)), axis=1)
-        cut_grad = lax.all_to_all(cut_grad.reshape(F, depth, -1), "fsdp", 0, 0)
-        cut_grad = lax.all_gather(cut_grad, "ctx", axis=0, tiled=False)
-        out_grad = lax.all_gather(collected(2), "ctx", axis=0, tiled=False)
-        down_grad = lax.all_gather(collected(3), "ctx", axis=0, tiled=True).astype(F32)
-
-        def heads_of(columns, count):
-            folded = columns.astype(F32).reshape(count, C // count, F, depth, columns.shape[-1]).sum(axis=1)
-            return jnp.transpose(folded, (2, 1, 0, 3))
-
-        q_grad = join_halves(heads_of(cut_grad[..., :LANES], plan.heads_f)).reshape(depth, -1)
-        k_grad = join_halves(heads_of(cut_grad[..., LANES : 2 * LANES], plan.groups_f)).reshape(depth, -1)
-        v_grad = heads_of(cut_grad[..., 2 * LANES : 3 * LANES], plan.groups_f)[..., :HEAD].reshape(depth, -1)
-        mix_grad = jnp.concatenate([q_grad, k_grad, v_grad], axis=1)
-        both = jnp.transpose(cut_grad[..., 3 * LANES :], (2, 1, 0, 3)).astype(F32)
-        gate_up_grad = jnp.concatenate(
-            [both[..., : plan.units].reshape(depth, -1), both[..., plan.units :].reshape(depth, -1)], axis=1
-        )
-        out_grad = out_grad.astype(F32).reshape(plan.heads_f, plan.share, HEAD, depth * F).sum(axis=1).reshape(-1, depth * F)
-
-        gain_sum = lax.psum(gain_sum, ("section", "ctx", "fsdp"))
-    gain_sum = lax.dynamic_slice_in_dim(gain_sum, 2 * section, 2, 0)
-    gain_sum = lax.dynamic_slice_in_dim(gain_sum, plan.f * depth, depth, 1)
-    return mix_grad, gate_up_grad, out_grad, down_grad, gain_sum
+
+    def collected(index):
+        first, second = weight_grads[0][index], weight_grads[1][index]
+        own = jnp.where(section == 0, first, second)
+        away = jnp.where(section == 0, second, first)
+        return (own.astype(F32) + swap_sections(away).astype(F32)).astype(BF)
+
+    cut_grad = jnp.concatenate(list(collected(0)) + list(collected(1)), axis=1)
+    cut_grad = lax.all_to_all(cut_grad.reshape(F, depth, -1), "fsdp", 0, 0)
+    cut_grad = lax.all_gather(cut_grad, "ctx", axis=0, tiled=False)
+    out_grad = lax.all_gather(collected(2), "ctx", axis=0, tiled=False)
+    down_grad = lax.all_gather(collected(3), "ctx", axis=0, tiled=True).astype(F32)
+
+    def heads_of(columns, count):
+        folded = columns.astype(F32).reshape(count, C // count, F, depth, columns.shape[-1]).sum(axis=1)
+        return jnp.transpose(folded, (2, 1, 0, 3))
+
+    q_grad = join_halves(heads_of(cut_grad[..., :LANES], plan.heads_f)).reshape(depth, -1)
+    k_grad = join_halves(heads_of(cut_grad[..., LANES : 2 * LANES], plan.groups_f)).reshape(depth, -1)
+    v_grad = heads_of(cut_grad[..., 2 * LANES : 3 * LANES], plan.groups_f)[..., :HEAD].reshape(depth, -1)
+    mix_grad = jnp.concatenate([q_grad, k_grad, v_grad], axis=1)
+    both = jnp.transpose(cut_grad[..., 3 * LANES :], (2, 1, 0, 3)).astype(F32)
+    gate_up_grad = jnp.concatenate(
+        [both[..., : plan.units].reshape(depth, -1), both[..., plan.units :].reshape(depth, -1)], axis=1
+    )
+    out_grad = out_grad.astype(F32).reshape(plan.heads_f, plan.share, HEAD, depth * F).sum(axis=1).reshape(-1, depth * F)
+
+    gain_sum = lax.psum(gain_sum, ("section", "ctx", "fsdp"))
+    return mix_grad, gate_up_grad, out_grad, down_grad, own_gain_sums(plan, section, gain_sum, depth)
 
 
 def on_device(
@@ -1274,17 +1480,17 @@
     kept = []
     if on_line():
         own_gains = jnp.pad(jnp.concatenate([attention_gain, feed_gain]), ((0, 14), (0, 0)))
-        shared = share_call(query_key_value, output_weight, gate_up, down_weight, own_gains)
-        places = (positions[:, None], positions[None, :])
-        for s in range(2):
-            *keep, result = forward_call(s, x, shared, tables, places)
-            kept.append((x, keep))
-            results.append(result)
-            x = result
-        for s in (1, 0):
-            input_grads[s], grad, *weight_grads[s], gain_grads[s] = backward_call(
-                s, grad, shared, tables, places, *kept[s]
-            )
+        shards = (query_key_value, output_weight, gate_up, down_weight, own_gains)
+        common = tuple(tables) + (positions[:, None], positions[None, :])
+        first = forward_call(0, x, shards, common)
+        weights = first[10:]
+        results.append(first[9])
+        second = forward_call(1, first[9], weights, common)
+        results.append(second[9])
+        input_grads[1], *old, grad = backward_call(1, grad, weights, common, [first[9], *second[:9]])
+        input_grads[0], *wide, gain_sum = backward_call(0, grad, weights, common, [x, *first[:9]], old)
+        mix_grad, gate_up_grad, out_grad, down_grad = widen_call(*wide)
+        gain_sum = own_gain_sums(plan, section, gain_sum, depth)
     else:
         weights, gains = shared_weights(
             plan, section, attention_gain, query_key_value, output_weight, feed_gain, gate_up, down_weight
@@ -1298,6 +1504,8 @@
                 plan, grad, weights[s], gains[s], kept[s], positions, part_positions, tables, part_tables
             )
             grad = input_grads[s].astype(BF)
+        shard_grads = returned_grads(plan, section, weight_grads, gain_grads, depth)
+        mix_grad, gate_up_grad, out_grad, down_grad, gain_sum = shard_grads
 
     def mine_and_theirs(first, second):
         return jnp.where(section == 0, first, second), jnp.where(section == 0, second, first)
@@ -1309,8 +1517,6 @@
     section_outputs = by_batch(*results)
     section_input_grads = by_batch(*input_grads)
 
-    shard_grads = returned_grads(plan, section, weight_grads, gain_grads, depth)
-    mix_grad, gate_up_grad, out_grad, down_grad, gain_sum = shard_grads
     return (
         section_outputs[None],
         section_input_grads[None],

time: 872 us -> 708 us (0.81)
  Pallas kernels: 775 us -> 678 us
  local copies, waits for them, and re-layouts: 44.3 us -> 8.02 us
  other arithmetic: 38.7 us -> 8.17 us
    pallas_call x6 -> x5, Pallas kernels: 775 us -> 678 us  [the longest x2 431 us: backward_call(): pl.pallas_call(backward_return_kernel if returning else functools.partial...]
    slice x10 -> x0, local copies, waits for them, and re-layouts: 19.8 us -> none  [the longest x2 4.42 us: join_halves(): halves = columns.reshape(columns.shape[:-1] + (2, SPAN))[..., :HEAD // 2]]
    reduce_sum x1 -> x0, other arithmetic: 10.3 us -> none  [returned_grads(): pairs = slots[1:].reshape(2, depth, KV_HEADS, 2, LANES).sum(axis=3)]
    broadcast_in_dim x3 -> x0, other arithmetic: 9.77 us -> none  [the longest x1 5.61 us: on_device(): down_grad[None]]
    reshape x1 -> x0, local copies, waits for them, and re-layouts: 9.37 us -> none  [returned_grads(): pairs = slots[1:].reshape(2, depth, KV_HEADS, 2, LANES).sum(axis=3)]
  transfers between devices with their start and end apart: 2 -> 2, of which waited for: 0 -> 0; matrix products, arithmetic and copies ran while one was open for 8% -> 0% of each run, Pallas kernels for 57% -> 64%
where the time goes in v3:
time: 708 us; the launch traced here: 699 us
  Pallas kernels  678 us (96%)
  other arithmetic  8.17 us (1%)
  local copies, waits for them, and re-layouts  8.02 us (1%)
    pallas_call x2, Pallas kernels, backward_call(): pl.pallas_call(backward_return_kernel if returning else functools.partial...  431 us
    pallas_call x2, Pallas kernels, forward_call(): pl.pallas_call(forward_share_kernel if sharing else functools.partial(for...  231 us
    pallas_call x1, Pallas kernels, widen_call(): pl.pallas_call(widen_kernel, grid=(steps,), out_shape=(jax.ShapeDtypeStru...  16 us
  transfers between devices with their start and end apart: 2, of which 0 were waited for; matrix products, arithmetic and copies ran while one was open for 0% of the time, Pallas kernels for 64%

profile of v3, /device:TPU:0, one launch (start us, length us, event | category | flops | bytes accessed | tf_op | source)
XLA Modules:
  0.0 699.3 jit_solution(16362386248446677206)
XLA Ops:
  0.7 0.7 fusion.6
  1.4 0.1 iota_add_fusion
  1.5 0.7 add.62.refs_9_
  2.2 1.3 add.65.refs_8_
  3.4 0.1 convert_element_type.15
  3.5 0.7 dynamic-slice_bitcast_fusion.1.refs_0_.refs_10_
  4.2 1.3 fusion.3.refs_5_
  5.5 1.9 fusion
  7.4 1.3 pad_maximum_fusion
  8.7 136.1 %shard_map.152 = (bf16[1024,1536]{1,0:T(8,128)(2,1)}, bf16[1024,128]{1,0:T(8,128)(2,1)}, bf16[1024,128]{1,0:T(8,128)(2,1)}, bf16[1024,128]{1,0:T(8,128)(2,1)}, b...) custom-call(bf16[64,1536]{1,0:T(8,128)(2,1)} %dynamic-slice_bitcast_, ...), custom_call_target="tpu_custom_call" | custom-call | tf_op jit(solution)/shard_map/pallas_call | solution.py:897
  144.9 95.4 %shard_map.153 = (bf16[1024,1536]{1,0:T(8,128)(2,1)}, bf16[1024,128]{1,0:T(8,128)(2,1)}, bf16[1024,128]{1,0:T(8,128)(2,1)}, bf16[1024,128]{1,0:T(8,128)(2,1)}, b...) custom-call(bf16[64,1536]{1,0:T(8,128)(2,1)} %get-tuple-element.50.r, ...), custom_call_target="tpu_custom_call" | custom-call | tf_op jit(solution)/shard_map/pallas_call | solution.py:897
  240.2 1.0 broadcast_select_fusion.2
  241.2 0.6 collective-permute-start
  241.8 0.7 dynamic-slice_bitcast_fusion.refs_0_
  242.5 99.3 %shard_map.154 = (f32[64,1536]{1,0:T(8,128)}, bf16[2,1536,128]{2,1,0:T(8,128)(2,1)}, bf16[2,1536,256]{2,1,0:T(8,128)(2,1)}, bf16[96,1536]{1,0:T(8,128)(2,1)}, bf...) custom-call(bf16[64,1536]{1,0:T(8,128)(2,1)} %dynamic-slice_bitcast_fusion.refs_0_, ...), custom_call_target="tpu_custom_call" | custom-call | tf_op jit(solution)/shard_map/pallas_call | solution.py:934
  341.8 331.3 %shard_map.155 = (f32[64,1536]{1,0:T(8,128)}, bf16[2,384,2048]{2,1,0:T(8,128)(2,1)}, bf16[2,384,4096]{2,1,0:T(8,128)(2,1)}, bf16[384,1536]{1,0:T(8,128)(2,1)}, b...) custom-call(bf16[64,1536]{1,0:T(8,128)(2,1)} %get-tuple-element.66.refs_0_, ...), custom_call_target="tpu_custom_call" | custom-call | tf_op jit(solution)/shard_map/pallas_call | solution.py:934
  673.2 3.2 collective-permute-start.1
  676.4 1.9 copy-done.2
  678.3 1.3 copy-done.3
  679.6 16.0 %shard_map.156 = (f32[384,3072]{1,0:T(8,128)}, f32[384,8192]{1,0:T(8,128)}, f32[384,1536]{1,0:T(8,128)}, f32[1024,1536]{1,0:T(8,128)}) custom-call(bf16[2,384,2048]{2,1,0:T(8,128)(2,1)S(1)} %copy-done.2, bf16[2,384,4096]{2,1,0:T(8,128)(2,1)} %get-tuple-element.85.gate, bf16[384,1536]{1,0:T(8,128)(2,1)S(1)} %copy-done.3, ...), custom_call_target="tpu_custom_call" | custom-call | tf_op jit(solution)/shard_map/pallas_call | solution.py:1158
  695.5 1.4 fusion.7
  697.0 0.8 maximum_bitcast_fusion.1
  697.8 0.1 select_bitcast_fusion.1
  697.9 0.9 maximum_bitcast_fusion
  (24 shorter events, 0.2 us)
Async XLA Ops:
  0.6 2.9 copy-start
  144.8 95.4 %copy-start.4 = (bf16[64,1536]{1,0:T(8,128)(2,1)S(1)}, bf16[64,1536]{1,0:T(8,128)(2,1)}, u32[]{:S(2)}) copy-start(bf16[64,1536]{1,0:T(8,128)(2,1)} %get-tuple-element.50.refs_0_.refs_10_) | copy-start | bytes 589828
  144.8 96.9 %copy-start.9 = (bf16[2,64,1536]{2,1,0:T(8,128)(2,1)S(1)}, bf16[2,64,1536]{2,1,0:T(8,128)(2,1)}, u32[]{:S(2)}) copy-start(bf16[2,64,1536]{2,1,0:T(8,128)(2,1)} %param.10) | copy-start | bytes 1179652
  241.2 455.8 %collective-permute-start = (bf16[64,1536]{1,0:T(8,128)(2,1)S(1)}, bf16[64,1536]{1,0:T(8,128)(2,1)S(1)}, u32[]{:S(2)}, u32[]{:S(2)}) collective-permute-start(bf16[64,1536]{1,0:T(8,128)(2,1)S(1)} %broadcast_select_fusion.2), channel_id=1, source_target_pairs={{0,16},{16,0},{1,17},{17,1},{2,18},{18,2},{3,19},{19,3},{4,20},{20... | collective-permute-start | bytes 589832 | tf_op jit(solution)/shard_map/ppermute | solution.py:1385
  341.8 331.4 %copy-start.6 = (f32[64,1536]{1,0:T(8,128)S(1)}, f32[64,1536]{1,0:T(8,128)}, u32[]{:S(2)}) copy-start(f32[64,1536]{1,0:T(8,128)} %get-tuple-element.82) | copy-start | bytes 1179652
  673.2 24.6 %collective-permute-start.1 = (f32[64,1536]{1,0:T(8,128)S(1)}, f32[64,1536]{1,0:T(8,128)S(1)}, u32[]{:S(2)}, u32[]{:S(2)}) collective-permute-start(f32[64,1536]{1,0:T(8,128)S(1)} %broadcast_select_fusion), channel_id=1, source_target_pairs={{0,16},{16,0},{1,17},{17,1},{2,18},{18,2},{3,19},{19,3},{4,20},{20... | collective-permute-start | bytes 1179656 | tf_op jit(solution)/shard_map/ppermute | solution.py:1385
  676.4 1.9 copy-start.2
  678.3 1.3 copy-start.3
  679.6 17.4 %copy-start.5 = (bf16[64,1536]{1,0:T(8,128)(2,1)S(1)}, bf16[64,1536]{1,0:T(8,128)(2,1)}, u32[]{:S(2)}) copy-start(bf16[64,1536]{1,0:T(8,128)(2,1)} %get-tuple-element.50.refs_0_.refs_10_) | copy-start | bytes 589828
  679.6 17.4 %copy-start.8 = (bf16[64,1536]{1,0:T(8,128)(2,1)S(1)}, bf16[64,1536]{1,0:T(8,128)(2,1)}, u32[]{:S(2)}) copy-start(bf16[64,1536]{1,0:T(8,128)(2,1)} %get-tuple-element.56) | copy-start | bytes 589828
  679.6 18.3 %copy-start.7 = (f32[64,1536]{1,0:T(8,128)S(1)}, f32[64,1536]{1,0:T(8,128)}, u32[]{:S(2)}) copy-start(f32[64,1536]{1,0:T(8,128)} %get-tuple-element.81) | copy-start | bytes 1179652
  679.6 19.3 %copy-start.1 = (bf16[2,64,1536]{2,1,0:T(8,128)(2,1)S(1)}, bf16[2,64,1536]{2,1,0:T(8,128)(2,1)}, u32[]{:S(2)}) copy-start(bf16[2,64,1536]{2,1,0:T(8,128)(2,1)} %param.9) | copy-start | bytes 1179652

commit v4 on v3

--- a/solution.py
+++ b/solution.py
@@ -27,6 +27,7 @@
     inner = jnp.logical_and(c > 0, c < 3)
     for peer in (f + 2 - 4 * (f // 2), f + 1 - 2 * lax.rem(f, 2)):
         pl.semaphore_signal(barrier, inc=1, device_id={"fsdp": peer}, device_id_type=MESH)
+    pl.semaphore_signal(barrier, inc=1, device_id={"ctx": lax.rem(c + 2, 4)}, device_id_type=MESH)
 
     @pl.when(c < 3)
     def _():
@@ -38,11 +39,11 @@
 
     @pl.when(inner)
     def _():
-        pl.semaphore_wait(barrier, 4)
+        pl.semaphore_wait(barrier, 5)
 
     @pl.when(jnp.logical_not(inner))
     def _():
-        pl.semaphore_wait(barrier, 3)
+        pl.semaphore_wait(barrier, 4)
 
 
 def near_order(c):
@@ -50,21 +51,32 @@
     return [c, c + 1 - 2 * lax.rem(c, 2), jnp.where(low, 2, 1), jnp.where(low, 3, 0)]
 
 
+def own_block(c, f):
+    return c * 4 + lax.rem(f, 2) * 2 + f // 2
+
+
 def gather_rows(whole, rows, send, recv, ready=None, started=None):
     c = lax.axis_index("ctx")
     f = lax.axis_index("fsdp")
-    across = f + 2 - 4 * (f // 2)
-    twin = f + 1 - 2 * lax.rem(f, 2)
-    cross = across + 1 - 2 * lax.rem(f, 2)
+    y = f // 2
+    lane = lax.rem(f, 2)
     inner = jnp.logical_and(c > 0, c < 3)
     outer = jnp.logical_not(inner)
     order = near_order(c)
     pair = order[1]
     half = rows // 2
-    sent = []
-
-    def at(cc, ff, h):
-        return whole.at[pl.ds(pl.multiple_of((cc * 4 + ff) * rows + h * half, half), half)]
+    to_across = {"fsdp": f + 2 - 4 * y}
+    to_twin = {"fsdp": f + 1 - 2 * lane}
+    to_pair = {"ctx": pair}
+
+    def at(d, k, yy, h):
+        return whole.at[pl.ds(pl.multiple_of((d * 4 + k * 2 + yy) * rows + h * half, half), half)]
+
+    def block(d, k, yy):
+        return whole.at[pl.ds(pl.multiple_of((d * 4 + k * 2 + yy) * rows, rows), rows)]
+
+    def two(d, k):
+        return whole.at[pl.ds(pl.multiple_of((d * 4 + k * 2) * rows, rows), 2 * rows)]
 
     def copy(src, slot, arrival, peer):
         return pltpu.make_async_remote_copy(
@@ -77,94 +89,96 @@
             one.start()
         else:
             pl.when(when)(one.start)
-        sent.append((one, when))
 
     def arrived(ref, arrival):
-        copy(ref, 0, arrival, {"fsdp": twin}).wait_recv()
-
-    up_to = {"ctx": jnp.minimum(c + 1, 3)}
-    down_to = {"ctx": jnp.maximum(c - 1, 0)}
+        copy(ref, 0, arrival, to_twin).wait_recv()
+
+    def gone(count, slot):
+        copy(whole.at[pl.ds(0, count * half)], slot, 0, to_twin).wait_send()
+
     for h in range(2):
-        go(at(c, f, h), h, 2 * c + h, up_to, c < 3)
-        go(at(c, f, h), 2 + h, 2 * c + h, down_to, c > 0)
-        go(at(c, f, h), 4 + h, 8 + 2 * c + h, {"fsdp": across})
-    for h in range(2):
-        go(at(c, f, h), 12 + h, 16 + 2 * c + h, {"fsdp": twin})
+        go(at(c, lane, y, h), 0, 2 * c + h, {"ctx": jnp.minimum(c + 1, 3)}, c < 3)
+        go(at(c, lane, y, h), 1, 2 * c + h, {"ctx": jnp.maximum(c - 1, 0)}, c > 0)
+        go(at(c, lane, y, h), 3, 8 + c, to_across)
     if started is not None:
         started()
 
-    def along(step, h):
-        d = order[step]
-        block = at(d, f, h)
-        arrived(block, 2 * d + h)
-        go(block, 28 + 2 * step + h, 2 * d + h, {"ctx": jnp.where(d < c, jnp.minimum(c + 1, 3), jnp.maximum(c - 1, 0))}, inner)
-        if (step, h) != (1, 0):
-            go(block, 4 + 2 * step + h, 8 + 2 * d + h, {"fsdp": across})
-        go(block, 12 + 2 * step + h, 16 + 2 * d + h, {"fsdp": twin})
-
-    def over(step, h):
-        d = order[step]
-        block = at(d, across, h)
-        arrived(block, 32 if (step, h) == (1, 0) else 8 + 2 * d + h)
-        go(block, 20 + 2 * step + h, 24 + 2 * d + h, {"fsdp": twin})
-
-    def complete(step):
-        d = order[step]
-        for h in range(2):
-            arrived(at(d, twin, h), 16 + 2 * d + h)
-            arrived(at(d, cross, h), 24 + 2 * d + h)
+    events = [
+        (pair, 0),
+        (jnp.where(inner, order[2], pair), jnp.where(inner, 0, 1)),
+        (jnp.where(inner, pair, order[2]), jnp.where(inner, 1, 0)),
+        (order[2], 1),
+        (order[3], 0),
+        (order[3], 1),
+    ]
+
+    def along(index):
+        d, h = events[index]
+        piece = at(d, lane, y, h)
+        arrived(piece, 2 * d + h)
+        go(piece, 2, 2 * d + h, {"ctx": jnp.where(d < c, c + 1, c - 1)}, inner)
+        go(piece, 3, 8 + d, to_across, jnp.logical_or(d != pair, h == 0) if index in (1, 2) else None)
+
+    def complete(d):
+        arrived(two(d, 1 - lane), 13 + d)
         if ready is not None:
             ready(d)
 
-    along(1, 0)
-    over(0, 0)
-    go(at(c, across, 0), 36, 32, {"ctx": pair}, outer)
-    along(1, 1)
-    over(0, 1)
-    along(2, 0)
-    along(2, 1)
-    complete(0)
-    over(1, 1)
-    along(3, 0)
-    over(2, 0)
-    along(3, 1)
-    go(at(c, across, 0), 37, 32, {"ctx": pair}, inner)
-    over(2, 1)
-    complete(2)
-    over(3, 0)
-    over(1, 0)
-    complete(1)
-    over(3, 1)
-    complete(3)
-    for one, when in sent:
-        if when is None:
-            one.wait_send()
-        else:
-            pl.when(when)(one.wait_send)
-
-
-GATHER_SENDS = 38
-GATHER_RECVS = 33
-
-
-def scatter_sum(part, total, land, send, recv, produce=None, meanwhile=None, tick=None):
+    def pair_half(when):
+        go(at(c, lane, 1 - y, 1), 4, 12, to_pair, when)
+
+    along(0)
+    along(1)
+    along(2)
+    arrived(block(c, lane, 1 - y), 8 + c)
+    pair_half(outer)
+    go(two(c, lane), 5, 13 + c, to_twin)
+    along(3)
+    complete(c)
+    along(4)
+    along(5)
+    pair_half(inner)
+    arrived(block(order[2], lane, 1 - y), 8 + order[2])
+    go(two(order[2], lane), 5, 13 + order[2], to_twin)
+    go(block(order[3], lane, y), 5, 13 + order[3], to_twin)
+    complete(order[2])
+    arrived(at(pair, lane, 1 - y, 0), 8 + pair)
+    arrived(at(pair, lane, 1 - y, 1), 12)
+    go(two(pair, lane), 5, 13 + pair, to_twin)
+    arrived(block(order[3], lane, 1 - y), 8 + order[3])
+    go(block(order[3], lane, 1 - y), 5, 17, to_twin)
+    complete(pair)
+    arrived(block(order[3], 1 - lane, y), 13 + order[3])
+    arrived(block(order[3], 1 - lane, 1 - y), 17)
+    if ready is not None:
+        ready(order[3])
+    pl.when(c < 3)(lambda: gone(2, 0))
+    pl.when(c > 0)(lambda: gone(2, 1))
+    pl.when(inner)(lambda: gone(6, 2))
+    gone(7, 3)
+    gone(1, 4)
+    gone(16, 5)
+
+
+GATHER_SENDS = 6
+GATHER_RECVS = 18
+
+
+def scatter_sum(part, total, land, send, recv, produce=None, meanwhile=None):
     c = lax.axis_index("ctx")
     f = lax.axis_index("fsdp")
-    across = f + 2 - 4 * (f // 2)
-    twin = f + 1 - 2 * lax.rem(f, 2)
-    cross = across + 1 - 2 * lax.rem(f, 2)
+    y = f // 2
+    lane = lax.rem(f, 2)
     inner = jnp.logical_and(c > 0, c < 3)
     rows = total.shape[0]
     half = rows // 2
     order = near_order(c)[::-1]
-    pair = order[2]
-    sent = []
-
-    def rows_at(cc, ff, h=None):
-        start = (cc * 4 + ff) * rows
-        if h is None:
-            return pl.ds(pl.multiple_of(start, rows), rows)
-        return pl.ds(pl.multiple_of(start + h * half, half), half)
+    to_across = {"fsdp": f + 2 - 4 * y}
+    to_twin = {"fsdp": f + 1 - 2 * lane}
+    to_pair = {"ctx": order[2]}
+
+    def rows_at(d, yy, h):
+        return pl.ds(pl.multiple_of((d * 4 + lane * 2 + yy) * rows + h * half, half), half)
 
     def copy(src, dst, slot, arrival, peer):
         return pltpu.make_async_remote_copy(
@@ -172,86 +186,96 @@
         )
 
     def go(src, dst, slot, arrival, peer):
-        one = copy(src, dst, slot, arrival, peer)
-        one.start()
-        sent.append(one)
+        copy(src, dst, slot, arrival, peer).start()
+
+    def gone(count, slot):
+        ref = part.at[pl.ds(0, count * half)]
+        copy(ref, ref, slot, 0, to_twin).wait_send()
 
     def piece(slot, h):
         return land.at[slot, pl.ds(h * half, half)]
 
     def landed(ref, arrival):
-        copy(ref, ref, 0, arrival, {"fsdp": twin}).wait_recv()
+        copy(ref, ref, 0, arrival, to_twin).wait_recv()
         return ref[...].astype(F32)
 
     def begin(step):
         d = order[step]
         if produce is not None:
             produce(d)
-        go(part.at[rows_at(d, cross)], land.at[step], step, step, {"fsdp": twin})
-        go(part.at[rows_at(d, twin)], land.at[4 + step], 4 + step, 4 + step, {"fsdp": twin})
-
-    def over(step, h):
+        for yy, slot in ((1 - y, step), (y, 27 + step)):
+            other = pl.ds(pl.multiple_of((d * 4 + 2 - lane * 2 + yy) * rows, rows), rows)
+            go(part.at[other], land.at[2 * step + yy], 0, slot, to_twin)
+
+    def twin_there(step, yy, slot):
+        ref = land.at[2 * step + yy]
+        copy(ref, ref, 0, slot, to_twin).wait_recv()
+
+    def over(step, h, first=False):
         d = order[step]
-        mine = rows_at(d, across, h)
-        if h == 0:
-            copy(land.at[step], land.at[step], 0, step, {"fsdp": twin}).wait_recv()
-        value = part[mine, :].astype(F32) + land[step, h * half : (h + 1) * half, :].astype(F32)
-        if (step, h) == (3, 0):
+        if first:
+            twin_there(step, 1 - y, step)
+        mine = rows_at(d, 1 - y, h)
+        value = part[mine, :].astype(F32) + piece(2 * step + 1 - y, h)[...].astype(F32)
+        if (step, h) == (3, 1):
             value = value + landed(piece(17, 0), 26)
         part[mine, :] = value.astype(BF)
-        if (step, h) == (2, 0):
-            go(part.at[mine], piece(17, 0), 16, 26, {"ctx": pair})
+        if (step, h) == (2, 1):
+            go(part.at[mine], piece(17, 0), 3, 26, to_pair)
         else:
-            go(part.at[mine], piece(8 + step, h), 8 + 2 * step + h, 8 + 2 * step + h, {"fsdp": across})
-
-    def onward(step, h):
+            go(part.at[mine], piece(8 + step, h), 1, 8 + 2 * step + h, to_across)
+
+    def onward(step, h, first=False):
         d = order[step]
-        mine = rows_at(d, f, h)
-        if h == 0:
-            copy(land.at[4 + step], land.at[4 + step], 0, 4 + step, {"fsdp": twin}).wait_recv()
-        value = part[mine, :].astype(F32) + land[4 + step, h * half : (h + 1) * half, :].astype(F32)
-        if (step, h) != (2, 0):
+        mine = rows_at(d, y, h)
+        if first:
+            twin_there(step, y, 27 + step)
+        value = part[mine, :].astype(F32) + piece(2 * step + y, h)[...].astype(F32)
+        if (step, h) != (2, 1):
             value = value + landed(piece(8 + step, h), 8 + 2 * step + h)
         if step == 3:
             total[h * half : (h + 1) * half, :] = value
             return
         part[mine, :] = value.astype(BF)
 
-        @pl.when(inner)
-        def _():
-            part[mine, :] = (part[mine, :].astype(F32) + landed(piece(12 + d, h), 16 + 2 * d + h)).astype(BF)
-
+        if step < 2:
+
+            @pl.when(inner)
+            def _():
+                part[mine, :] = (part[mine, :].astype(F32) + landed(piece(12 + d, h), 16 + 2 * d + h)).astype(BF)
+
+        here = jnp.logical_and(d < c, d == c - 1)
         target = jnp.where(d > c, c + 1, c - 1)
-        here = jnp.logical_and(d < c, d == c - 1)
-        go(part.at[mine], piece(jnp.where(here, 16, 12 + d), h), 17 + 2 * step + h,
-           jnp.where(here, 24, 16 + 2 * d) + h, {"ctx": target})
+        slot = jnp.where(here, 16, 12 + d)
+        arrival = jnp.where(here, 24, 16 + 2 * d) + h
+        if step == 0:
+            target = jnp.where(inner, d, target)
+            slot = jnp.where(inner, 18, slot)
+            arrival = jnp.where(inner, 31 + h, arrival)
+        go(part.at[mine], piece(slot, h), 2, arrival, {"ctx": target})
 
     begin(0)
-    over(0, 0)
+    over(0, 0, True)
     over(0, 1)
     begin(1)
     begin(2)
-    over(2, 0)
-    over(1, 0)
-    onward(0, 0)
+    over(2, 1, True)
+    over(1, 0, True)
+    onward(0, 0, True)
     over(1, 1)
     onward(0, 1)
+    if meanwhile is not None:
+        meanwhile()
     begin(3)
-    over(2, 1)
-    onward(1, 0)
-    if tick is not None:
-        tick()
-    over(3, 0)
+    over(2, 0)
+    onward(1, 0, True)
+    over(3, 0, True)
     onward(1, 1)
     over(3, 1)
-    if tick is not None:
-        tick()
+    onward(2, 1, True)
     onward(2, 0)
-    onward(2, 1)
-    if meanwhile is not None:
-        meanwhile()
     for h in range(2):
-        onward(3, h)
+        onward(3, h, h == 0)
 
         @pl.when(c > 0)
         def _():
@@ -261,12 +285,18 @@
         def _():
             total[h * half : (h + 1) * half, :] += landed(piece(16, h), 24 + h)
 
-    for one in sent:
-        one.wait_send()
-
-
-SCATTER_SENDS = 23
-SCATTER_RECVS = 27
+        @pl.when(jnp.logical_not(inner))
+        def _():
+            total[h * half : (h + 1) * half, :] += landed(piece(18, h), 31 + h)
+
+    gone(16, 0)
+    gone(7, 1)
+    gone(6, 2)
+    gone(1, 3)
+
+
+SCATTER_SENDS = 4
+SCATTER_RECVS = 33
 
 
 def kernel_dot(left, right):
@@ -337,7 +367,7 @@
     def __init__(self, sources, targets, scratch, sems):
         self.mix, self.out, self.gate_up, self.down, self.gains = sources
         self.w_mix, self.w_gate, self.w_out, self.w_down, self.w_gains = targets
-        self.mix_v, self.heads_v = scratch
+        self.mix_v, self.heads_v, self.gate_s, self.out_s, self.down_s = scratch
         self.local, self.send, self.recv = sems
         self.s = lax.axis_index("section")
         self.c = lax.axis_index("ctx")
@@ -352,7 +382,7 @@
     def greeted(self):
         return (
             [{"fsdp": peer} for peer in self.peers]
-            + [{"section": self.other}]
+            + [{"section": self.other}, {"ctx": lax.rem(self.c + 2, 4)}]
             + [{"section": self.other, "fsdp": peer} for peer in self.peers]
         )
 
@@ -373,6 +403,14 @@
 
     def load(self):
         self.loaded = self.keep(self.mix.at[0], self.mix_v, 0)
+        out_rows = self.out.at[0, pl.ds(pl.multiple_of(self.c * HEAD, HEAD), HEAD)]
+        down_rows = self.down.at[0, pl.ds(pl.multiple_of(self.c * self.units, self.units), self.units)]
+        self.staged = [
+            self.keep(self.gate_piece(self.f, part), self.gate_s.at[:, pl.ds(part * self.units, self.units)], 5 + part)
+            for part in range(2)
+        ]
+        self.staged.append(self.keep(out_rows, self.out_s, 7))
+        self.staged.append(self.keep(down_rows, self.down_s, 8))
 
     def lanes(self, peer, part):
         head = peer * 4 + self.c
@@ -392,10 +430,11 @@
             for part in range(3):
                 self.copy(self.lanes(peer, part), self.put(part), k, self.f, {"fsdp": peer}).start()
         self.own_mix = [self.keep(self.lanes(self.f, part), self.put(part), 2 + part) for part in range(3)]
-        out_rows = self.out.at[0, pl.ds(pl.multiple_of(self.c * HEAD, HEAD), HEAD)]
-        down_rows = self.down.at[0, pl.ds(pl.multiple_of(self.c * self.units, self.units), self.units)]
-        self.own_out = self.keep(out_rows, self.w_out.at[self.s], 7)
-        self.own_down = self.keep(down_rows, self.w_down.at[self.s], 8)
+        for one in self.staged:
+            one.wait()
+        self.own_gate = self.keep(self.gate_s, self.slab(self.w_gate, self.f), 5)
+        self.own_out = self.keep(self.out_s, self.w_out.at[self.s], 7)
+        self.own_down = self.keep(self.down_s, self.w_down.at[self.s], 8)
         mine = self.w_gains.at[self.s, :, pl.ds(pl.multiple_of(self.f * self.depth, self.depth), self.depth)]
         for k, peer in enumerate(self.peers):
             self.go(self.gains, mine, 20 + k, 16 + 4 * self.s + self.f, {"fsdp": peer})
@@ -416,16 +455,8 @@
             for part in range(2):
                 self.copy(self.gate_piece(peer, part), self.gate_put(part), 3 + k, 4 + self.f, {"fsdp": peer}).start()
 
-    def keep_gate(self):
-        self.own_gate = [self.keep(self.gate_piece(self.f, part), self.gate_put(part), 5 + part) for part in range(2)]
-
     def slab(self, ref, origin):
         return ref.at[self.s, pl.ds(pl.multiple_of(origin * self.depth, self.depth), self.depth)]
-
-    def cross_own(self, ref, copies, slot, base):
-        for one in copies:
-            one.wait()
-        self.go(self.slab(ref, self.f), self.slab(ref, self.f), slot, base + self.f, {"section": self.other})
 
     def cross_slab(self, ref, k, slot, arrival, base):
         origin = lax.rem(self.f + 3 - k, 4)
@@ -434,24 +465,26 @@
         self.go(block, block, slot + k, base + origin, {"section": self.other})
 
     def cross_mix(self):
-        self.cross_own(self.w_mix, self.own_mix, 6, 8)
+        for one in self.own_mix:
+            one.wait()
+        self.go(self.slab(self.w_mix, self.f), self.slab(self.w_mix, self.f), 6, 8 + self.f, {"section": self.other})
         for k in range(3):
             self.cross_slab(self.w_mix, k, 7, 0, 8)
-        self.own_out.wait()
-        self.go(self.w_out.at[self.s], self.w_out.at[self.s], 10, 24, {"section": self.other})
-        self.cross_own(self.w_gate, self.own_gate, 11, 12)
+        self.send_gate()
+        self.go(self.out_s, self.w_out.at[self.s], 10, 24, {"section": self.other})
+        self.go(self.gate_s, self.slab(self.w_gate, self.f), 11, 12 + self.f, {"section": self.other})
 
     def cross_gate(self):
         for k in range(3):
             self.cross_slab(self.w_gate, k, 12, 4, 12)
-        self.own_down.wait()
-        self.go(self.w_down.at[self.s], self.w_down.at[self.s], 15, 25, {"section": self.other})
+        self.go(self.down_s, self.w_down.at[self.s], 15, 25, {"section": self.other})
 
     def there(self, ref, arrival):
         self.copy(ref, ref, 0, arrival, {"section": self.other}).wait_recv()
 
     def mix_there(self):
-        self.own_gains.wait()
+        for one in (self.own_gains, self.own_gate, self.own_out, self.own_down):
+            one.wait()
         for origin in range(4):
             rows = pl.ds(origin * self.depth, self.depth)
             self.there(self.w_mix.at[self.other, rows], 8 + origin)
@@ -506,7 +539,7 @@
     f = lax.axis_index("fsdp")
     rows = x_own.shape[0]
     units = down_v.shape[0]
-    own_rows = pl.ds(pl.multiple_of((c * 4 + f) * rows, rows), rows)
+    own_rows = pl.ds(pl.multiple_of(own_block(c, f) * rows, rows), rows)
     loads = Loads(local)
     saves = Loads(save)
     load_x = loads.start(x_own, x_v.at[own_rows])
@@ -544,12 +577,10 @@
         gather_rows(x_v, rows, send_a, recv_a, project)
     else:
         share.load()
-        share.keep_gate()
         greet_more(share.greeted())
         load_x.wait()
         share.send_mix()
         gather_rows(x_v, rows, send_a, recv_a, started=share.cross_mix)
-        share.send_gate()
         share.mix_there()
         first = load_first()
         for one in first:
@@ -634,7 +665,7 @@
     kept, refs = refs[:10], refs[10:]
     weights, refs = refs[:5], refs[5:]
     scratch, refs = refs[:21], refs[21:]
-    packing, refs = refs[:2], refs[2:]
+    packing, refs = refs[:5], refs[5:]
     sems, share_sems = refs[:10], refs[10:]
     share = Share(sources, weights, packing, share_sems)
     forward_body(0, share, x_own, weights, tables, kept, scratch, sems)
@@ -654,7 +685,7 @@
     odd = lax.rem(c, 2)
     rows = grad_own.shape[0]
     units = down_v.shape[0]
-    own_rows = pl.ds(pl.multiple_of((c * 4 + f) * rows, rows), rows)
+    own_rows = pl.ds(pl.multiple_of(own_block(c, f) * rows, rows), rows)
     loads = Loads(local)
     saves = Loads(save)
     load_grad = loads.start(grad_own, grad_v.at[own_rows])
@@ -682,8 +713,8 @@
     load_down.wait()
     load_both.wait()
     if returning is not None:
-        begin_feed, begin_mix, feed_steps, mix_steps, sum_gains, along_line = returning
-        steps = feed_steps()
+        begin_old, begin_feed, begin_mix, finish = returning
+        begin_old()
 
     def feed(d):
         here = plane_rows(d, rows)
@@ -770,36 +801,34 @@
 
     def mix_weights():
         out_grad_v[...] = kernel_dot_tn(context_v[...], low_v[...])[:HEAD].astype(BF)
-        mix_grad_v[0] = kernel_dot_tn(normed_v[...], mixed_v[:, :LANES]).astype(BF)
+        half = HEAD // 2
+        columns = kernel_dot_tn(mixed_v[:, :LANES], normed_v[...])
+        mix_grad_v[:half, :] = columns[:half].astype(BF)
+        mix_grad_v[half:HEAD, :] = columns[SPAN : SPAN + half].astype(BF)
         pair_copy(1).wait_recv()
         mine = jnp.where(odd == 0, mixed_v[:, LANES : 2 * LANES].astype(F32), mixed_v[:, 2 * LANES :].astype(F32))
         kv_v[...] = (mine + kv_land[...].astype(F32)).astype(BF)
-        mix_grad_v[1] = kernel_dot_tn(normed_v[...], kv_v[...]).astype(BF)
+        columns = kernel_dot_tn(kv_v[...], normed_v[...])
+        mix_grad_v[HEAD : HEAD + half, :] = columns[:half].astype(BF)
+        mix_grad_v[HEAD + half :, :] = jnp.where(
+            odd == 0, columns[SPAN : SPAN + half], columns[half:HEAD]
+        ).astype(BF)
         if returning is None:
             saves.start(out_grad_v, outs[3])
             saves.start(mix_grad_v, outs[1])
         else:
             begin_mix()
 
-    def next_step():
-        if returning is not None:
-            next(steps)()
-
-    scatter_sum(part_v, total_v, land_b, send_d, recv_d, spread_two, mix_weights, next_step)
+    scatter_sum(part_v, total_v, land_b, send_d, recv_d, spread_two, mix_weights)
     start_grad = norm_grads(total_v[...], x_v[...].astype(F32), gains_v[0:1, :].astype(F32), 0) + middle_v[...]
     start_v[...] = start_grad
-    saves.start(start_v, outs[0])
     if returning is None:
+        saves.start(start_v, outs[0])
         start_low_v[...] = start_grad.astype(BF)
         saves.start(start_low_v, outs[6])
         saves.start(gain_grad_v, outs[5])
     else:
-        for step in steps:
-            step()
-        for step in mix_steps():
-            step()
-        sum_gains(gain_grad_v)
-        along_line()
+        finish(gain_grad_v)
     pair_copy(1).wait_send()
     for one in saves.copies:
         one.wait()
@@ -824,28 +853,52 @@
     weights, refs = refs[:5], refs[5:]
     tables, refs = refs[:4], refs[4:]
     saved, refs = refs[:SAVED], refs[SAVED:]
-    (mix_old, gate_old, out_old, down_old, gain_old), refs = refs[:5], refs[5:]
-    outs, refs = refs[:1], refs[1:]
+    (start_old, mix_old, gate_old, out_old, down_old, gain_old), refs = refs[:6], refs[6:]
+    (result_new, result_old), refs = refs[:2], refs[2:]
+    (results_o, starts_o), refs = refs[:2], refs[2:]
     finals, refs = refs[:5], refs[5:]
     scratch, refs = refs[:BACK_SCRATCH], refs[BACK_SCRATCH:]
     own, refs = refs[:10], refs[10:]
-    sems, return_sems = refs[:11], refs[11:]
+    sems, return_sems, swap_sems = refs[:11], refs[11:16], refs[16]
+    start_new = scratch[19]
     mix_new, gate_new, out_new, down_new, gain_new = scratch[21:26]
     gain_v = own[8]
-    *steps, sum_gains, along_line = returner(
+    s = lax.axis_index("section")
+    begin_old, begin_feed, begin_mix, steps_after, wait_all = returner(
         tuple(finals) + tuple(own), return_sems,
         gate_new, down_new, mix_new, out_new, gate_old, down_old, mix_old, out_old,
     )
 
-    def all_gains(gain_grad_v):
+    def swap_copy(src, dst, slot):
+        return pltpu.make_async_remote_copy(
+            src, dst, swap_sems.at[slot], swap_sems.at[2 + slot], device_id={"section": 1 - s}, device_id_type=MESH
+        )
+
+    def swap_rows(away, home, out, slot):
+        swap_copy(away, out.at[s], slot).start()
+        pltpu.make_async_copy(home, out.at[s], swap_sems.at[4 + slot]).start()
+
+    def finish(gain_grad_v):
+        @pl.when(s == 0)
+        def _():
+            swap_rows(result_old, result_new, results_o, 0)
+            swap_rows(start_old, start_new, starts_o, 1)
+
+        @pl.when(s == 1)
+        def _():
+            swap_rows(result_new, result_old, results_o, 0)
+            swap_rows(start_new, start_old, starts_o, 1)
+
         gain_v[0] = jnp.zeros(gain_v.shape[1:], F32)
         gain_v[0, 0:2, :] = gain_grad_v[...]
         gain_v[0, 2:4, :] = gain_old[...]
-        sum_gains()
-
-    backward_body(
-        0, grad_own, weights, tables, saved, outs, scratch, sems, tuple(steps) + (all_gains, along_line)
-    )
+        steps_after()
+        wait_all()
+        for slot, out in enumerate((results_o, starts_o)):
+            pltpu.make_async_copy(out.at[s], out.at[s], swap_sems.at[4 + slot]).wait()
+            swap_copy(out.at[s], out.at[1 - s], slot).wait()
+
+    backward_body(0, grad_own, weights, tables, saved, None, scratch, sems, (begin_old, begin_feed, begin_mix, finish))
 
 
 def link_sems():
@@ -880,7 +933,8 @@
     if sharing:
         depth = weights[0].shape[1]
         units = weights[2].shape[2] // 32
-        packing = [low(depth, weights[0].shape[2]), low(depth, 32 * LANES)]
+        packing = [low(depth, weights[0].shape[2]), low(depth, 32 * LANES), low(depth, 2 * units), low(HEAD, width),
+                   low(units, width)]
     else:
         units = weights[3].shape[1]
         packing = []
@@ -892,7 +946,7 @@
     scratch = [low(length, width), low(length, width)] + [low(length, LANES)] * 4 + [
         full(length, LANES), full(rows, width), low(length, width), full(length, 2 * units), low(length, units),
         low(rows, width), low(width, 3 * LANES), low(width, 2 * units), low(LANES, width), low(units, width),
-        low(16, width), low(length, width), low(18, rows, width), low(18, rows, width), full(rows, width)]
+        low(16, width), low(length, width), low(19, rows, width), low(19, rows, width), full(rows, width)]
     outs = kept + shared if sharing else kept
     return pl.pallas_call(
         forward_share_kernel if sharing else functools.partial(forward_kernel, layer),
@@ -905,7 +959,7 @@
     )(x_own, *weights, *tables)
 
 
-def backward_call(layer, grad_own, weights, tables, saved, old=()):
+def backward_call(layer, grad_own, weights, tables, saved, old=(), results=()):
     rows, width = grad_own.shape
     length = 16 * rows
     units = weights[3].shape[1]
@@ -913,33 +967,34 @@
     returning = layer == 0
     anywhere = pl.BlockSpec(memory_space=pl.ANY)
     inside = pl.BlockSpec(memory_space=pltpu.VMEM)
-    grads = [low(2, width, LANES), low(2, width, units), low(HEAD, width), low(units, width), full(2, width)]
+    grads = [low(2 * HEAD, width), low(2, width, units), low(HEAD, width), low(units, width), full(2, width)]
     scratch = [low(length, width), low(rows, width), low(length, width)] + [low(length, LANES)] * 4 + [
         full(length, LANES), full(rows, width), low(length, width), full(length, 2 * units), low(length, 2 * units),
         low(length, units), low(length, width), low(length, 3 * LANES), low(length, LANES), low(length, LANES),
         full(length, LANES), full(length, LANES),
         full(rows, width), low(rows, width)] + grads + [
         low(width, 3 * LANES), low(width, 2 * units), low(LANES, width), low(units, width),
-        low(16, width), low(length, width), low(18, rows, width), low(18, rows, width), full(rows, width)]
+        low(16, width), low(length, width), low(19, rows, width), low(19, rows, width), full(rows, width)]
     sems = signals(16, 7, 2) + link_sems()
     if returning:
-        outs = [full(rows, width), low(2, depth, 16 * LANES), low(2, depth, 16 * units), low(4 * HEAD, width),
-                low(4 * units, width), full(8, width)]
-        out_specs = [anywhere] * 5 + [inside]
+        outs = [low(2, rows, width), full(2, rows, width), low(16 * 2 * HEAD, depth), low(2, depth, 16 * units),
+                low(4 * HEAD, width), low(4 * units, width), full(8, width)]
+        out_specs = [anywhere] * 6 + [inside]
         scratch += grads[:4] + grads[:4] + [full(5, 8, width), full(5, 8, width)]
-        sems += signals(5, 23, 23, 50, 40)
+        sems += signals(5, 23, 23, 50, 40, 6)
     else:
         outs = [full(rows, width)] + grads + [low(rows, width)]
         out_specs = [anywhere] * len(outs)
     return pl.pallas_call(
         backward_return_kernel if returning else functools.partial(backward_kernel, layer),
         out_shape=shapes(outs),
-        in_specs=[anywhere] * 6 + [inside] * 4 + [anywhere] * SAVED + ([anywhere] * 4 + [inside] if returning else []),
+        in_specs=[anywhere] * 6 + [inside] * 4 + [anywhere] * SAVED
+        + ([anywhere] * 5 + [inside] + [anywhere] * 2 if returning else []),
         out_specs=out_specs,
         scratch_shapes=rooms(scratch) + sems,
         compiler_params=pltpu.CompilerParams(
             collective_id=2 + layer, has_side_effects=True, vmem_limit_bytes=60 << 20),
-    )(grad_own, *weights, *tables, *saved, *old)
+    )(grad_own, *weights, *tables, *saved, *old, *results)
 
 
 def returner(refs, sems, gate_new, down_new, mix_new, out_new, gate_old, down_old, mix_old, out_old):
@@ -951,7 +1006,7 @@
     f = lax.axis_index("fsdp")
     other = {"section": 1 - s}
     units = down_v.shape[0]
-    depth = mix_out.shape[1]
+    depth = gate_out.shape[1]
     inner = jnp.logical_and(c > 0, c < 3)
     above = jnp.minimum(c + 1, 3)
     below = jnp.maximum(c - 1, 0)
@@ -961,30 +1016,57 @@
             src, dst, send.at[slot], recv.at[arrival], device_id=peer, device_id_type=MESH
         )
 
-    def rows_of(k):
-        return pl.ds(k * depth, depth)
-
-    def cross_feed(gate_away, down_away, gate_home, down_home):
-        copy(down_away, down_x, 8, 8, other).start()
+    def owner_part(owner):
+        return pl.ds(pl.multiple_of(owner * depth, depth), depth)
+
+    def cross_parts(away, theirs, first):
         for k in range(4):
-            copy(gate_away.at[:, rows_of(k)], gate_x.at[:, rows_of(k)], k, k, other).start()
-        pltpu.make_async_copy(down_home, down_v, local.at[0]).start()
-        pltpu.make_async_copy(gate_home, gate_v, local.at[1]).start()
-
-    def cross_mix(mix_away, out_away, mix_home, out_home):
-        copy(out_away, out_x, 9, 9, other).start()
-        for k in range(4):
-            copy(mix_away.at[:, rows_of(k)], mix_x.at[:, rows_of(k)], 4 + k, 4 + k, other).start()
-        pltpu.make_async_copy(out_home, out_v, local.at[2]).start()
-        pltpu.make_async_copy(mix_home, mix_v, local.at[3]).start()
+            owner = lax.rem(f + k, 4)
+            part = owner_part(owner)
+            copy(away.at[:, part], theirs.at[:, part], first + k, first + owner, other).start()
+
+    def cross_whole(away, theirs, slot):
+        copy(away, theirs, slot, slot, other).start()
+
+    def home(src, dst, k):
+        pltpu.make_async_copy(src, dst, local.at[k]).start()
+
+    def begin_old():
+        @pl.when(s == 0)
+        def _():
+            cross_whole(down_old, down_x, 8)
+            cross_parts(gate_old, gate_x, 0)
+            cross_whole(out_old, out_x, 9)
+            cross_parts(mix_old, mix_x, 4)
+
+        @pl.when(s == 1)
+        def _():
+            home(down_old, down_v, 0)
+            home(gate_old, gate_v, 1)
+            home(out_old, out_v, 2)
+            home(mix_old, mix_v, 3)
 
     def begin_feed():
-        pl.when(s == 0)(lambda: cross_feed(gate_old, down_old, gate_new, down_new))
-        pl.when(s == 1)(lambda: cross_feed(gate_new, down_new, gate_old, down_old))
+        @pl.when(s == 0)
+        def _():
+            home(down_new, down_v, 0)
+            home(gate_new, gate_v, 1)
+
+        @pl.when(s == 1)
+        def _():
+            cross_whole(down_new, down_x, 8)
+            cross_parts(gate_new, gate_x, 0)
 
     def begin_mix():
-        pl.when(s == 0)(lambda: cross_mix(mix_old, out_old, mix_new, out_new))
-        pl.when(s == 1)(lambda: cross_mix(mix_new, out_new, mix_old, out_old))
+        @pl.when(s == 0)
+        def _():
+            home(out_new, out_v, 2)
+            home(mix_new, mix_v, 3)
+
+        @pl.when(s == 1)
+        def _():
+            cross_whole(out_new, out_x, 9)
+            cross_parts(mix_new, mix_x, 4)
 
     def home_wait(k, dst):
         pltpu.make_async_copy(dst, dst, local.at[k]).wait()
@@ -996,13 +1078,16 @@
         return gate_out.at[:, :, pl.ds(pl.multiple_of((ff * 4 + cc) * units, units), units)]
 
     def mix_at(cc, ff):
-        return mix_out.at[:, :, pl.ds(pl.multiple_of((ff * 4 + cc) * LANES, LANES), LANES)]
+        return mix_out.at[pl.ds(pl.multiple_of((ff * 4 + cc) * 2 * HEAD, 2 * HEAD), 2 * HEAD)]
+
+    def rows_at(ref, cc, count):
+        return ref.at[pl.ds(pl.multiple_of(cc * count, count), count)]
 
     def out_at(cc, ff):
-        return out_out.at[pl.ds(pl.multiple_of(cc * HEAD, HEAD), HEAD)]
+        return rows_at(out_out, cc, HEAD)
 
     def down_at(cc, ff):
-        return down_out.at[pl.ds(pl.multiple_of(cc * units, units), units)]
+        return rows_at(down_out, cc, units)
 
     origins = [lax.rem(f + k, 4) for k in (0, 3, 2, 1)]
     items = [(down_at, f)] + [(gate_at, one) for one in origins] + [(out_at, f)] + [(mix_at, one) for one in origins]
@@ -1035,7 +1120,7 @@
 
     def to_owner(k, mine, theirs, place, arrival_x, arrival_y, slot, index):
         owner = lax.rem(f + k, 4)
-        rows = pl.ds(pl.multiple_of(owner * depth, depth), depth)
+        rows = owner_part(owner)
         fold(mine.at[:, rows], theirs.at[:, rows], arrival_x + owner)
         if k:
             copy(mine.at[:, rows], place(c, f), slot + k, arrival_y + f, {"fsdp": owner}).start()
@@ -1047,101 +1132,130 @@
         arrived(place(c, origins[k]), arrival + origins[k])
         start_line(index)
 
-    def feed_steps():
-        yield lambda: whole_item(0, down_v, down_x, 8, down_at, 0)
-
-        def first():
-            home_wait(1, gate_v)
-            to_owner(1, gate_v, gate_x, gate_at, 0, 10, 10, 1)
-
-        yield first
-        for k in (2, 3, 0):
-            yield functools.partial(to_owner, k, gate_v, gate_x, gate_at, 0, 10, 10, 1)
-        for k in range(1, 4):
-            yield functools.partial(from_owner, k, gate_at, 10, 1 + k)
-
-    def mix_steps():
-        yield lambda: whole_item(2, out_v, out_x, 9, out_at, 5)
-
-        def first():
-            home_wait(3, mix_v)
-            to_owner(1, mix_v, mix_x, mix_at, 4, 14, 14, 6)
-
-        yield first
-        for k in (2, 3, 0):
-            yield functools.partial(to_owner, k, mix_v, mix_x, mix_at, 4, 14, 14, 6)
-        for k in range(1, 4):
-            yield functools.partial(from_owner, k, mix_at, 14, 6 + k)
-
-    def sum_gains():
-        targets = [other, {"fsdp": f + 1 - 2 * lax.rem(f, 2)}, {"fsdp": f + 2 - 4 * (f // 2)},
-                   {"ctx": c + 1 - 2 * lax.rem(c, 2)}, {"ctx": lax.rem(c + 2, 4)}]
-        copies = []
-        for k, target in enumerate(targets):
-            one = copy(gain_v.at[k], gain_x.at[k], 18 + k, 18 + k, target)
-            one.start()
-            one.wait_recv()
-            copies.append(one)
-            if k < 4:
-                gain_v[k + 1] = gain_v[k] + gain_x[k]
-            else:
-                gain_out[...] = gain_v[k] + gain_x[k]
-        for one in copies:
-            one.wait_send()
-
-    def along_line():
-        order = near_order(c)
-        forwards = []
-        for step in range(1, 4):
-            d = order[step]
-            for index in range(10):
-                one = line(index, d, 20 + (step - 1) * 10 + index, jnp.where(d < c, above, below))
-                one.wait_recv()
-                pl.when(inner)(one.start)
-                forwards.append(one)
+    gain_targets = [other, {"fsdp": f + 1 - 2 * lax.rem(f, 2)}, {"fsdp": f + 2 - 4 * (f // 2)},
+                    {"ctx": c + 1 - 2 * lax.rem(c, 2)}, {"ctx": lax.rem(c + 2, 4)}]
+
+    def gain_copy(k):
+        return copy(gain_v.at[k], gain_x.at[k], 18 + k, 18 + k, gain_targets[k])
+
+    def gain_sum(k):
+        gain_copy(k).wait_recv()
+        if k < 4:
+            gain_v[k + 1] = gain_v[k] + gain_x[k]
+            gain_copy(k + 1).start()
+        else:
+            gain_out[...] = gain_v[k] + gain_x[k]
+
+    order = near_order(c)
+
+    def onward(index, step):
+        d = order[step]
+        return line(index, d, 20 + (step - 1) * 10 + index, jnp.where(d < c, above, below))
+
+    def pass_on(index, step):
+        one = onward(index, step)
+        one.wait_recv()
+        pl.when(inner)(one.start)
+
+    def near(index):
+        pass_on(index, 1)
+        pl.when(inner)(lambda: pass_on(index, 2))
+
+    def far(index):
+        pl.when(jnp.logical_not(inner))(lambda: pass_on(index, 2))
+        pass_on(index, 3)
+
+    def gate_first():
+        home_wait(1, gate_v)
+        to_owner(0, gate_v, gate_x, gate_at, 0, 10, 10, 1)
+
+    def gate_rest(k):
+        return lambda: to_owner(k, gate_v, gate_x, gate_at, 0, 10, 10, 1)
+
+    def gate_from(k):
+        return lambda: from_owner(k, gate_at, 10, 1 + k)
+
+    def mix_first():
+        home_wait(3, mix_v)
+        to_owner(0, mix_v, mix_x, mix_at, 4, 14, 14, 6)
+
+    def mix_rest(k):
+        return lambda: to_owner(k, mix_v, mix_x, mix_at, 4, 14, 14, 6)
+
+    def mix_from(k):
+        return lambda: from_owner(k, mix_at, 14, 6 + k)
+
+    def down_first():
+        whole_item(0, down_v, down_x, 8, down_at, 0)
+
+    def out_first():
+        whole_item(2, out_v, out_x, 9, out_at, 5)
+
+    def passing(*steps):
+        return [functools.partial(near if sign > 0 else far, abs(sign) - 1) for sign in steps]
+
+    after = [
+        [down_first, gate_first, gate_rest(1), gate_rest(2), gate_rest(3)],
+        passing(1) + [gate_from(1), gate_from(2), gate_from(3), out_first, mix_first, mix_rest(1), mix_rest(2), mix_rest(3)],
+        passing(2, -1, 3, -2, 4) + [mix_from(1), mix_from(2), mix_from(3)],
+        passing(-3, 5, -4, 6, -5, 7),
+        passing(-6, 8, -7, 9, -8, 10, -9, -10),
+    ]
+    def steps_after():
+        gain_copy(0).start()
+        for k, steps in enumerate(after):
+            for step in steps:
+                step()
+            gain_sum(k)
+
+    def wait_all():
         for index in range(10):
             pl.when(c < 3)(line(index, c, index, above).wait_send)
             pl.when(c > 0)(line(index, c, 10 + index, below).wait_send)
-        for one in forwards:
-            pl.when(inner)(one.wait_send)
+            for step in range(1, 4):
+                pl.when(inner)(onward(index, step).wait_send)
+        for k in range(5):
+            gain_copy(k).wait_send()
         for k in range(4):
-            gate_rows = gate_x.at[:, rows_of(k)]
-            mix_rows = mix_x.at[:, rows_of(k)]
-            copy(gate_rows, gate_rows, k, 0, other).wait_send()
-            copy(mix_rows, mix_rows, 4 + k, 0, other).wait_send()
-            if k:
-                copy(gate_rows, gate_rows, 10 + k, 0, other).wait_send()
-                copy(mix_rows, mix_rows, 14 + k, 0, other).wait_send()
+            gate_part = gate_x.at[:, pl.ds(k * depth, depth)]
+            mix_part = mix_x.at[:, pl.ds(k * depth, depth)]
+            for slot in (k, 10 + k) if k else (k,):
+                copy(gate_part, gate_part, slot, 0, other).wait_send()
+                copy(mix_part, mix_part, 4 + slot, 0, other).wait_send()
         copy(down_x, down_x, 8, 0, other).wait_send()
         copy(out_x, out_x, 9, 0, other).wait_send()
 
-    return begin_feed, begin_mix, feed_steps, mix_steps, sum_gains, along_line
-
-
-def widen_kernel(mix, gate, out, down, mix_f, gate_f, out_f, down_f):
-    rows = mix.shape[1]
-
-    def choice(count, wanted):
-        lane = lax.broadcasted_iota(jnp.int32, (count, 4 * HEAD), 0)
-        column = lax.broadcasted_iota(jnp.int32, (count, 4 * HEAD), 1)
-        return jnp.where(lane == wanted(column // HEAD, lax.rem(column, HEAD)), 1.0, 0.0).astype(BF)
-
-    def halves(place):
-        half = place // (HEAD // 2)
-        return half * SPAN + place - half * (HEAD // 2)
-
-    queries = choice(4 * LANES, lambda head, place: head * LANES + halves(place))
-    keys = choice(8 * LANES, lambda head, place: 2 * head * LANES + halves(place))
-    values = choice(8 * LANES, lambda head, place: (2 * head + 1) * LANES + place)
-    width = 4 * 4 * HEAD
-    for g in range(4):
-        mix_f[:, g * 4 * HEAD : (g + 1) * 4 * HEAD] = kernel_dot(mix[0, :, g * 4 * LANES : (g + 1) * 4 * LANES], queries)
-    for g in range(2):
-        slots = mix[1, :, g * 8 * LANES : (g + 1) * 8 * LANES]
-        at = width + g * 4 * HEAD
-        mix_f[:, at : at + 4 * HEAD] = kernel_dot(slots, keys)
-        at = width + (g + 2) * 4 * HEAD
-        mix_f[:, at : at + 4 * HEAD] = kernel_dot(slots, values)
+    return begin_old, begin_feed, begin_mix, steps_after, wait_all
+
+
+def widen_kernel(mix, gate, out, down, mix_f, gate_f, out_f, down_f, places, turned):
+    step = pl.program_id(0)
+    rows = gate.shape[1]
+    four = 4 * HEAD
+    width = 4 * four
+
+    @pl.when(step == 0)
+    def _():
+        source = lax.broadcasted_iota(jnp.int32, (2 * four, 2 * four), 0)
+        column = lax.broadcasted_iota(jnp.int32, (2 * four, 2 * four), 1)
+        query = (column // HEAD) * 2 * HEAD + lax.rem(column, HEAD)
+        rest = column - four
+        kind = rest // (2 * HEAD)
+        rest = rest - kind * 2 * HEAD
+        other = (2 * (rest // HEAD) + kind) * 2 * HEAD + HEAD + lax.rem(rest, HEAD)
+        places[...] = jnp.where(source == jnp.where(column < four, query, other), 1.0, 0.0).astype(BF)
+        groups = [kernel_dot_tn(mix[g * 2 * four : (g + 1) * 2 * four, :], places[...]) for g in range(4)]
+        for g in range(4):
+            turned[:, g * four : (g + 1) * four] = groups[g][:, :four]
+        for g in range(2):
+            for kind in range(2):
+                at = width + kind * 2 * four + g * four
+                low_part = four + kind * 2 * HEAD
+                turned[:, at : at + four] = jnp.concatenate(
+                    [groups[2 * g + k][:, low_part : low_part + 2 * HEAD] for k in range(2)], axis=1
+                )
+
+    mix_f[...] = turned[pl.ds(pl.multiple_of(step * rows, rows), rows), :]
     half = gate.shape[2]
     gate_f[:, :half] = gate[0].astype(F32)
     gate_f[:, half:] = gate[1].astype(F32)
@@ -1151,31 +1265,29 @@
 
 def widen_call(mix, gate, out, down):
     steps = 8
-    depth = mix.shape[1]
+    depth = gate.shape[1]
     width = out.shape[1]
     rows = depth // steps
     down_rows = down.shape[0] // steps
     return pl.pallas_call(
         widen_kernel,
         grid=(steps,),
-        out_shape=(
-            jax.ShapeDtypeStruct((depth, 2 * width), F32),
-            jax.ShapeDtypeStruct((depth, 2 * gate.shape[2]), F32),
-            jax.ShapeDtypeStruct(out.shape, F32),
-            jax.ShapeDtypeStruct(down.shape, F32),
-        ),
+        out_shape=shapes([
+            full(depth, 2 * width), full(depth, 2 * gate.shape[2]), full(*out.shape), full(*down.shape)
+        ]),
         in_specs=[
-            pl.BlockSpec((2, rows, mix.shape[2]), lambda i: (0, i, 0)),
+            pl.BlockSpec(mix.shape, lambda i: (0, 0)),
             pl.BlockSpec((2, rows, gate.shape[2]), lambda i: (0, i, 0)),
             pl.BlockSpec((rows, width), lambda i: (i, 0)),
             pl.BlockSpec((down_rows, width), lambda i: (i, 0)),
         ],
-        out_specs=(
+        out_specs=[
             pl.BlockSpec((rows, 2 * width), lambda i: (i, 0)),
             pl.BlockSpec((rows, 2 * gate.shape[2]), lambda i: (i, 0)),
             pl.BlockSpec((rows, width), lambda i: (i, 0)),
             pl.BlockSpec((down_rows, width), lambda i: (i, 0)),
-        ),
+        ],
+        scratch_shapes=rooms([low(8 * HEAD, 8 * HEAD), full(depth, 2 * width)]),
         compiler_params=pltpu.CompilerParams(vmem_limit_bytes=48 << 20),
     )(mix, gate, out, down)
 
@@ -1465,6 +1577,8 @@
         return jnp.where(first, own, other), jnp.where(first, other, own)
 
     order = pick(block_order, section, 0)
+    if on_line():
+        order = jnp.swapaxes(order.reshape(C, F // 2, 2), 1, 2).reshape(C * F)
     positions = (order[:, None] * rows + jnp.arange(rows, dtype=jnp.int32)[None, :]).reshape(length)
     part_rows = length // plan.share
     part_positions = lax.dynamic_slice_in_dim(positions, plan.part * part_rows, part_rows, 0)
@@ -1488,7 +1602,9 @@
         second = forward_call(1, first[9], weights, common)
         results.append(second[9])
         input_grads[1], *old, grad = backward_call(1, grad, weights, common, [first[9], *second[:9]])
-        input_grads[0], *wide, gain_sum = backward_call(0, grad, weights, common, [x, *first[:9]], old)
+        section_outputs, section_input_grads, *wide, gain_sum = backward_call(
+            0, grad, weights, common, [x, *first[:9]], [input_grads[1], *old], results
+        )
         mix_grad, gate_up_grad, out_grad, down_grad = widen_call(*wide)
         gain_sum = own_gain_sums(plan, section, gain_sum, depth)
     else:
@@ -1504,18 +1620,18 @@
                 plan, grad, weights[s], gains[s], kept[s], positions, part_positions, tables, part_tables
             )
             grad = input_grads[s].astype(BF)
+        def mine_and_theirs(first, second):
+            return jnp.where(section == 0, first, second), jnp.where(section == 0, second, first)
+
+        def by_batch(first, second):
+            own, away = mine_and_theirs(first, second)
+            return jnp.stack(by_layer(own, swap_sections(away)))
+
+        section_outputs = by_batch(*results)
+        section_input_grads = by_batch(*input_grads)
+
         shard_grads = returned_grads(plan, section, weight_grads, gain_grads, depth)
         mix_grad, gate_up_grad, out_grad, down_grad, gain_sum = shard_grads
-
-    def mine_and_theirs(first, second):
-        return jnp.where(section == 0, first, second), jnp.where(section == 0, second, first)
-
-    def by_batch(first, second):
-        own, away = mine_and_theirs(first, second)
-        return jnp.stack(by_layer(own, swap_sections(away)))
-
-    section_outputs = by_batch(*results)
-    section_input_grads = by_batch(*input_grads)
 
     return (
         section_outputs[None],

time: 708 us -> 679 us (0.959)
  Pallas kernels: 678 us -> 654 us
    pallas_call x2, Pallas kernels: 431 us -> 413 us  [backward_call(): pl.pallas_call(backward_return_kernel if returning else functools.partial...]
  transfers between devices with their start and end apart: 2 -> 0, of which waited for: 0 -> 0; matrix products, arithmetic and copies ran while one was open for 0% -> 0% of each run, Pallas kernels for 64% -> 0%
where the time goes in v4:
time: 679 us; the launch traced here: 670 us
  Pallas kernels  654 us (96%)
  local copies, waits for them, and re-layouts  10.1 us (1%)
    pallas_call x2, Pallas kernels, backward_call(): pl.pallas_call(backward_return_kernel if returning else functools.partial...  413 us
    pallas_call x2, Pallas kernels, forward_call(): pl.pallas_call(forward_share_kernel if sharing else functools.partial(for...  226 us
    pallas_call x1, Pallas kernels, widen_call(): pl.pallas_call(widen_kernel, grid=(steps,), out_shape=shapes([full(depth,...  14.9 us

profile of v4, /device:TPU:0, one launch (start us, length us, event | category | flops | bytes accessed | tf_op | source)
XLA Modules:
  0.0 670.2 jit_solution(6840170306025126872)
XLA Ops:
  0.6 0.7 fusion.6
  1.4 0.1 mul.36
  1.5 0.1 copy.18
  1.6 0.1 mul.38
  1.7 1.3 fusion.3.refs_5_
  3.0 0.1 iota_add_fusion
  3.0 0.1 convert_element_type.15
  3.1 0.7 add.62.refs_9_
  3.8 1.8 dynamic-slice_bitcast_fusion
  5.6 1.3 add.65.refs_8_
  6.8 1.9 fusion
  8.7 1.3 pad_maximum_fusion
  10.0 132.7 %shard_map.152 = (bf16[1024,1536]{1,0:T(8,128)(2,1)}, bf16[1024,128]{1,0:T(8,128)(2,1)}, bf16[1024,128]{1,0:T(8,128)(2,1)}, bf16[1024,128]{1,0:T(8,128)(2,1)}, b...) custom-call(bf16[64,1536]{1,0:T(8,128)(2,1)} %get-tuple-element.101., ...), custom_call_target="tpu_custom_call" | custom-call | tf_op jit(solution)/shard_map/pallas_call | solution.py:951
  142.8 93.0 %shard_map.153 = (bf16[1024,1536]{1,0:T(8,128)(2,1)}, bf16[1024,128]{1,0:T(8,128)(2,1)}, bf16[1024,128]{1,0:T(8,128)(2,1)}, bf16[1024,128]{1,0:T(8,128)(2,1)}, b...) custom-call(bf16[64,1536]{1,0:T(8,128)(2,1)} %get-tuple-element.56.r, ...), custom_call_target="tpu_custom_call" | custom-call | tf_op jit(solution)/shard_map/pallas_call | solution.py:951
  235.8 98.2 %shard_map.154 = (f32[64,1536]{1,0:T(8,128)}, bf16[192,1536]{1,0:T(8,128)(2,1)}, bf16[2,1536,256]{2,1,0:T(8,128)(2,1)}, bf16[96,1536]{1,0:T(8,128)(2,1)}, bf16[2...) custom-call(bf16[64,1536]{1,0:T(8,128)(2,1)} %get-tuple-element.102.refs_0_, ...), custom_call_target="tpu_custom_call" | custom-call | tf_op jit(solution)/shard_map/pallas_call | solution.py:988
  334.0 314.8 %shard_map.155 = (bf16[2,64,1536]{2,1,0:T(8,128)(2,1)}, f32[2,64,1536]{2,1,0:T(8,128)}, bf16[3072,384]{1,0:T(8,128)(2,1)}, bf16[2,384,4096]{2,1,0:T(8,128)(2,1)}...) custom-call(bf16[64,1536]{1,0:T(8,128)(2,1)} %get-tuple-element.66.refs_0_, ...), custom_call_target="tpu_custom_call" | custom-call | tf_op jit(solution)/shard_map/pallas_call | solution.py:988
  648.8 1.5 fusion.7
  650.2 1.7 copy-done
  651.9 1.3 copy-done.1
  653.2 14.9 %shard_map.156 = (f32[384,3072]{1,0:T(8,128)}, f32[384,8192]{1,0:T(8,128)}, f32[384,1536]{1,0:T(8,128)}, f32[1024,1536]{1,0:T(8,128)}) custom-call(bf16[3072,384]{1,0:T(8,128)(2,1)S(1)} %copy-done, bf16[2,384,4096]{2,1,0:T(8,128)(2,1)} %get-tuple-element.87.gate, bf16[384,1536]{1,0:T(8,128)(2,1)S(1)} %copy-done.1, bf16[1024,1536]{1,0:T(8,128)(2,1)} %get-tuple-element.89.down), custom_call_target="tpu_custom_call" | custom-call | tf_op jit(solution)/shard_map/pallas_call | solution.py:1272
  668.1 0.0 copy-done.3
  668.1 0.7 copy.25
  668.9 0.0 copy-done.2
  668.9 0.9 copy.26
  (6 shorter events, 0.0 us)
Async XLA Ops:
  650.2 1.7 copy-start
  651.9 1.3 copy-start.1
  653.2 14.9 %copy-start.3 = (bf16[2,64,1536]{2,1,0:T(8,128)(2,1)S(1)}, bf16[2,64,1536]{2,1,0:T(8,128)(2,1)}, u32[]{:S(2)}) copy-start(bf16[2,64,1536]{2,1,0:T(8,128)(2,1)} %get-tuple-element.83) | copy-start | bytes 1179652
  653.2 15.7 %copy-start.2 = (f32[2,64,1536]{2,1,0:T(8,128)S(1)}, f32[2,64,1536]{2,1,0:T(8,128)}, u32[]{:S(2)}) copy-start(f32[2,64,1536]{2,1,0:T(8,128)} %get-tuple-element.84) | copy-start | bytes 2359300

commit v5 on v4

--- a/solution.py
+++ b/solution.py
@@ -2,6 +2,7 @@
 
 import jax
 import jax.numpy as jnp
+import numpy as np
 from jax import lax
 from jax.experimental import pallas as pl
 from jax.experimental.pallas import tpu as pltpu
@@ -164,7 +165,7 @@
 GATHER_RECVS = 18
 
 
-def scatter_sum(part, total, land, send, recv, produce=None, meanwhile=None):
+def scatter_sum(part, total, land, send, recv, produce=None, meanwhile=None, ending=None):
     c = lax.axis_index("ctx")
     f = lax.axis_index("fsdp")
     y = f // 2
@@ -274,6 +275,8 @@
     over(3, 1)
     onward(2, 1, True)
     onward(2, 0)
+    if ending is not None:
+        ending()
     for h in range(2):
         onward(3, h, h == 0)
 
@@ -365,9 +368,9 @@
 
 class Share:
     def __init__(self, sources, targets, scratch, sems):
-        self.mix, self.out, self.gate_up, self.down, self.gains = sources
+        self.mix, self.out, self.gate_up, self.down, self.attention_gain, self.feed_gain = sources
         self.w_mix, self.w_gate, self.w_out, self.w_down, self.w_gains = targets
-        self.mix_v, self.heads_v, self.gate_s, self.out_s, self.down_s = scratch
+        self.mix_v, self.heads_v, self.gate_s, self.out_s, self.down_s, self.gains = scratch
         self.local, self.send, self.recv = sems
         self.s = lax.axis_index("section")
         self.c = lax.axis_index("ctx")
@@ -402,6 +405,9 @@
         return one
 
     def load(self):
+        self.gains[...] = jnp.zeros_like(self.gains)
+        self.gains[0:1, :] = self.attention_gain[...]
+        self.gains[1:2, :] = self.feed_gain[...]
         self.loaded = self.keep(self.mix.at[0], self.mix_v, 0)
         out_rows = self.out.at[0, pl.ds(pl.multiple_of(self.c * HEAD, HEAD), HEAD)]
         down_rows = self.down.at[0, pl.ds(pl.multiple_of(self.c * self.units, self.units), self.units)]
@@ -464,10 +470,11 @@
         self.copy(block, block, 0, arrival + origin, {"fsdp": origin}).wait_recv()
         self.go(block, block, slot + k, base + origin, {"section": self.other})
 
-    def cross_mix(self):
+    def cross_mix(self, between):
         for one in self.own_mix:
             one.wait()
         self.go(self.slab(self.w_mix, self.f), self.slab(self.w_mix, self.f), 6, 8 + self.f, {"section": self.other})
+        between()
         for k in range(3):
             self.cross_slab(self.w_mix, k, 7, 0, 8)
         self.send_gate()
@@ -528,7 +535,32 @@
     return pl.ds(pl.multiple_of(d * 4 * rows, 4 * rows), 4 * rows)
 
 
-def forward_body(layer, share, x_own, weights, tables, kept, scratch, sems):
+def make_tables(block_order, frequency, cosine, sine, place_col, place_row):
+    s = lax.axis_index("section")
+    blocks = block_order.shape[1]
+    rows = place_col.shape[0] // blocks
+    order = jnp.where(s == 0, block_order[0:1, :], block_order[1:2, :])
+    inside_col = lax.broadcasted_iota(jnp.int32, (rows, 1), 0)
+    inside_row = lax.broadcasted_iota(jnp.int32, (1, 2 * rows), 1)
+    firsts = []
+    for b in range(blocks):
+        source = b - b % 4 + (b % 2) * 2 + (b % 4) // 2
+        firsts.append(order[:, source : source + 1] * rows)
+        place_col[b * rows : (b + 1) * rows, :] = firsts[b] + inside_col
+    for b in range(0, blocks, 2):
+        place_row[:, b * rows : (b + 2) * rows] = jnp.where(
+            inside_row < rows, firsts[b] + inside_row, firsts[b + 1] + inside_row - rows
+        )
+    lane = lax.broadcasted_iota(jnp.int32, (4 * rows, LANES), 1)
+    for part in range(blocks // 4):
+        here = pl.ds(part * 4 * rows, 4 * rows)
+        angles = place_col[here, :].astype(F32) * frequency[...]
+        wave = jnp.sin(angles)
+        cosine[here, :] = jnp.cos(angles)
+        sine[here, :] = jnp.where(lane < SPAN, -wave, wave)
+
+
+def forward_body(layer, share, x_own, weights, tables, kept, scratch, sems, prepare=None):
     w_mix, w_gate, w_out, w_down, w_gains = weights
     cosine, sine, place_col, place_row = tables
     normed_o, q_o, k_o, v_o, context_o, log_o, middle_o, normed_two_o, both_o, result_o = kept
@@ -580,7 +612,7 @@
         greet_more(share.greeted())
         load_x.wait()
         share.send_mix()
-        gather_rows(x_v, rows, send_a, recv_a, started=share.cross_mix)
+        gather_rows(x_v, rows, send_a, recv_a, started=lambda: share.cross_mix(prepare))
         share.mix_there()
         first = load_first()
         for one in first:
@@ -659,16 +691,20 @@
 
 
 def forward_share_kernel(*refs):
-    x_own, *refs = refs
-    sources, refs = refs[:5], refs[5:]
-    tables, refs = refs[:4], refs[4:]
+    inputs, *refs = refs
+    sources, refs = refs[:6], refs[6:]
+    (block_order, frequency), refs = refs[:2], refs[2:]
     kept, refs = refs[:10], refs[10:]
     weights, refs = refs[:5], refs[5:]
+    tables, refs = refs[:4], refs[4:]
     scratch, refs = refs[:21], refs[21:]
-    packing, refs = refs[:5], refs[5:]
+    packing, refs = refs[:6], refs[6:]
     sems, share_sems = refs[:10], refs[10:]
     share = Share(sources, weights, packing, share_sems)
-    forward_body(0, share, x_own, weights, tables, kept, scratch, sems)
+    forward_body(
+        0, share, inputs.at[lax.axis_index("section")], weights, tables, kept, scratch, sems,
+        lambda: make_tables(block_order, frequency, *tables),
+    )
 
 
 def backward_body(layer, grad_own, weights, tables, saved, outs, scratch, sems, returning):
@@ -683,7 +719,7 @@
     c = lax.axis_index("ctx")
     f = lax.axis_index("fsdp")
     odd = lax.rem(c, 2)
-    rows = grad_own.shape[0]
+    rows = x_own.shape[0]
     units = down_v.shape[0]
     own_rows = pl.ds(pl.multiple_of(own_block(c, f) * rows, rows), rows)
     loads = Loads(local)
@@ -713,7 +749,7 @@
     load_down.wait()
     load_both.wait()
     if returning is not None:
-        begin_old, begin_feed, begin_mix, finish = returning
+        begin_old, begin_feed, begin_mix, begin_return, finish = returning
         begin_old()
 
     def feed(d):
@@ -819,7 +855,8 @@
         else:
             begin_mix()
 
-    scatter_sum(part_v, total_v, land_b, send_d, recv_d, spread_two, mix_weights)
+    scatter_sum(part_v, total_v, land_b, send_d, recv_d, spread_two, mix_weights,
+                None if returning is None else begin_return)
     start_grad = norm_grads(total_v[...], x_v[...].astype(F32), gains_v[0:1, :].astype(F32), 0) + middle_v[...]
     start_v[...] = start_grad
     if returning is None:
@@ -845,7 +882,7 @@
     saved, refs = refs[:SAVED], refs[SAVED:]
     outs, refs = refs[:7], refs[7:]
     scratch, sems = refs[:BACK_SCRATCH], refs[BACK_SCRATCH:]
-    backward_body(layer, grad_own, weights, tables, saved, outs, scratch, sems, None)
+    backward_body(layer, grad_own.at[lax.axis_index("section")], weights, tables, saved, outs, scratch, sems, None)
 
 
 def backward_return_kernel(*refs):
@@ -864,7 +901,7 @@
     mix_new, gate_new, out_new, down_new, gain_new = scratch[21:26]
     gain_v = own[8]
     s = lax.axis_index("section")
-    begin_old, begin_feed, begin_mix, steps_after, wait_all = returner(
+    begin_old, begin_feed, begin_mix, begin_return, steps_after, wait_all = returner(
         tuple(finals) + tuple(own), return_sems,
         gate_new, down_new, mix_new, out_new, gate_old, down_old, mix_old, out_old,
     )
@@ -898,7 +935,8 @@
             pltpu.make_async_copy(out.at[s], out.at[s], swap_sems.at[4 + slot]).wait()
             swap_copy(out.at[s], out.at[1 - s], slot).wait()
 
-    backward_body(0, grad_own, weights, tables, saved, None, scratch, sems, (begin_old, begin_feed, begin_mix, finish))
+    saved = [saved[0].at[s], *saved[1:]]
+    backward_body(0, grad_own, weights, tables, saved, None, scratch, sems, (begin_old, begin_feed, begin_mix, begin_return, finish))
 
 
 def link_sems():
@@ -926,41 +964,63 @@
     return [pltpu.SemaphoreType.DMA((count,)) for count in counts]
 
 
-def forward_call(layer, x_own, weights, tables):
-    rows, width = x_own.shape
+def forward_scratch(rows, width, units):
     length = 16 * rows
-    sharing = layer == 0
-    if sharing:
-        depth = weights[0].shape[1]
-        units = weights[2].shape[2] // 32
-        packing = [low(depth, weights[0].shape[2]), low(depth, 32 * LANES), low(depth, 2 * units), low(HEAD, width),
-                   low(units, width)]
-    else:
-        units = weights[3].shape[1]
-        packing = []
-    anywhere = pl.BlockSpec(memory_space=pl.ANY)
-    inside = pl.BlockSpec(memory_space=pltpu.VMEM)
-    kept = [low(length, width)] + [low(length, LANES)] * 4 + [
-        full(length, LANES), full(rows, width), low(length, width), full(length, 2 * units), low(rows, width)]
-    shared = [low(2, width, 3 * LANES), low(2, width, 2 * units), low(2, HEAD, width), low(2, units, width), low(2, 16, width)]
-    scratch = [low(length, width), low(length, width)] + [low(length, LANES)] * 4 + [
+    return [low(length, width), low(length, width)] + [low(length, LANES)] * 4 + [
         full(length, LANES), full(rows, width), low(length, width), full(length, 2 * units), low(length, units),
         low(rows, width), low(width, 3 * LANES), low(width, 2 * units), low(LANES, width), low(units, width),
         low(16, width), low(length, width), low(19, rows, width), low(19, rows, width), full(rows, width)]
-    outs = kept + shared if sharing else kept
+
+
+def forward_kept(rows, width, units):
+    length = 16 * rows
+    return [low(length, width)] + [low(length, LANES)] * 4 + [
+        full(length, LANES), full(rows, width), low(length, width), full(length, 2 * units), low(rows, width)]
+
+
+ANYWHERE = pl.BlockSpec(memory_space=pl.ANY)
+INSIDE = pl.BlockSpec(memory_space=pltpu.VMEM)
+
+
+def forward_share_call(inputs, shards, gains, block_order):
+    rows, width = inputs.shape[1:]
+    length = 16 * rows
+    depth = shards[0].shape[1]
+    units = shards[2].shape[2] // 32
+    frequency = np.zeros((2, SPAN), np.float32)
+    frequency[:, : HEAD // 2] = np.float32(rope_base) ** (-(np.arange(HEAD // 2, dtype=np.float32) * 2.0 / HEAD))
+    packing = [low(depth, shards[0].shape[2]), low(depth, 32 * LANES), low(depth, 2 * units), low(HEAD, width),
+               low(units, width), low(16, depth)]
+    kept = forward_kept(rows, width, units)
+    weights = [low(2, width, 3 * LANES), low(2, width, 2 * units), low(2, HEAD, width), low(2, units, width), low(2, 16, width)]
+    tables = [full(length, LANES), full(length, LANES), ((length, 1), jnp.int32), ((1, length), jnp.int32)]
     return pl.pallas_call(
-        forward_share_kernel if sharing else functools.partial(forward_kernel, layer),
-        out_shape=shapes(outs),
-        in_specs=[anywhere] * 6 + [inside] * 4,
-        out_specs=[anywhere] * len(outs),
-        scratch_shapes=rooms(scratch + packing) + signals(6, 10) + link_sems() + (signals(9, 27, 26) if sharing else []),
-        compiler_params=pltpu.CompilerParams(
-            collective_id=layer, has_side_effects=True, vmem_limit_bytes=60 << 20),
+        forward_share_kernel,
+        out_shape=shapes(kept + weights + tables),
+        in_specs=[ANYWHERE] * 5 + [INSIDE] * 4,
+        out_specs=[ANYWHERE] * 15 + [INSIDE] * 4,
+        scratch_shapes=rooms(forward_scratch(rows, width, units) + packing) + signals(6, 10) + link_sems()
+        + signals(9, 27, 26),
+        compiler_params=pltpu.CompilerParams(collective_id=0, has_side_effects=True, vmem_limit_bytes=60 << 20),
+    )(inputs, *shards, *gains, block_order, jnp.asarray(frequency.reshape(1, LANES)))
+
+
+def forward_call(layer, x_own, weights, tables):
+    rows, width = x_own.shape
+    units = weights[3].shape[1]
+    kept = forward_kept(rows, width, units)
+    return pl.pallas_call(
+        functools.partial(forward_kernel, layer),
+        out_shape=shapes(kept),
+        in_specs=[ANYWHERE] * 6 + [INSIDE] * 4,
+        out_specs=[ANYWHERE] * len(kept),
+        scratch_shapes=rooms(forward_scratch(rows, width, units)) + signals(6, 10) + link_sems(),
+        compiler_params=pltpu.CompilerParams(collective_id=layer, has_side_effects=True, vmem_limit_bytes=60 << 20),
     )(x_own, *weights, *tables)
 
 
 def backward_call(layer, grad_own, weights, tables, saved, old=(), results=()):
-    rows, width = grad_own.shape
+    rows, width = grad_own.shape[-2:]
     length = 16 * rows
     units = weights[3].shape[1]
     depth = width // 4
@@ -1195,12 +1255,18 @@
         return [functools.partial(near if sign > 0 else far, abs(sign) - 1) for sign in steps]
 
     after = [
-        [down_first, gate_first, gate_rest(1), gate_rest(2), gate_rest(3)],
         passing(1) + [gate_from(1), gate_from(2), gate_from(3), out_first, mix_first, mix_rest(1), mix_rest(2), mix_rest(3)],
         passing(2, -1, 3, -2, 4) + [mix_from(1), mix_from(2), mix_from(3)],
         passing(-3, 5, -4, 6, -5, 7),
-        passing(-6, 8, -7, 9, -8, 10, -9, -10),
+        passing(-6, 8, -7, 9),
+        passing(-8, 10, -9, -10),
     ]
+    def begin_return():
+        down_first()
+        gate_first()
+        for k in range(1, 4):
+            gate_rest(k)()
+
     def steps_after():
         gain_copy(0).start()
         for k, steps in enumerate(after):
@@ -1225,10 +1291,11 @@
         copy(down_x, down_x, 8, 0, other).wait_send()
         copy(out_x, out_x, 9, 0, other).wait_send()
 
-    return begin_old, begin_feed, begin_mix, steps_after, wait_all
-
-
-def widen_kernel(mix, gate, out, down, mix_f, gate_f, out_f, down_f, places, turned):
+    return begin_old, begin_feed, begin_mix, begin_return, steps_after, wait_all
+
+
+def widen_kernel(mix, gate, out, down, gains, results, starts,
+                 mix_f, gate_f, out_f, down_f, attention_f, feed_f, results_f, starts_f, places, turned):
     step = pl.program_id(0)
     rows = gate.shape[1]
     four = 4 * HEAD
@@ -1236,6 +1303,14 @@
 
     @pl.when(step == 0)
     def _():
+        s = lax.axis_index("section")
+        f = lax.axis_index("fsdp")
+        depth = attention_f.shape[1]
+        columns = pl.ds(pl.multiple_of(f * depth, depth), depth)
+        attention_f[...] = gains[pl.ds(2 * s, 1), columns]
+        feed_f[...] = gains[pl.ds(2 * s + 1, 1), columns]
+        results_f[...] = results[...]
+        starts_f[...] = starts[...]
         source = lax.broadcasted_iota(jnp.int32, (2 * four, 2 * four), 0)
         column = lax.broadcasted_iota(jnp.int32, (2 * four, 2 * four), 1)
         query = (column // HEAD) * 2 * HEAD + lax.rem(column, HEAD)
@@ -1263,33 +1338,45 @@
     down_f[...] = down[...].astype(F32)
 
 
-def widen_call(mix, gate, out, down):
+def widen_call(results, starts, mix, gate, out, down, gains):
     steps = 8
     depth = gate.shape[1]
     width = out.shape[1]
     rows = depth // steps
+
+    def whole(array):
+        return pl.BlockSpec(array.shape, lambda i: (0,) * array.ndim)
+
     down_rows = down.shape[0] // steps
     return pl.pallas_call(
         widen_kernel,
         grid=(steps,),
         out_shape=shapes([
-            full(depth, 2 * width), full(depth, 2 * gate.shape[2]), full(*out.shape), full(*down.shape)
+            full(depth, 2 * width), full(depth, 2 * gate.shape[2]), full(*out.shape), full(*down.shape),
+            full(1, depth), full(1, depth), low(*results.shape), full(*starts.shape),
         ]),
         in_specs=[
-            pl.BlockSpec(mix.shape, lambda i: (0, 0)),
+            whole(mix),
             pl.BlockSpec((2, rows, gate.shape[2]), lambda i: (0, i, 0)),
             pl.BlockSpec((rows, width), lambda i: (i, 0)),
             pl.BlockSpec((down_rows, width), lambda i: (i, 0)),
+            whole(gains),
+            whole(results),
+            whole(starts),
         ],
         out_specs=[
             pl.BlockSpec((rows, 2 * width), lambda i: (i, 0)),
             pl.BlockSpec((rows, 2 * gate.shape[2]), lambda i: (i, 0)),
             pl.BlockSpec((rows, width), lambda i: (i, 0)),
             pl.BlockSpec((down_rows, width), lambda i: (i, 0)),
+            pl.BlockSpec((1, depth), lambda i: (0, 0)),
+            pl.BlockSpec((1, depth), lambda i: (0, 0)),
+            whole(results),
+            whole(starts),
         ],
         scratch_shapes=rooms([low(8 * HEAD, 8 * HEAD), full(depth, 2 * width)]),
-        compiler_params=pltpu.CompilerParams(vmem_limit_bytes=48 << 20),
-    )(mix, gate, out, down)
+        compiler_params=pltpu.CompilerParams(vmem_limit_bytes=60 << 20),
+    )(mix, gate, out, down, gains, results, starts)
 
 
 def on_line():
@@ -1576,38 +1663,35 @@
         first = section == 0
         return jnp.where(first, own, other), jnp.where(first, other, own)
 
-    order = pick(block_order, section, 0)
-    if on_line():
-        order = jnp.swapaxes(order.reshape(C, F // 2, 2), 1, 2).reshape(C * F)
-    positions = (order[:, None] * rows + jnp.arange(rows, dtype=jnp.int32)[None, :]).reshape(length)
-    part_rows = length // plan.share
-    part_positions = lax.dynamic_slice_in_dim(positions, plan.part * part_rows, part_rows, 0)
-    tables = angle_tables(positions)
-    part_tables = angle_tables(part_positions)
-
-    x = pick(inputs, section, 0)
-    grad = pick(cotangent, section, 0)
     results = []
     input_grads = [None, None]
     weight_grads = [None, None]
     gain_grads = [None, None]
     kept = []
     if on_line():
-        own_gains = jnp.pad(jnp.concatenate([attention_gain, feed_gain]), ((0, 14), (0, 0)))
-        shards = (query_key_value, output_weight, gate_up, down_weight, own_gains)
-        common = tuple(tables) + (positions[:, None], positions[None, :])
-        first = forward_call(0, x, shards, common)
-        weights = first[10:]
+        shards = (query_key_value, output_weight, gate_up, down_weight)
+        first = forward_share_call(inputs, shards, (attention_gain, feed_gain), block_order)
+        weights = first[10:15]
+        common = first[15:]
         results.append(first[9])
         second = forward_call(1, first[9], weights, common)
         results.append(second[9])
-        input_grads[1], *old, grad = backward_call(1, grad, weights, common, [first[9], *second[:9]])
-        section_outputs, section_input_grads, *wide, gain_sum = backward_call(
-            0, grad, weights, common, [x, *first[:9]], [input_grads[1], *old], results
+        input_grads[1], *old, grad = backward_call(1, cotangent, weights, common, [first[9], *second[:9]])
+        last = backward_call(
+            0, grad, weights, common, [inputs, *first[:9]], [input_grads[1], *old], results
         )
-        mix_grad, gate_up_grad, out_grad, down_grad = widen_call(*wide)
-        gain_sum = own_gain_sums(plan, section, gain_sum, depth)
+        (mix_grad, gate_up_grad, out_grad, down_grad, attention_gain_grad, feed_gain_grad,
+         section_outputs, section_input_grads) = widen_call(*last)
     else:
+        order = pick(block_order, section, 0)
+        positions = (order[:, None] * rows + jnp.arange(rows, dtype=jnp.int32)[None, :]).reshape(length)
+        part_rows = length // plan.share
+        part_positions = lax.dynamic_slice_in_dim(positions, plan.part * part_rows, part_rows, 0)
+        tables = angle_tables(positions)
+        part_tables = angle_tables(part_positions)
+
+        x = pick(inputs, section, 0)
+        grad = pick(cotangent, section, 0)
         weights, gains = shared_weights(
             plan, section, attention_gain, query_key_value, output_weight, feed_gain, gate_up, down_weight
         )
@@ -1632,14 +1716,15 @@
 
         shard_grads = returned_grads(plan, section, weight_grads, gain_grads, depth)
         mix_grad, gate_up_grad, out_grad, down_grad, gain_sum = shard_grads
+        attention_gain_grad, feed_gain_grad = gain_sum[0][None], gain_sum[1][None]
 
     return (
         section_outputs[None],
         section_input_grads[None],
-        gain_sum[0][None],
+        attention_gain_grad,
         mix_grad[None],
         out_grad[None],
-        gain_sum[1][None],
+        feed_gain_grad,
         gate_up_grad[None],
         down_grad[None],
     )

time: 679 us -> 661 us (0.973)
  local copies, waits for them, and re-layouts: 10.1 us -> 0 us
where the time goes in v5:
time: 661 us; the launch traced here: 653 us
  Pallas kernels  652 us (99%)
    pallas_call x2, Pallas kernels, backward_call(): pl.pallas_call(backward_return_kernel if returning else functools.partial...  409 us
    pallas_call x1, Pallas kernels, forward_share_call(): pl.pallas_call(forward_share_kernel, out_shape=shapes(kept + weights + ta...  133 us
    pallas_call x1, Pallas kernels, forward_call(): pl.pallas_call(functools.partial(forward_kernel, layer), out_shape=shapes...  92.9 us
    pallas_call x1, Pallas kernels, widen_call(): pl.pallas_call(widen_kernel, grid=(steps,), out_shape=shapes([full(depth,...  16.9 us

profile of v5, /device:TPU:0, one launch (start us, length us, event | category | flops | bytes accessed | tf_op | source)
XLA Modules:
  0.0 653.0 jit_solution(14399868050260046440)
XLA Ops:
  0.6 133.2 %shard_map.161 = (bf16[1024,1536]{1,0:T(8,128)(2,1)}, bf16[1024,128]{1,0:T(8,128)(2,1)}, bf16[1024,128]{1,0:T(8,128)(2,1)}, bf16[1024,128]{1,0:T(8,128)(2,1)}, b...) custom-call(bf16[2,64,1536]{2,1,0:T(8,128)(2,1)} %refs_10_.1, ...), custom_call_target="tpu_custom_call" | custom-call | tf_op jit(solution)/shard_map/pallas_call | solution.py:997
  133.8 92.9 %shard_map.162 = (bf16[1024,1536]{1,0:T(8,128)(2,1)}, bf16[1024,128]{1,0:T(8,128)(2,1)}, bf16[1024,128]{1,0:T(8,128)(2,1)}, bf16[1024,128]{1,0:T(8,128)(2,1)}, b...) custom-call(bf16[64,1536]{1,0:T(8,128)(2,1)} %get-tuple-element.68.r, ...), custom_call_target="tpu_custom_call" | custom-call | tf_op jit(solution)/shard_map/pallas_call | solution.py:1012
  226.7 97.6 %shard_map.163 = (f32[64,1536]{1,0:T(8,128)}, bf16[192,1536]{1,0:T(8,128)(2,1)}, bf16[2,1536,256]{2,1,0:T(8,128)(2,1)}, bf16[96,1536]{1,0:T(8,128)(2,1)}, bf16[2...) custom-call(bf16[2,64,1536]{2,1,0:T(8,128)(2,1)} %refs_0_.3, ...), custom_call_target="tpu_custom_call" | custom-call | tf_op jit(solution)/shard_map/pallas_call | solution.py:1048
  324.3 311.3 %shard_map.164 = (bf16[2,64,1536]{2,1,0:T(8,128)(2,1)}, f32[2,64,1536]{2,1,0:T(8,128)}, bf16[3072,384]{1,0:T(8,128)(2,1)}, bf16[2,384,4096]{2,1,0:T(8,128)(2,1)}...) custom-call(bf16[64,1536]{1,0:T(8,128)(2,1)} %get-tuple-element.78.refs_0_, ...), custom_call_target="tpu_custom_call" | custom-call | tf_op jit(solution)/shard_map/pallas_call | solution.py:1048
  635.6 16.9 %shard_map.165 = (f32[384,3072]{1,0:T(8,128)}, f32[384,8192]{1,0:T(8,128)}, f32[384,1536]{1,0:T(8,128)}, f32[1024,1536]{1,0:T(8,128)}, f32[1,384]{1,0:T(1,128)},...) custom-call(bf16[3072,384]{1,0:T(8,128)(2,1)} %get-tuple-element.95.mix, ...), custom_call_target="tpu_custom_call" | custom-call | tf_op jit(solution)/shard_map/pallas_call | solution.py:1351

commit v6 on v5

--- a/solution.py
+++ b/solution.py
@@ -56,7 +56,23 @@
     return c * 4 + lax.rem(f, 2) * 2 + f // 2
 
 
-def gather_rows(whole, rows, send, recv, ready=None, started=None):
+def begin_rows(whole, rows, send, recv, h):
+    c = lax.axis_index("ctx")
+    f = lax.axis_index("fsdp")
+    half = rows // 2
+    mine = whole.at[pl.ds(pl.multiple_of(own_block(c, f) * rows + h * half, half), half)]
+
+    def copy(slot, arrival, peer):
+        return pltpu.make_async_remote_copy(
+            mine, mine, send.at[slot], recv.at[arrival], device_id=peer, device_id_type=MESH
+        )
+
+    pl.when(c < 3)(copy(0, 2 * c + h, {"ctx": jnp.minimum(c + 1, 3)}).start)
+    pl.when(c > 0)(copy(1, 2 * c + h, {"ctx": jnp.maximum(c - 1, 0)}).start)
+    copy(3, 8 + c, {"fsdp": f + 2 - 4 * (f // 2)}).start()
+
+
+def gather_rows(whole, rows, send, recv, ready=None, started=None, begun=False):
     c = lax.axis_index("ctx")
     f = lax.axis_index("fsdp")
     y = f // 2
@@ -97,10 +113,9 @@
     def gone(count, slot):
         copy(whole.at[pl.ds(0, count * half)], slot, 0, to_twin).wait_send()
 
-    for h in range(2):
-        go(at(c, lane, y, h), 0, 2 * c + h, {"ctx": jnp.minimum(c + 1, 3)}, c < 3)
-        go(at(c, lane, y, h), 1, 2 * c + h, {"ctx": jnp.maximum(c - 1, 0)}, c > 0)
-        go(at(c, lane, y, h), 3, 8 + c, to_across)
+    if not begun:
+        for h in range(2):
+            begin_rows(whole, rows, send, recv, h)
     if started is not None:
         started()
 
@@ -165,7 +180,7 @@
 GATHER_RECVS = 18
 
 
-def scatter_sum(part, total, land, send, recv, produce=None, meanwhile=None, ending=None):
+def scatter_sum(part, total, land, send, recv, produce=None, meanwhile=None, ending=None, done=None):
     c = lax.axis_index("ctx")
     f = lax.axis_index("fsdp")
     y = f // 2
@@ -292,6 +307,9 @@
         def _():
             total[h * half : (h + 1) * half, :] += landed(piece(18, h), 31 + h)
 
+        if done is not None:
+            done(h)
+
     gone(16, 0)
     gone(7, 1)
     gone(6, 2)
@@ -350,20 +368,6 @@
     @pl.when(jnp.logical_not(inner))
     def _():
         pl.semaphore_wait(barrier, count + 1)
-
-
-def head_choice(value_part):
-    source = lax.broadcasted_iota(jnp.int32, (4 * HEAD, 4 * LANES), 0)
-    lane = lax.broadcasted_iota(jnp.int32, (4 * HEAD, 4 * LANES), 1)
-    head = lane // LANES
-    inside = lane - head * LANES
-    if value_part:
-        wanted = jnp.where(inside < HEAD, head * HEAD + inside, -1)
-    else:
-        half = inside // SPAN
-        place = inside - half * SPAN
-        wanted = jnp.where(place < HEAD // 2, head * HEAD + half * (HEAD // 2) + place, -1)
-    return jnp.where(source == wanted, 1.0, 0.0).astype(BF)
 
 
 class Share:
@@ -418,24 +422,23 @@
         self.staged.append(self.keep(out_rows, self.out_s, 7))
         self.staged.append(self.keep(down_rows, self.down_s, 8))
 
-    def lanes(self, peer, part):
+    def head_rows(self, peer, part):
         head = peer * 4 + self.c
-        start = head * LANES if part == 0 else (16 + 8 * (part - 1) + head // 2) * LANES
-        return self.heads_v.at[:, pl.ds(pl.multiple_of(start, LANES), LANES)]
+        start = head * HEAD if part == 0 else (16 + 8 * (part - 1) + head // 2) * HEAD
+        return self.heads_v.at[pl.ds(pl.multiple_of(start, HEAD), HEAD)]
 
     def put(self, part):
-        return self.w_mix.at[self.s, self.rows, pl.ds(part * LANES, LANES)]
+        return self.w_mix.at[self.s, pl.ds(part * HEAD, HEAD), self.rows]
 
     def send_mix(self):
         self.loaded.wait()
         for g in range(8):
-            self.heads_v[:, g * 4 * LANES : (g + 1) * 4 * LANES] = kernel_dot(
-                self.mix_v[:, g * 4 * HEAD : (g + 1) * 4 * HEAD], head_choice(g >= 6)
-            ).astype(BF)
+            here = slice(g * 4 * HEAD, (g + 1) * 4 * HEAD)
+            self.heads_v[here, :] = self.mix_v[:, here].T
         for k, peer in enumerate(self.peers):
             for part in range(3):
-                self.copy(self.lanes(peer, part), self.put(part), k, self.f, {"fsdp": peer}).start()
-        self.own_mix = [self.keep(self.lanes(self.f, part), self.put(part), 2 + part) for part in range(3)]
+                self.copy(self.head_rows(peer, part), self.put(part), k, self.f, {"fsdp": peer}).start()
+        self.own_mix = [self.keep(self.head_rows(self.f, part), self.put(part), 2 + part) for part in range(3)]
         for one in self.staged:
             one.wait()
         self.own_gate = self.keep(self.gate_s, self.slab(self.w_gate, self.f), 5)
@@ -462,7 +465,8 @@
                 self.copy(self.gate_piece(peer, part), self.gate_put(part), 3 + k, 4 + self.f, {"fsdp": peer}).start()
 
     def slab(self, ref, origin):
-        return ref.at[self.s, pl.ds(pl.multiple_of(origin * self.depth, self.depth), self.depth)]
+        part = pl.ds(pl.multiple_of(origin * self.depth, self.depth), self.depth)
+        return ref.at[self.s, :, part] if ref is self.w_mix else ref.at[self.s, part]
 
     def cross_slab(self, ref, k, slot, arrival, base):
         origin = lax.rem(self.f + 3 - k, 4)
@@ -494,7 +498,7 @@
             one.wait()
         for origin in range(4):
             rows = pl.ds(origin * self.depth, self.depth)
-            self.there(self.w_mix.at[self.other, rows], 8 + origin)
+            self.there(self.w_mix.at[self.other, :, rows], 8 + origin)
             self.there(self.w_gains.at[self.other, :, rows], 16 + 4 * self.other + origin)
         for k in range(3):
             origin = lax.rem(self.f + 3 - k, 4)
@@ -529,6 +533,14 @@
         one.start()
         self.copies.append(one)
         return one
+
+
+def load_heads(loads, source, target):
+    half = HEAD // 2
+    target[...] = jnp.zeros_like(target)
+    pieces = [(part * HEAD + h * half, part * LANES + h * SPAN, half) for part in range(2) for h in range(2)]
+    pieces.append((2 * HEAD, 2 * LANES, HEAD))
+    return [loads.start(source.at[pl.ds(a, count)], target.at[pl.ds(b, count)]) for a, b, count in pieces]
 
 
 def plane_rows(d, rows):
@@ -560,7 +572,7 @@
         sine[here, :] = jnp.where(lane < SPAN, -wave, wave)
 
 
-def forward_body(layer, share, x_own, weights, tables, kept, scratch, sems, prepare=None):
+def forward_body(layer, share, x_own, weights, tables, kept, scratch, sems, prepare=None, before=None, ending=None):
     w_mix, w_gate, w_out, w_down, w_gains = weights
     cosine, sine, place_col, place_row = tables
     normed_o, q_o, k_o, v_o, context_o, log_o, middle_o, normed_two_o, both_o, result_o = kept
@@ -574,22 +586,26 @@
     own_rows = pl.ds(pl.multiple_of(own_block(c, f) * rows, rows), rows)
     loads = Loads(local)
     saves = Loads(save)
+
+    def save_to(src, dst):
+        if dst is not None:
+            saves.start(src, dst)
+
     load_x = loads.start(x_own, x_v.at[own_rows])
     out_v[...] = jnp.zeros_like(out_v)
 
     def load_first():
         return [
             loads.start(w_gains.at[layer], gains_v),
-            loads.start(w_mix.at[layer], mix_v),
             loads.start(w_out.at[layer], out_v.at[pl.ds(0, HEAD)]),
-        ]
+        ] + load_heads(loads, w_mix.at[layer], mix_v)
 
     def project(d):
         here = plane_rows(d, rows)
         x = x_v[here, :].astype(F32)
         normed = (x * mean_square(x) * gains_v[0:1, :].astype(F32)).astype(BF)
         normed_v[here, :] = normed
-        mixed = kernel_dot(normed, mix_v[...])
+        mixed = kernel_dot_nt(normed, mix_v[...])
         cos = cosine[here, :]
         sin = sine[here, :]
         q = mixed[:, :LANES]
@@ -621,7 +637,7 @@
             project(d)
         share.cross_gate()
     for src, dst in ((normed_v, normed_o), (q_v, q_o), (k_v, k_o), (v_v, v_o)):
-        saves.start(src, dst)
+        save_to(src, dst)
     scale = HEAD ** (-0.5)
 
     def attention(d):
@@ -637,13 +653,22 @@
         log_v[here, :] = jnp.broadcast_to(top + jnp.log(amount), (4 * rows, LANES))
         part_v[here, :] = kernel_dot(context, out_v[...]).astype(BF)
 
-    scatter_sum(part_v, total_v, land_a, send_b, recv_b, attention)
-    saves.start(context_v, context_o)
-    saves.start(log_v, log_o)
-    middle = x_v[own_rows, :].astype(F32) + total_v[...]
-    middle_v[...] = middle
-    saves.start(middle_v, middle_o)
-    two_v[own_rows, :] = (middle * mean_square(middle) * gains_v[1:2, :].astype(F32)).astype(BF)
+    half = rows // 2
+
+    def own_half(h):
+        return pl.ds(pl.multiple_of(own_block(c, f) * rows + h * half, half), half)
+
+    def middle_half(h):
+        part = slice(h * half, (h + 1) * half)
+        middle = x_v[own_half(h), :].astype(F32) + total_v[part, :]
+        middle_v[part, :] = middle
+        two_v[own_half(h), :] = (middle * mean_square(middle) * gains_v[1:2, :].astype(F32)).astype(BF)
+        begin_rows(two_v, rows, send_c, recv_c, h)
+
+    scatter_sum(part_v, total_v, land_a, send_b, recv_b, attention, done=middle_half)
+    save_to(context_v, context_o)
+    save_to(log_v, log_o)
+    save_to(middle_v, middle_o)
 
     def gate_ready():
         if share is None:
@@ -659,9 +684,16 @@
         gate = both[:, :units]
         hidden_v[here, :] = (gate * jax.nn.sigmoid(gate) * both[:, units:]).astype(BF)
 
-    gather_rows(two_v, rows, send_c, recv_c, feed, gate_ready)
-    saves.start(two_v, normed_two_o)
-    saves.start(both_v, both_o)
+    first = iter((True, False, False, False))
+
+    def feed_when_ready(d):
+        if next(first):
+            gate_ready()
+        feed(d)
+
+    gather_rows(two_v, rows, send_c, recv_c, feed_when_ready, begun=True)
+    save_to(two_v, normed_two_o)
+    save_to(both_v, both_o)
     if share is None:
         load_down.wait()
     else:
@@ -672,22 +704,15 @@
         here = plane_rows(d, rows)
         part_v[here, :] = kernel_dot(hidden_v[here, :], down_v[...]).astype(BF)
 
-    scatter_sum(part_v, total_v, land_b, send_d, recv_d, lower)
+    if before is not None:
+        before()
+    scatter_sum(part_v, total_v, land_b, send_d, recv_d, lower, ending=ending)
     result_v[...] = (middle_v[...] + total_v[...]).astype(BF)
     saves.start(result_v, result_o)
     for one in saves.copies:
         one.wait()
     if share is not None:
         share.finish()
-
-
-def forward_kernel(layer, *refs):
-    x_own, *refs = refs
-    weights, refs = refs[:5], refs[5:]
-    tables, refs = refs[:4], refs[4:]
-    kept, refs = refs[:10], refs[10:]
-    scratch, sems = refs[:21], refs[21:]
-    forward_body(layer, None, x_own, weights, tables, kept, scratch, sems)
 
 
 def forward_share_kernel(*refs):
@@ -707,10 +732,9 @@
     )
 
 
-def backward_body(layer, grad_own, weights, tables, saved, outs, scratch, sems, returning):
+def backward_body(layer, grad_own, weights, tables, saved, outs, scratch, sems, returning, forward=None):
     w_mix, w_gate, w_out, w_down, w_gains = weights
     cosine, sine, place_col, place_row = tables
-    x_own, normed, q, k, v, context, log, middle, normed_two, both = saved
     (grad_v, x_v, normed_v, q_v, k_v, v_v, context_v, log_v, middle_v, two_v, both_v, both_grad_v, hidden_v,
      low_v, mixed_v, kv_land, kv_v, key_grad_v, value_grad_v, start_v, start_low_v,
      mix_grad_v, gate_grad_v, out_grad_v, down_grad_v, gain_grad_v,
@@ -719,35 +743,39 @@
     c = lax.axis_index("ctx")
     f = lax.axis_index("fsdp")
     odd = lax.rem(c, 2)
-    rows = x_own.shape[0]
+    rows = x_v.shape[0]
     units = down_v.shape[0]
     own_rows = pl.ds(pl.multiple_of(own_block(c, f) * rows, rows), rows)
     loads = Loads(local)
     saves = Loads(save)
     load_grad = loads.start(grad_own, grad_v.at[own_rows])
-    load_down = loads.start(w_down.at[layer], down_v)
-    load_both = loads.start(both, both_v)
-    load_gate = loads.start(w_gate.at[layer], gate_v)
-    out_v[...] = jnp.zeros_like(out_v)
     key_grad_v[...] = jnp.zeros_like(key_grad_v)
     value_grad_v[...] = jnp.zeros_like(value_grad_v)
     gain_grad_v[...] = jnp.zeros_like(gain_grad_v)
-    if returning is None:
-        greet()
+    if forward is None:
+        x_own, normed, q, k, v, context, log, middle, normed_two, both = saved
+        load_down = loads.start(w_down.at[layer], down_v)
+        load_both = loads.start(both, both_v)
+        load_gate = loads.start(w_gate.at[layer], gate_v)
+        out_v[...] = jnp.zeros_like(out_v)
+        if returning is None:
+            greet()
+        else:
+            peers = [{"fsdp": lax.rem(f + k, 4)} for k in range(1, 4)]
+            greet_more(peers + [{"section": 1 - lax.axis_index("section")}, {"ctx": lax.rem(c + 2, 4)}])
+        load_grad.wait()
+        later = [
+            loads.start(src, dst)
+            for src, dst in (
+                (normed_two, two_v), (middle, middle_v), (w_gains.at[layer], gains_v),
+                (w_out.at[layer], out_v.at[pl.ds(0, HEAD)]), (q, q_v), (k, k_v), (v, v_v),
+                (context, context_v), (log, log_v), (normed, normed_v), (x_own, x_v),
+            )
+        ] + load_heads(loads, w_mix.at[layer], mix_v)
+        load_down.wait()
+        load_both.wait()
     else:
-        peers = [{"fsdp": lax.rem(f + k, 4)} for k in range(1, 4)]
-        greet_more(peers + [{"section": 1 - lax.axis_index("section")}, {"ctx": lax.rem(c + 2, 4)}])
-    load_grad.wait()
-    later = [
-        loads.start(src, dst)
-        for src, dst in (
-            (normed_two, two_v), (middle, middle_v), (w_gains.at[layer], gains_v),
-            (w_out.at[layer], out_v.at[pl.ds(0, HEAD)]), (q, q_v), (k, k_v), (v, v_v),
-            (context, context_v), (log, log_v), (w_mix.at[layer], mix_v), (normed, normed_v), (x_own, x_v),
-        )
-    ]
-    load_down.wait()
-    load_both.wait()
+        later = []
     if returning is not None:
         begin_old, begin_feed, begin_mix, begin_return, finish = returning
         begin_old()
@@ -763,15 +791,25 @@
         both_grad_v[here, :units] = (hidden_grad * up * sig * (1.0 + gate * (1.0 - sig))).astype(BF)
         both_grad_v[here, units:] = (hidden_grad * silu).astype(BF)
 
-    gather_rows(grad_v, rows, send_a, recv_a, feed)
-    load_gate.wait()
+    if forward is None:
+        gather_rows(grad_v, rows, send_a, recv_a, feed)
+        load_gate.wait()
+    else:
+
+        def before():
+            load_grad.wait()
+            for h in range(2):
+                begin_rows(grad_v, rows, send_a, recv_a, h)
+
+        forward(before, lambda: gather_rows(grad_v, rows, send_a, recv_a, feed, begun=True))
 
     def spread(d):
         here = plane_rows(d, rows)
         part_v[here, :] = kernel_dot_nt(both_grad_v[here, :], gate_v[...]).astype(BF)
 
     def feed_weights():
-        later[0].wait()
+        for one in later[:1]:
+            one.wait()
         down_grad_v[...] = kernel_dot_tn(hidden_v[...], grad_v[...]).astype(BF)
         for part in range(2):
             gate_grad_v[part] = kernel_dot_tn(
@@ -783,21 +821,28 @@
         else:
             begin_feed()
 
-    scatter_sum(part_v, total_v, land_a, send_b, recv_b, spread, feed_weights)
-    for one in later[1:]:
-        one.wait()
-
     def norm_grads(error, value, gain, row):
         factor = mean_square(value)
         shaped = error * gain
         common = jnp.mean(shaped * value, axis=-1, keepdims=True)
-        gain_grad_v[row : row + 1, :] = jnp.sum(error * value * factor, axis=0, keepdims=True)
+        gain_grad_v[row : row + 1, :] += jnp.sum(error * value * factor, axis=0, keepdims=True)
         return factor * shaped - value * (factor * factor * factor) * common
 
-    middle_grad = norm_grads(total_v[...], middle_v[...], gains_v[1:2, :].astype(F32), 1)
-    middle_grad = middle_grad + grad_v[own_rows, :].astype(F32)
-    middle_v[...] = middle_grad
-    low_v[own_rows, :] = middle_grad.astype(BF)
+    half = rows // 2
+
+    def middle_half(h):
+        part = slice(h * half, (h + 1) * half)
+        own_half = pl.ds(pl.multiple_of(own_block(c, f) * rows + h * half, half), half)
+        if h == 0:
+            for one in later[1:]:
+                one.wait()
+        middle_grad = norm_grads(total_v[part, :], middle_v[part, :], gains_v[1:2, :].astype(F32), 1)
+        middle_grad = middle_grad + grad_v[own_half, :].astype(F32)
+        middle_v[part, :] = middle_grad
+        low_v[own_half, :] = middle_grad.astype(BF)
+        begin_rows(low_v, rows, send_c, recv_c, h)
+
+    scatter_sum(part_v, total_v, land_a, send_b, recv_b, spread, feed_weights, done=middle_half)
     scale = HEAD ** (-0.5)
 
     def attention(d):
@@ -816,7 +861,7 @@
         query_grad = kernel_dot(score_grad, k_v[...]) * scale
         mixed_v[here, :LANES] = (query_grad * cosine[here, :] - turn(query_grad) * sine[here, :]).astype(BF)
 
-    gather_rows(low_v, rows, send_c, recv_c, attention)
+    gather_rows(low_v, rows, send_c, recv_c, attention, begun=True)
     key_grad = key_grad_v[...] * scale
     mixed_v[:, LANES : 2 * LANES] = (key_grad * cosine[...] - turn(key_grad) * sine[...]).astype(BF)
     mixed_v[:, 2 * LANES :] = value_grad_v[...].astype(BF)
@@ -833,21 +878,21 @@
 
     def spread_two(d):
         here = plane_rows(d, rows)
-        part_v[here, :] = kernel_dot_nt(mixed_v[here, :], mix_v[...]).astype(BF)
+        part_v[here, :] = kernel_dot(mixed_v[here, :], mix_v[...]).astype(BF)
 
     def mix_weights():
         out_grad_v[...] = kernel_dot_tn(context_v[...], low_v[...])[:HEAD].astype(BF)
-        half = HEAD // 2
+        short = HEAD // 2
         columns = kernel_dot_tn(mixed_v[:, :LANES], normed_v[...])
-        mix_grad_v[:half, :] = columns[:half].astype(BF)
-        mix_grad_v[half:HEAD, :] = columns[SPAN : SPAN + half].astype(BF)
+        mix_grad_v[:short, :] = columns[:short].astype(BF)
+        mix_grad_v[short:HEAD, :] = columns[SPAN : SPAN + short].astype(BF)
         pair_copy(1).wait_recv()
         mine = jnp.where(odd == 0, mixed_v[:, LANES : 2 * LANES].astype(F32), mixed_v[:, 2 * LANES :].astype(F32))
         kv_v[...] = (mine + kv_land[...].astype(F32)).astype(BF)
         columns = kernel_dot_tn(kv_v[...], normed_v[...])
-        mix_grad_v[HEAD : HEAD + half, :] = columns[:half].astype(BF)
-        mix_grad_v[HEAD + half :, :] = jnp.where(
-            odd == 0, columns[SPAN : SPAN + half], columns[half:HEAD]
+        mix_grad_v[HEAD : HEAD + short, :] = columns[:short].astype(BF)
+        mix_grad_v[HEAD + short :, :] = jnp.where(
+            odd == 0, columns[SPAN : SPAN + short], columns[short:HEAD]
         ).astype(BF)
         if returning is None:
             saves.start(out_grad_v, outs[3])
@@ -875,14 +920,34 @@
 BACK_SCRATCH = 35
 
 
-def backward_kernel(layer, *refs):
-    grad_own, *refs = refs
+def forward_backward_kernel(layer, *refs):
+    (x_own, cotangent), refs = refs[:2], refs[2:]
     weights, refs = refs[:5], refs[5:]
     tables, refs = refs[:4], refs[4:]
-    saved, refs = refs[:SAVED], refs[SAVED:]
+    result_o, *refs = refs
     outs, refs = refs[:7], refs[7:]
-    scratch, sems = refs[:BACK_SCRATCH], refs[BACK_SCRATCH:]
-    backward_body(layer, grad_own.at[lax.axis_index("section")], weights, tables, saved, outs, scratch, sems, None)
+    ahead, refs = refs[:21], refs[21:]
+    more, refs = refs[:16], refs[16:]
+    ahead_sems, sems = refs[:10], refs[10:]
+    (x_v, normed_v, q_v, k_v, v_v, context_v, log_v, middle_v, two_v, both_v, hidden_v, result_v,
+     mix_v, gate_v, out_v, down_v, gains_v, part_v, land_a, land_b, total_v) = ahead
+    grad_v, own_v, both_grad_v, low_v = more[:4]
+    scratch = [
+        grad_v, own_v, normed_v, q_v, k_v, v_v, context_v, log_v, middle_v, two_v, both_v, both_grad_v, hidden_v,
+        low_v, *more[4:], mix_v, gate_v, out_v, down_v, gains_v, part_v, land_a, land_b, total_v,
+    ]
+
+    def forward(before, ending):
+        forward_body(
+            layer, None, x_own, weights, tables, [None] * 9 + [result_o], ahead, ahead_sems, None, before, ending
+        )
+        rows = own_v.shape[0]
+        place = own_block(lax.axis_index("ctx"), lax.axis_index("fsdp"))
+        own_v[...] = x_v[pl.ds(pl.multiple_of(place * rows, rows), rows), :]
+
+    backward_body(
+        layer, cotangent.at[lax.axis_index("section")], weights, tables, None, outs, scratch, sems, None, forward
+    )
 
 
 def backward_return_kernel(*refs):
@@ -968,7 +1033,7 @@
     length = 16 * rows
     return [low(length, width), low(length, width)] + [low(length, LANES)] * 4 + [
         full(length, LANES), full(rows, width), low(length, width), full(length, 2 * units), low(length, units),
-        low(rows, width), low(width, 3 * LANES), low(width, 2 * units), low(LANES, width), low(units, width),
+        low(rows, width), low(3 * LANES, width), low(width, 2 * units), low(LANES, width), low(units, width),
         low(16, width), low(length, width), low(19, rows, width), low(19, rows, width), full(rows, width)]
 
 
@@ -989,71 +1054,69 @@
     units = shards[2].shape[2] // 32
     frequency = np.zeros((2, SPAN), np.float32)
     frequency[:, : HEAD // 2] = np.float32(rope_base) ** (-(np.arange(HEAD // 2, dtype=np.float32) * 2.0 / HEAD))
-    packing = [low(depth, shards[0].shape[2]), low(depth, 32 * LANES), low(depth, 2 * units), low(HEAD, width),
+    packing = [low(depth, shards[0].shape[2]), low(shards[0].shape[2], depth), low(depth, 2 * units), low(HEAD, width),
                low(units, width), low(16, depth)]
     kept = forward_kept(rows, width, units)
-    weights = [low(2, width, 3 * LANES), low(2, width, 2 * units), low(2, HEAD, width), low(2, units, width), low(2, 16, width)]
+    weights = [low(2, 3 * HEAD, width), low(2, width, 2 * units), low(2, HEAD, width), low(2, units, width), low(2, 16, width)]
     tables = [full(length, LANES), full(length, LANES), ((length, 1), jnp.int32), ((1, length), jnp.int32)]
     return pl.pallas_call(
         forward_share_kernel,
         out_shape=shapes(kept + weights + tables),
         in_specs=[ANYWHERE] * 5 + [INSIDE] * 4,
         out_specs=[ANYWHERE] * 15 + [INSIDE] * 4,
-        scratch_shapes=rooms(forward_scratch(rows, width, units) + packing) + signals(6, 10) + link_sems()
+        scratch_shapes=rooms(forward_scratch(rows, width, units) + packing) + signals(10, 10) + link_sems()
         + signals(9, 27, 26),
         compiler_params=pltpu.CompilerParams(collective_id=0, has_side_effects=True, vmem_limit_bytes=60 << 20),
     )(inputs, *shards, *gains, block_order, jnp.asarray(frequency.reshape(1, LANES)))
 
 
-def forward_call(layer, x_own, weights, tables):
+def backward_grads(width, units):
+    return [low(2 * HEAD, width), low(2, width, units), low(HEAD, width), low(units, width), full(2, width)]
+
+
+def forward_backward_call(layer, x_own, cotangent, weights, tables):
     rows, width = x_own.shape
+    length = 16 * rows
     units = weights[3].shape[1]
-    kept = forward_kept(rows, width, units)
+    grads = backward_grads(width, units)
+    more = [low(length, width), low(rows, width), low(length, 2 * units), low(length, width), low(length, 3 * LANES),
+            low(length, LANES), low(length, LANES), full(length, LANES), full(length, LANES), full(rows, width),
+            low(rows, width)] + grads
+    outs = [low(rows, width), full(rows, width)] + grads + [low(rows, width)]
     return pl.pallas_call(
-        functools.partial(forward_kernel, layer),
-        out_shape=shapes(kept),
-        in_specs=[ANYWHERE] * 6 + [INSIDE] * 4,
-        out_specs=[ANYWHERE] * len(kept),
-        scratch_shapes=rooms(forward_scratch(rows, width, units)) + signals(6, 10) + link_sems(),
+        functools.partial(forward_backward_kernel, layer),
+        out_shape=shapes(outs),
+        in_specs=[ANYWHERE] * 7 + [INSIDE] * 4,
+        out_specs=[ANYWHERE] * len(outs),
+        scratch_shapes=rooms(forward_scratch(rows, width, units) + more) + signals(10, 10) + link_sems()
+        + signals(20, 7, 2) + link_sems(),
         compiler_params=pltpu.CompilerParams(collective_id=layer, has_side_effects=True, vmem_limit_bytes=60 << 20),
-    )(x_own, *weights, *tables)
-
-
-def backward_call(layer, grad_own, weights, tables, saved, old=(), results=()):
-    rows, width = grad_own.shape[-2:]
+    )(x_own, cotangent, *weights, *tables)
+
+
+def backward_return_call(grad_own, weights, tables, saved, old, results):
+    rows, width = grad_own.shape
     length = 16 * rows
     units = weights[3].shape[1]
     depth = width // 4
-    returning = layer == 0
-    anywhere = pl.BlockSpec(memory_space=pl.ANY)
-    inside = pl.BlockSpec(memory_space=pltpu.VMEM)
-    grads = [low(2 * HEAD, width), low(2, width, units), low(HEAD, width), low(units, width), full(2, width)]
+    grads = backward_grads(width, units)
     scratch = [low(length, width), low(rows, width), low(length, width)] + [low(length, LANES)] * 4 + [
         full(length, LANES), full(rows, width), low(length, width), full(length, 2 * units), low(length, 2 * units),
         low(length, units), low(length, width), low(length, 3 * LANES), low(length, LANES), low(length, LANES),
         full(length, LANES), full(length, LANES),
         full(rows, width), low(rows, width)] + grads + [
-        low(width, 3 * LANES), low(width, 2 * units), low(LANES, width), low(units, width),
+        low(3 * LANES, width), low(width, 2 * units), low(LANES, width), low(units, width),
         low(16, width), low(length, width), low(19, rows, width), low(19, rows, width), full(rows, width)]
-    sems = signals(16, 7, 2) + link_sems()
-    if returning:
-        outs = [low(2, rows, width), full(2, rows, width), low(16 * 2 * HEAD, depth), low(2, depth, 16 * units),
-                low(4 * HEAD, width), low(4 * units, width), full(8, width)]
-        out_specs = [anywhere] * 6 + [inside]
-        scratch += grads[:4] + grads[:4] + [full(5, 8, width), full(5, 8, width)]
-        sems += signals(5, 23, 23, 50, 40, 6)
-    else:
-        outs = [full(rows, width)] + grads + [low(rows, width)]
-        out_specs = [anywhere] * len(outs)
+    scratch += grads[:4] + grads[:4] + [full(5, 8, width), full(5, 8, width)]
+    outs = [low(2, rows, width), full(2, rows, width), low(16 * 2 * HEAD, depth), low(2, depth, 16 * units),
+            low(4 * HEAD, width), low(4 * units, width), full(8, width)]
     return pl.pallas_call(
-        backward_return_kernel if returning else functools.partial(backward_kernel, layer),
+        backward_return_kernel,
         out_shape=shapes(outs),
-        in_specs=[anywhere] * 6 + [inside] * 4 + [anywhere] * SAVED
-        + ([anywhere] * 5 + [inside] + [anywhere] * 2 if returning else []),
-        out_specs=out_specs,
-        scratch_shapes=rooms(scratch) + sems,
-        compiler_params=pltpu.CompilerParams(
-            collective_id=2 + layer, has_side_effects=True, vmem_limit_bytes=60 << 20),
+        in_specs=[ANYWHERE] * 6 + [INSIDE] * 4 + [ANYWHERE] * SAVED + [ANYWHERE] * 5 + [INSIDE] + [ANYWHERE] * 2,
+        out_specs=[ANYWHERE] * 6 + [INSIDE],
+        scratch_shapes=rooms(scratch) + signals(20, 7, 2) + link_sems() + signals(5, 23, 23, 50, 40, 6),
+        compiler_params=pltpu.CompilerParams(collective_id=2, has_side_effects=True, vmem_limit_bytes=60 << 20),
     )(grad_own, *weights, *tables, *saved, *old, *results)
 
 
@@ -1295,7 +1358,7 @@
 
 
 def widen_kernel(mix, gate, out, down, gains, results, starts,
-                 mix_f, gate_f, out_f, down_f, attention_f, feed_f, results_f, starts_f, places, turned):
+                 mix_f, gate_f, out_f, down_f, attention_f, feed_f, results_f, starts_f, places, turned, rest):
     step = pl.program_id(0)
     rows = gate.shape[1]
     four = 4 * HEAD
@@ -1314,23 +1377,28 @@
         source = lax.broadcasted_iota(jnp.int32, (2 * four, 2 * four), 0)
         column = lax.broadcasted_iota(jnp.int32, (2 * four, 2 * four), 1)
         query = (column // HEAD) * 2 * HEAD + lax.rem(column, HEAD)
-        rest = column - four
-        kind = rest // (2 * HEAD)
-        rest = rest - kind * 2 * HEAD
-        other = (2 * (rest // HEAD) + kind) * 2 * HEAD + HEAD + lax.rem(rest, HEAD)
+        beyond = column - four
+        kind = beyond // (2 * HEAD)
+        beyond = beyond - kind * 2 * HEAD
+        other = (2 * (beyond // HEAD) + kind) * 2 * HEAD + HEAD + lax.rem(beyond, HEAD)
         places[...] = jnp.where(source == jnp.where(column < four, query, other), 1.0, 0.0).astype(BF)
-        groups = [kernel_dot_tn(mix[g * 2 * four : (g + 1) * 2 * four, :], places[...]) for g in range(4)]
-        for g in range(4):
-            turned[:, g * four : (g + 1) * four] = groups[g][:, :four]
+
+    @pl.when(step < 4)
+    def _():
+        group = kernel_dot_tn(mix[...], places[...])
+        turned[:, pl.ds(pl.multiple_of(step * four, four), four)] = group[:, :four]
+        rest[step] = group[:, four:]
+
+    @pl.when(step >= 4)
+    def _():
+        here = pl.ds(pl.multiple_of((step - 4) * 2 * rows, 2 * rows), 2 * rows)
+        mix_f[:, :width] = turned[here, :]
         for g in range(2):
             for kind in range(2):
                 at = width + kind * 2 * four + g * four
-                low_part = four + kind * 2 * HEAD
-                turned[:, at : at + four] = jnp.concatenate(
-                    [groups[2 * g + k][:, low_part : low_part + 2 * HEAD] for k in range(2)], axis=1
-                )
-
-    mix_f[...] = turned[pl.ds(pl.multiple_of(step * rows, rows), rows), :]
+                part = slice(kind * 2 * HEAD, (kind + 1) * 2 * HEAD)
+                mix_f[:, at : at + four] = jnp.concatenate([rest[2 * g + k, here, part] for k in range(2)], axis=1)
+
     half = gate.shape[2]
     gate_f[:, :half] = gate[0].astype(F32)
     gate_f[:, half:] = gate[1].astype(F32)
@@ -1356,7 +1424,7 @@
             full(1, depth), full(1, depth), low(*results.shape), full(*starts.shape),
         ]),
         in_specs=[
-            whole(mix),
+            pl.BlockSpec((8 * HEAD, depth), lambda i: (jnp.minimum(i, 3), 0)),
             pl.BlockSpec((2, rows, gate.shape[2]), lambda i: (0, i, 0)),
             pl.BlockSpec((rows, width), lambda i: (i, 0)),
             pl.BlockSpec((down_rows, width), lambda i: (i, 0)),
@@ -1365,7 +1433,7 @@
             whole(starts),
         ],
         out_specs=[
-            pl.BlockSpec((rows, 2 * width), lambda i: (i, 0)),
+            pl.BlockSpec((2 * rows, 2 * width), lambda i: (jnp.maximum(i - 4, 0), 0)),
             pl.BlockSpec((rows, 2 * gate.shape[2]), lambda i: (i, 0)),
             pl.BlockSpec((rows, width), lambda i: (i, 0)),
             pl.BlockSpec((down_rows, width), lambda i: (i, 0)),
@@ -1374,7 +1442,7 @@
             whole(results),
             whole(starts),
         ],
-        scratch_shapes=rooms([low(8 * HEAD, 8 * HEAD), full(depth, 2 * width)]),
+        scratch_shapes=rooms([low(8 * HEAD, 8 * HEAD), full(depth, width), full(4, depth, 4 * HEAD)]),
         compiler_params=pltpu.CompilerParams(vmem_limit_bytes=60 << 20),
     )(mix, gate, out, down, gains, results, starts)
 
@@ -1674,12 +1742,9 @@
         weights = first[10:15]
         common = first[15:]
         results.append(first[9])
-        second = forward_call(1, first[9], weights, common)
-        results.append(second[9])
-        input_grads[1], *old, grad = backward_call(1, cotangent, weights, common, [first[9], *second[:9]])
-        last = backward_call(
-            0, grad, weights, common, [inputs, *first[:9]], [input_grads[1], *old], results
-        )
+        result, *old, grad = forward_backward_call(1, first[9], cotangent, weights, common)
+        results.append(result)
+        last = backward_return_call(grad, weights, common, [inputs, *first[:9]], old, results)
         (mix_grad, gate_up_grad, out_grad, down_grad, attention_gain_grad, feed_gain_grad,
          section_outputs, section_input_grads) = widen_call(*last)
     else:

time: 661 us -> 646 us (0.977)
  Pallas kernels: 652 us -> 637 us
    pallas_call x3 -> x2, Pallas kernels: 502 us -> 493 us  [the longest x1 309 us: backward_return_call(): pl.pallas_call(backward_return_kernel, out_shape=shapes(outs), in_specs=[...]
where the time goes in v6:
time: 646 us; the launch traced here: 638 us
  Pallas kernels  637 us (99%)
    pallas_call x1, Pallas kernels, backward_return_call(): pl.pallas_call(backward_return_kernel, out_shape=shapes(outs), in_specs=[...  309 us
    pallas_call x1, Pallas kernels, forward_backward_call(): pl.pallas_call(functools.partial(forward_backward_kernel, layer), out_sha...  183 us
    pallas_call x1, Pallas kernels, forward_share_call(): pl.pallas_call(forward_share_kernel, out_shape=shapes(kept + weights + ta...  128 us
    pallas_call x1, Pallas kernels, widen_call(): pl.pallas_call(widen_kernel, grid=(steps,), out_shape=shapes([full(depth,...  16.1 us

profile of v6, /device:TPU:0, one launch (start us, length us, event | category | flops | bytes accessed | tf_op | source)
XLA Modules:
  0.0 637.8 jit_solution(3878059859260417909)
XLA Ops:
  0.6 127.8 %shard_map.161 = (bf16[1024,1536]{1,0:T(8,128)(2,1)}, bf16[1024,128]{1,0:T(8,128)(2,1)}, bf16[1024,128]{1,0:T(8,128)(2,1)}, bf16[1024,128]{1,0:T(8,128)(2,1)}, b...) custom-call(bf16[2,64,1536]{2,1,0:T(8,128)(2,1)} %refs_10_.1, ...), custom_call_target="tpu_custom_call" | custom-call | tf_op jit(solution)/shard_map/pallas_call | solution.py:1062
  128.5 183.4 %shard_map.162 = (bf16[64,1536]{1,0:T(8,128)(2,1)}, f32[64,1536]{1,0:T(8,128)}, bf16[192,1536]{1,0:T(8,128)(2,1)}, bf16[2,1536,256]{2,1,0:T(8,128)(2,1)}, bf16[9...) custom-call(bf16[64,1536]{1,0:T(8,128)(2,1)} %get-tuple-element.50.refs_0_.refs_26, ...), custom_call_target="tpu_custom_call" | custom-call | tf_op jit(solution)/shard_map/pallas_call | solution.py:1086
  311.9 309.4 %shard_map.163 = (bf16[2,64,1536]{2,1,0:T(8,128)(2,1)}, f32[2,64,1536]{2,1,0:T(8,128)}, bf16[3072,384]{1,0:T(8,128)(2,1)}, bf16[2,384,4096]{2,1,0:T(8,128)(2,1)}...) custom-call(bf16[64,1536]{1,0:T(8,128)(2,1)} %get-tuple-element.60.refs_0_, ...), custom_call_target="tpu_custom_call" | custom-call | tf_op jit(solution)/shard_map/pallas_call | solution.py:1113
  621.3 16.1 %shard_map.164 = (f32[384,3072]{1,0:T(8,128)}, f32[384,8192]{1,0:T(8,128)}, f32[384,1536]{1,0:T(8,128)}, f32[1024,1536]{1,0:T(8,128)}, f32[1,384]{1,0:T(1,128)},...) custom-call(bf16[3072,384]{1,0:T(8,128)(2,1)} %get-tuple-element.77.mix, ...), custom_call_target="tpu_custom_call" | custom-call | tf_op jit(solution)/shard_map/pallas_call | solution.py:1419

commit v7 on v6

--- a/solution.py
+++ b/solution.py
@@ -572,7 +572,7 @@
         sine[here, :] = jnp.where(lane < SPAN, -wave, wave)
 
 
-def forward_body(layer, share, x_own, weights, tables, kept, scratch, sems, prepare=None, before=None, ending=None):
+def forward_body(layer, share, x_own, weights, tables, kept, scratch, sems, prepare=None, before=None, ending=None, meet=None):
     w_mix, w_gate, w_out, w_down, w_gains = weights
     cosine, sine, place_col, place_row = tables
     normed_o, q_o, k_o, v_o, context_o, log_o, middle_o, normed_two_o, both_o, result_o = kept
@@ -618,7 +618,7 @@
         first = load_first()
         load_gate = loads.start(w_gate.at[layer], gate_v)
         load_down = loads.start(w_down.at[layer], down_v)
-        greet()
+        meet()
         load_x.wait()
         for one in first:
             one.wait()
@@ -732,11 +732,11 @@
     )
 
 
-def backward_body(layer, grad_own, weights, tables, saved, outs, scratch, sems, returning, forward=None):
+def backward_body(layer, grad_own, weights, tables, saved, outs, scratch, sems, returning, forward=None, hand_on=None):
     w_mix, w_gate, w_out, w_down, w_gains = weights
     cosine, sine, place_col, place_row = tables
     (grad_v, x_v, normed_v, q_v, k_v, v_v, context_v, log_v, middle_v, two_v, both_v, both_grad_v, hidden_v,
-     low_v, mixed_v, kv_land, kv_v, key_grad_v, value_grad_v, start_v, start_low_v,
+     low_v, mixed_v, kv_land, kv_v, key_grad_v, value_grad_v, start_v,
      mix_grad_v, gate_grad_v, out_grad_v, down_grad_v, gain_grad_v,
      mix_v, gate_v, out_v, down_v, gains_v, part_v, land_a, land_b, total_v) = scratch
     local, save, pair_sems, send_a, recv_a, send_b, recv_b, send_c, recv_c, send_d, recv_d = sems
@@ -748,7 +748,6 @@
     own_rows = pl.ds(pl.multiple_of(own_block(c, f) * rows, rows), rows)
     loads = Loads(local)
     saves = Loads(save)
-    load_grad = loads.start(grad_own, grad_v.at[own_rows])
     key_grad_v[...] = jnp.zeros_like(key_grad_v)
     value_grad_v[...] = jnp.zeros_like(value_grad_v)
     gain_grad_v[...] = jnp.zeros_like(gain_grad_v)
@@ -758,12 +757,6 @@
         load_both = loads.start(both, both_v)
         load_gate = loads.start(w_gate.at[layer], gate_v)
         out_v[...] = jnp.zeros_like(out_v)
-        if returning is None:
-            greet()
-        else:
-            peers = [{"fsdp": lax.rem(f + k, 4)} for k in range(1, 4)]
-            greet_more(peers + [{"section": 1 - lax.axis_index("section")}, {"ctx": lax.rem(c + 2, 4)}])
-        load_grad.wait()
         later = [
             loads.start(src, dst)
             for src, dst in (
@@ -776,6 +769,7 @@
         load_both.wait()
     else:
         later = []
+        load_grad = loads.start(grad_own, grad_v.at[own_rows])
     if returning is not None:
         begin_old, begin_feed, begin_mix, begin_return, finish = returning
         begin_old()
@@ -792,7 +786,7 @@
         both_grad_v[here, units:] = (hidden_grad * silu).astype(BF)
 
     if forward is None:
-        gather_rows(grad_v, rows, send_a, recv_a, feed)
+        gather_rows(grad_v, rows, send_a, recv_a, feed, begun=True)
         load_gate.wait()
     else:
 
@@ -900,14 +894,18 @@
         else:
             begin_mix()
 
+    def start_half(h):
+        part = slice(h * half, (h + 1) * half)
+        start_grad = norm_grads(total_v[part, :], x_v[part, :].astype(F32), gains_v[0:1, :].astype(F32), 0)
+        start_grad = start_grad + middle_v[part, :]
+        start_v[part, :] = start_grad
+        if hand_on is not None:
+            hand_on(h, start_grad)
+
     scatter_sum(part_v, total_v, land_b, send_d, recv_d, spread_two, mix_weights,
-                None if returning is None else begin_return)
-    start_grad = norm_grads(total_v[...], x_v[...].astype(F32), gains_v[0:1, :].astype(F32), 0) + middle_v[...]
-    start_v[...] = start_grad
+                None if returning is None else begin_return, start_half)
     if returning is None:
         saves.start(start_v, outs[0])
-        start_low_v[...] = start_grad.astype(BF)
-        saves.start(start_low_v, outs[6])
         saves.start(gain_grad_v, outs[5])
     else:
         finish(gain_grad_v)
@@ -916,19 +914,20 @@
         one.wait()
 
 
-SAVED = 10
-BACK_SCRATCH = 35
-
-
-def forward_backward_kernel(layer, *refs):
-    (x_own, cotangent), refs = refs[:2], refs[2:]
+def turn_kernel(*refs):
+    (x_own, cotangent, inputs), refs = refs[:3], refs[3:]
     weights, refs = refs[:5], refs[5:]
     tables, refs = refs[:4], refs[4:]
-    result_o, *refs = refs
-    outs, refs = refs[:7], refs[7:]
+    saved, refs = refs[:9], refs[9:]
+    (results_o, starts_o), refs = refs[:2], refs[2:]
+    finals, refs = refs[:5], refs[5:]
+    (result_old, start_old, mix_old, gate_old, out_old, down_old), refs = refs[:6], refs[6:]
     ahead, refs = refs[:21], refs[21:]
-    more, refs = refs[:16], refs[16:]
-    ahead_sems, sems = refs[:10], refs[10:]
+    more, refs = refs[:15], refs[15:]
+    own, refs = refs[:10], refs[10:]
+    gain_old, *refs = refs
+    ahead_sems, first_sems, second_sems = refs[:10], refs[10:21], refs[21:32]
+    return_sems, swap_sems = refs[32:37], refs[37]
     (x_v, normed_v, q_v, k_v, v_v, context_v, log_v, middle_v, two_v, both_v, hidden_v, result_v,
      mix_v, gate_v, out_v, down_v, gains_v, part_v, land_a, land_b, total_v) = ahead
     grad_v, own_v, both_grad_v, low_v = more[:4]
@@ -936,36 +935,34 @@
         grad_v, own_v, normed_v, q_v, k_v, v_v, context_v, log_v, middle_v, two_v, both_v, both_grad_v, hidden_v,
         low_v, *more[4:], mix_v, gate_v, out_v, down_v, gains_v, part_v, land_a, land_b, total_v,
     ]
+    start_new = more[9]
+    mix_new, gate_new, out_new, down_new, gain_new = more[10:]
+    gain_v = own[8]
+    s = lax.axis_index("section")
+    c = lax.axis_index("ctx")
+    f = lax.axis_index("fsdp")
+    rows = own_v.shape[0]
+    half = rows // 2
+    first_row = own_block(c, f) * rows
+
+    def meet():
+        peers = [{"fsdp": lax.rem(f + k, 4)} for k in range(1, 4)]
+        greet_more(peers + [{"section": 1 - s}, {"ctx": lax.rem(c + 2, 4)}])
 
     def forward(before, ending):
         forward_body(
-            layer, None, x_own, weights, tables, [None] * 9 + [result_o], ahead, ahead_sems, None, before, ending
+            1, None, x_own, weights, tables, [None] * 9 + [result_old], ahead, ahead_sems, None, before, ending, meet
         )
-        rows = own_v.shape[0]
-        place = own_block(lax.axis_index("ctx"), lax.axis_index("fsdp"))
-        own_v[...] = x_v[pl.ds(pl.multiple_of(place * rows, rows), rows), :]
+        own_v[...] = x_v[pl.ds(pl.multiple_of(first_row, rows), rows), :]
+
+    def hand_on(h, start_grad):
+        grad_v[pl.ds(pl.multiple_of(first_row + h * half, half), half), :] = start_grad.astype(BF)
+        begin_rows(grad_v, rows, second_sems[3], second_sems[4], h)
 
     backward_body(
-        layer, cotangent.at[lax.axis_index("section")], weights, tables, None, outs, scratch, sems, None, forward
+        1, cotangent.at[s], weights, tables, None, (start_old, mix_old, gate_old, out_old, down_old, gain_old),
+        scratch, first_sems, None, forward, hand_on,
     )
-
-
-def backward_return_kernel(*refs):
-    grad_own, *refs = refs
-    weights, refs = refs[:5], refs[5:]
-    tables, refs = refs[:4], refs[4:]
-    saved, refs = refs[:SAVED], refs[SAVED:]
-    (start_old, mix_old, gate_old, out_old, down_old, gain_old), refs = refs[:6], refs[6:]
-    (result_new, result_old), refs = refs[:2], refs[2:]
-    (results_o, starts_o), refs = refs[:2], refs[2:]
-    finals, refs = refs[:5], refs[5:]
-    scratch, refs = refs[:BACK_SCRATCH], refs[BACK_SCRATCH:]
-    own, refs = refs[:10], refs[10:]
-    sems, return_sems, swap_sems = refs[:11], refs[11:16], refs[16]
-    start_new = scratch[19]
-    mix_new, gate_new, out_new, down_new, gain_new = scratch[21:26]
-    gain_v = own[8]
-    s = lax.axis_index("section")
     begin_old, begin_feed, begin_mix, begin_return, steps_after, wait_all = returner(
         tuple(finals) + tuple(own), return_sems,
         gate_new, down_new, mix_new, out_new, gate_old, down_old, mix_old, out_old,
@@ -979,6 +976,8 @@
     def swap_rows(away, home, out, slot):
         swap_copy(away, out.at[s], slot).start()
         pltpu.make_async_copy(home, out.at[s], swap_sems.at[4 + slot]).start()
+
+    result_new = x_own
 
     def finish(gain_grad_v):
         @pl.when(s == 0)
@@ -1000,8 +999,10 @@
             pltpu.make_async_copy(out.at[s], out.at[s], swap_sems.at[4 + slot]).wait()
             swap_copy(out.at[s], out.at[1 - s], slot).wait()
 
-    saved = [saved[0].at[s], *saved[1:]]
-    backward_body(0, grad_own, weights, tables, saved, None, scratch, sems, (begin_old, begin_feed, begin_mix, begin_return, finish))
+    backward_body(
+        0, None, weights, tables, [inputs.at[s], *saved], None, scratch, second_sems,
+        (begin_old, begin_feed, begin_mix, begin_return, finish),
+    )
 
 
 def link_sems():
@@ -1074,50 +1075,27 @@
     return [low(2 * HEAD, width), low(2, width, units), low(HEAD, width), low(units, width), full(2, width)]
 
 
-def forward_backward_call(layer, x_own, cotangent, weights, tables):
+def turn_call(x_own, cotangent, inputs, weights, tables, saved):
     rows, width = x_own.shape
     length = 16 * rows
+    depth = width // 4
     units = weights[3].shape[1]
     grads = backward_grads(width, units)
     more = [low(length, width), low(rows, width), low(length, 2 * units), low(length, width), low(length, 3 * LANES),
-            low(length, LANES), low(length, LANES), full(length, LANES), full(length, LANES), full(rows, width),
-            low(rows, width)] + grads
-    outs = [low(rows, width), full(rows, width)] + grads + [low(rows, width)]
+            low(length, LANES), low(length, LANES), full(length, LANES), full(length, LANES), full(rows, width)] + grads
+    own = grads[:4] + grads[:4] + [full(5, 8, width), full(5, 8, width)]
+    finals = [low(2, rows, width), full(2, rows, width), low(16 * 2 * HEAD, depth), low(2, depth, 16 * units),
+              low(4 * HEAD, width), low(4 * units, width), full(8, width)]
+    old = [low(rows, width), full(rows, width)] + grads[:4]
     return pl.pallas_call(
-        functools.partial(forward_backward_kernel, layer),
-        out_shape=shapes(outs),
-        in_specs=[ANYWHERE] * 7 + [INSIDE] * 4,
-        out_specs=[ANYWHERE] * len(outs),
-        scratch_shapes=rooms(forward_scratch(rows, width, units) + more) + signals(10, 10) + link_sems()
-        + signals(20, 7, 2) + link_sems(),
-        compiler_params=pltpu.CompilerParams(collective_id=layer, has_side_effects=True, vmem_limit_bytes=60 << 20),
-    )(x_own, cotangent, *weights, *tables)
-
-
-def backward_return_call(grad_own, weights, tables, saved, old, results):
-    rows, width = grad_own.shape
-    length = 16 * rows
-    units = weights[3].shape[1]
-    depth = width // 4
-    grads = backward_grads(width, units)
-    scratch = [low(length, width), low(rows, width), low(length, width)] + [low(length, LANES)] * 4 + [
-        full(length, LANES), full(rows, width), low(length, width), full(length, 2 * units), low(length, 2 * units),
-        low(length, units), low(length, width), low(length, 3 * LANES), low(length, LANES), low(length, LANES),
-        full(length, LANES), full(length, LANES),
-        full(rows, width), low(rows, width)] + grads + [
-        low(3 * LANES, width), low(width, 2 * units), low(LANES, width), low(units, width),
-        low(16, width), low(length, width), low(19, rows, width), low(19, rows, width), full(rows, width)]
-    scratch += grads[:4] + grads[:4] + [full(5, 8, width), full(5, 8, width)]
-    outs = [low(2, rows, width), full(2, rows, width), low(16 * 2 * HEAD, depth), low(2, depth, 16 * units),
-            low(4 * HEAD, width), low(4 * units, width), full(8, width)]
-    return pl.pallas_call(
-        backward_return_kernel,
-        out_shape=shapes(outs),
-        in_specs=[ANYWHERE] * 6 + [INSIDE] * 4 + [ANYWHERE] * SAVED + [ANYWHERE] * 5 + [INSIDE] + [ANYWHERE] * 2,
-        out_specs=[ANYWHERE] * 6 + [INSIDE],
-        scratch_shapes=rooms(scratch) + signals(20, 7, 2) + link_sems() + signals(5, 23, 23, 50, 40, 6),
-        compiler_params=pltpu.CompilerParams(collective_id=2, has_side_effects=True, vmem_limit_bytes=60 << 20),
-    )(grad_own, *weights, *tables, *saved, *old, *results)
+        turn_kernel,
+        out_shape=shapes(finals + old),
+        in_specs=[ANYWHERE] * 8 + [INSIDE] * 4 + [ANYWHERE] * 9,
+        out_specs=[ANYWHERE] * 6 + [INSIDE] + [ANYWHERE] * 6,
+        scratch_shapes=rooms(forward_scratch(rows, width, units) + more + own + grads[4:]) + signals(10, 10) + link_sems()
+        + signals(20, 7, 2) + link_sems() + signals(20, 7, 2) + link_sems() + signals(5, 23, 23, 50, 40, 6),
+        compiler_params=pltpu.CompilerParams(collective_id=1, has_side_effects=True, vmem_limit_bytes=60 << 20),
+    )(x_own, cotangent, inputs, *weights, *tables, *saved)
 
 
 def returner(refs, sems, gate_new, down_new, mix_new, out_new, gate_old, down_old, mix_old, out_old):
@@ -1741,10 +1719,7 @@
         first = forward_share_call(inputs, shards, (attention_gain, feed_gain), block_order)
         weights = first[10:15]
         common = first[15:]
-        results.append(first[9])
-        result, *old, grad = forward_backward_call(1, first[9], cotangent, weights, common)
-        results.append(result)
-        last = backward_return_call(grad, weights, common, [inputs, *first[:9]], old, results)
+        last = turn_call(first[9], cotangent, inputs, weights, common, first[:9])[:7]
         (mix_grad, gate_up_grad, out_grad, down_grad, attention_gain_grad, feed_gain_grad,
          section_outputs, section_input_grads) = widen_call(*last)
     else:

time: 646 us -> 639 us (0.989)
  Pallas kernels: 637 us -> 630 us
    pallas_call x2 -> x1, Pallas kernels: 493 us -> 486 us  [turn_call(): pl.pallas_call(turn_kernel, out_shape=shapes(finals + old), in_specs=[ANY...]
where the time goes in v7:
time: 639 us; the launch traced here: 631 us
  Pallas kernels  630 us (99%)
    pallas_call x1, Pallas kernels, turn_call(): pl.pallas_call(turn_kernel, out_shape=shapes(finals + old), in_specs=[ANY...  486 us
    pallas_call x1, Pallas kernels, forward_share_call(): pl.pallas_call(forward_share_kernel, out_shape=shapes(kept + weights + ta...  128 us
    pallas_call x1, Pallas kernels, widen_call(): pl.pallas_call(widen_kernel, grid=(steps,), out_shape=shapes([full(depth,...  16.1 us

profile of v7, /device:TPU:0, one launch (start us, length us, event | category | flops | bytes accessed | tf_op | source)
XLA Modules:
  0.0 631.4 jit_solution(16112353223226250258)
XLA Ops:
  0.6 127.8 %shard_map.161 = (bf16[1024,1536]{1,0:T(8,128)(2,1)}, bf16[1024,128]{1,0:T(8,128)(2,1)}, bf16[1024,128]{1,0:T(8,128)(2,1)}, bf16[1024,128]{1,0:T(8,128)(2,1)}, b...) custom-call(bf16[2,64,1536]{2,1,0:T(8,128)(2,1)} %refs_2_.3, ...), custom_call_target="tpu_custom_call" | custom-call | tf_op jit(solution)/shard_map/pallas_call | solution.py:1063
  128.5 486.3 %shard_map.162 = (bf16[2,64,1536]{2,1,0:T(8,128)(2,1)}, f32[2,64,1536]{2,1,0:T(8,128)}, bf16[3072,384]{1,0:T(8,128)(2,1)}, bf16[2,384,4096]{2,1,0:T(8,128)(2,1)}...) custom-call(bf16[64,1536]{1,0:T(8,128)(2,1)} %get-tuple-element.42.r, ...), custom_call_target="tpu_custom_call" | custom-call | tf_op jit(solution)/shard_map/pallas_call | solution.py:1090
  614.8 16.1 %shard_map.163 = (f32[384,3072]{1,0:T(8,128)}, f32[384,8192]{1,0:T(8,128)}, f32[384,1536]{1,0:T(8,128)}, f32[1024,1536]{1,0:T(8,128)}, f32[1,384]{1,0:T(1,128)},...) custom-call(bf16[3072,384]{1,0:T(8,128)(2,1)} %get-tuple-element.61.mix, ...), custom_call_target="tpu_custom_call" | custom-call | tf_op jit(solution)/shard_map/pallas_call | solution.py:1397

commit v8 on v7

--- a/solution.py
+++ b/solution.py
@@ -273,9 +273,9 @@
     begin(0)
     over(0, 0, True)
     over(0, 1)
-    begin(1)
     begin(2)
     over(2, 1, True)
+    begin(1)
     over(1, 0, True)
     onward(0, 0, True)
     over(1, 1)

time: 639 us -> 635 us (level)
  no operation moved by 1% of the time
where the time goes in v8:
time: 635 us; the launch traced here: 628 us
  Pallas kernels  627 us (99%)
    pallas_call x1, Pallas kernels, turn_call(): pl.pallas_call(turn_kernel, out_shape=shapes(finals + old), in_specs=[ANY...  484 us
    pallas_call x1, Pallas kernels, forward_share_call(): pl.pallas_call(forward_share_kernel, out_shape=shapes(kept + weights + ta...  127 us
    pallas_call x1, Pallas kernels, widen_call(): pl.pallas_call(widen_kernel, grid=(steps,), out_shape=shapes([full(depth,...  16.1 us

profile of v8, /device:TPU:0, one launch (start us, length us, event | category | flops | bytes accessed | tf_op | source)
XLA Modules:
  0.0 627.9 jit_solution(16561714771198926671)
XLA Ops:
  0.6 126.5 %shard_map.161 = (bf16[1024,1536]{1,0:T(8,128)(2,1)}, bf16[1024,128]{1,0:T(8,128)(2,1)}, bf16[1024,128]{1,0:T(8,128)(2,1)}, bf16[1024,128]{1,0:T(8,128)(2,1)}, b...) custom-call(bf16[2,64,1536]{2,1,0:T(8,128)(2,1)} %refs_2_.3, ...), custom_call_target="tpu_custom_call" | custom-call | tf_op jit(solution)/shard_map/pallas_call | solution.py:1063
  127.2 484.0 %shard_map.162 = (bf16[2,64,1536]{2,1,0:T(8,128)(2,1)}, f32[2,64,1536]{2,1,0:T(8,128)}, bf16[3072,384]{1,0:T(8,128)(2,1)}, bf16[2,384,4096]{2,1,0:T(8,128)(2,1)}...) custom-call(bf16[64,1536]{1,0:T(8,128)(2,1)} %get-tuple-element.42.r, ...), custom_call_target="tpu_custom_call" | custom-call | tf_op jit(solution)/shard_map/pallas_call | solution.py:1090
  611.2 16.1 %shard_map.163 = (f32[384,3072]{1,0:T(8,128)}, f32[384,8192]{1,0:T(8,128)}, f32[384,1536]{1,0:T(8,128)}, f32[1024,1536]{1,0:T(8,128)}, f32[1,384]{1,0:T(1,128)},...) custom-call(bf16[3072,384]{1,0:T(8,128)(2,1)} %get-tuple-element.61.mix, ...), custom_call_target="tpu_custom_call" | custom-call | tf_op jit(solution)/shard_map/pallas_call | solution.py:1397

commit v9 on v8

--- a/solution.py
+++ b/solution.py
@@ -493,17 +493,22 @@
     def there(self, ref, arrival):
         self.copy(ref, ref, 0, arrival, {"section": self.other}).wait_recv()
 
+    def gains_there(self):
+        self.own_gains.wait()
+        for origin in range(4):
+            columns = pl.ds(origin * self.depth, self.depth)
+            self.there(self.w_gains.at[self.other, :, columns], 16 + 4 * self.other + origin)
+        for k in range(3):
+            origin = lax.rem(self.f + 3 - k, 4)
+            columns = pl.ds(pl.multiple_of(origin * self.depth, self.depth), self.depth)
+            self.there(self.w_gains.at[self.s, :, columns], 16 + 4 * self.s + origin)
+
     def mix_there(self):
-        for one in (self.own_gains, self.own_gate, self.own_out, self.own_down):
+        for one in (self.own_gate, self.own_out, self.own_down):
             one.wait()
         for origin in range(4):
             rows = pl.ds(origin * self.depth, self.depth)
             self.there(self.w_mix.at[self.other, :, rows], 8 + origin)
-            self.there(self.w_gains.at[self.other, :, rows], 16 + 4 * self.other + origin)
-        for k in range(3):
-            origin = lax.rem(self.f + 3 - k, 4)
-            columns = pl.ds(pl.multiple_of(origin * self.depth, self.depth), self.depth)
-            self.there(self.w_gains.at[self.s, :, columns], 16 + 4 * self.s + origin)
         self.there(self.w_out.at[self.other], 24)
 
     def gate_there(self):
@@ -596,16 +601,17 @@
 
     def load_first():
         return [
-            loads.start(w_gains.at[layer], gains_v),
             loads.start(w_out.at[layer], out_v.at[pl.ds(0, HEAD)]),
         ] + load_heads(loads, w_mix.at[layer], mix_v)
 
-    def project(d):
+    def normalize(d):
         here = plane_rows(d, rows)
         x = x_v[here, :].astype(F32)
-        normed = (x * mean_square(x) * gains_v[0:1, :].astype(F32)).astype(BF)
-        normed_v[here, :] = normed
-        mixed = kernel_dot_nt(normed, mix_v[...])
+        normed_v[here, :] = (x * mean_square(x) * gains_v[0:1, :].astype(F32)).astype(BF)
+
+    def multiply(d):
+        here = plane_rows(d, rows)
+        mixed = kernel_dot_nt(normed_v[here, :], mix_v[...])
         cos = cosine[here, :]
         sin = sine[here, :]
         q = mixed[:, :LANES]
@@ -615,26 +621,39 @@
         v_v[here, :] = mixed[:, 2 * LANES :].astype(BF)
 
     if share is None:
-        first = load_first()
+        first = [loads.start(w_gains.at[layer], gains_v)] + load_first()
         load_gate = loads.start(w_gate.at[layer], gate_v)
         load_down = loads.start(w_down.at[layer], down_v)
         meet()
         load_x.wait()
         for one in first:
             one.wait()
+
+        def project(d):
+            normalize(d)
+            multiply(d)
+
         gather_rows(x_v, rows, send_a, recv_a, project)
     else:
         share.load()
         greet_more(share.greeted())
         load_x.wait()
         share.send_mix()
-        gather_rows(x_v, rows, send_a, recv_a, started=lambda: share.cross_mix(prepare))
+        turns = iter((True, False, False, False))
+
+        def normalize_when_ready(d):
+            if next(turns):
+                share.gains_there()
+                loads.start(w_gains.at[layer], gains_v).wait()
+            normalize(d)
+
+        gather_rows(x_v, rows, send_a, recv_a, normalize_when_ready, started=lambda: share.cross_mix(prepare))
         share.mix_there()
         first = load_first()
         for one in first:
             one.wait()
         for d in range(4):
-            project(d)
+            multiply(d)
         share.cross_gate()
     for src, dst in ((normed_v, normed_o), (q_v, q_o), (k_v, k_o), (v_v, v_o)):
         save_to(src, dst)

time: 635 us -> 636 us (level)
  no operation moved by 1% of the time
where the time goes in v9:
time: 636 us; the launch traced here: 628 us
  Pallas kernels  626 us (98%)
    pallas_call x1, Pallas kernels, turn_call(): pl.pallas_call(turn_kernel, out_shape=shapes(finals + old), in_specs=[ANY...  484 us
    pallas_call x1, Pallas kernels, forward_share_call(): pl.pallas_call(forward_share_kernel, out_shape=shapes(kept + weights + ta...  126 us
    pallas_call x1, Pallas kernels, widen_call(): pl.pallas_call(widen_kernel, grid=(steps,), out_shape=shapes([full(depth,...  16.1 us

profile of v9, /device:TPU:0, one launch (start us, length us, event | category | flops | bytes accessed | tf_op | source)
XLA Modules:
  0.0 627.7 jit_solution(14197603561847149779)
XLA Ops:
  0.6 126.2 %shard_map.161 = (bf16[1024,1536]{1,0:T(8,128)(2,1)}, bf16[1024,128]{1,0:T(8,128)(2,1)}, bf16[1024,128]{1,0:T(8,128)(2,1)}, bf16[1024,128]{1,0:T(8,128)(2,1)}, b...) custom-call(bf16[2,64,1536]{2,1,0:T(8,128)(2,1)} %refs_2_.3, ...), custom_call_target="tpu_custom_call" | custom-call | tf_op jit(solution)/shard_map/pallas_call | solution.py:1082
  126.8 484.2 %shard_map.162 = (bf16[2,64,1536]{2,1,0:T(8,128)(2,1)}, f32[2,64,1536]{2,1,0:T(8,128)}, bf16[3072,384]{1,0:T(8,128)(2,1)}, bf16[2,384,4096]{2,1,0:T(8,128)(2,1)}...) custom-call(bf16[64,1536]{1,0:T(8,128)(2,1)} %get-tuple-element.42.r, ...), custom_call_target="tpu_custom_call" | custom-call | tf_op jit(solution)/shard_map/pallas_call | solution.py:1109
  611.0 16.1 %shard_map.163 = (f32[384,3072]{1,0:T(8,128)}, f32[384,8192]{1,0:T(8,128)}, f32[384,1536]{1,0:T(8,128)}, f32[1024,1536]{1,0:T(8,128)}, f32[1,384]{1,0:T(1,128)},...) custom-call(bf16[3072,384]{1,0:T(8,128)(2,1)} %get-tuple-element.61.mix, ...), custom_call_target="tpu_custom_call" | custom-call | tf_op jit(solution)/shard_map/pallas_call | solution.py:1416
